TPU v7x, 32 devices: a whole 2x2x4 slice. The times are simulated.
32 devices in a mesh: dp: 4 (over x, core), seq: 4 (over z), head: 2 (over y).
Axes of the slice: x: 2, y: 2, z: 4, core: 2. Of those that a mesh axis runs over, the one named last changes fastest.
Arguments:
- hidden_in: bfloat16 [4096, 1024], P(('dp', 'seq')), may hold values from -6 to 6
- segment_ids: int32 [4, 1024], P('dp'), may hold values from 0 to 2, as said below
- gain_mix: bfloat16 [2, 1024], replicated, may hold values from 0.5 to 1.5
- w_zx: bfloat16 [2, 1024, 2, 1536], P(None, None, None, 'head'), may hold values from -0.1875 to 0.1875
- w_bc: bfloat16 [2, 1024, 256], replicated, may hold values from -0.1875 to 0.1875
- w_dt: bfloat16 [2, 1024, 24], P(None, None, 'head'), may hold values from -0.1875 to 0.1875
- conv_x: bfloat16 [2, 4, 24, 64], P(None, None, 'head'), may hold values from -3 to 3
- conv_bc: bfloat16 [2, 4, 256], replicated, may hold values from -3 to 3
- ssm_head: float32 [2, 3, 24], P(None, None, 'head'), may hold values from -6 to 2
- w_q: bfloat16 [2, 1024, 512], P(None, None, 'head'), may hold values from -0.1875 to 0.1875
- w_kv: bfloat16 [2, 1024, 2, 128], P(None, None, 'head'), may hold values from -0.1875 to 0.1875
- w_o: bfloat16 [2, 512, 1024], P(None, 'head'), may hold values from -1 to 1
- w_out: bfloat16 [2, 1536, 1024], P(None, 'head'), may hold values from -0.15625 to 0.15625
- gain_ff: bfloat16 [2, 1024], replicated, may hold values from 0.5 to 1.5
- w_gu: bfloat16 [2, 1024, 2, 2048], P(None, None, None, 'head'), may hold values from -0.1875 to 0.1875
- w_down: bfloat16 [2, 2048, 1024], P(None, 'head'), may hold values from -0.125 to 0.125
- cotangent: bfloat16 [4096, 1024], P(('dp', 'seq')), may hold values from -6 to 6
Outputs:
- block_out: bfloat16 [4096, 1024], P(('dp', 'seq'))
- grad_in: float32 [4096, 1024], P(('dp', 'seq'))
- grad_gain_mix: float32 [2, 1024], P(None, ('dp', 'seq'))
- grad_w_zx: float32 [2, 1024, 2, 1536], P(None, ('dp', 'seq'), None, 'head')
- grad_w_bc: float32 [2, 1024, 256], P(None, None, ('dp', 'seq', 'head'))
- grad_w_dt: float32 [2, 1024, 24], P(None, ('dp', 'seq'), 'head')
- grad_conv_x: float32 [2, 4, 24, 64], P(None, None, 'head', ('dp', 'seq'))
- grad_conv_bc: float32 [2, 4, 256], P(None, None, ('dp', 'seq', 'head'))
- grad_ssm_head: float32 [2, 3, 24], P(None, None, 'head')
- grad_w_q: float32 [2, 1024, 512], P(None, ('dp', 'seq'), 'head')
- grad_w_kv: float32 [2, 1024, 2, 128], P(None, ('dp', 'seq'), 'head')
- grad_w_o: float32 [2, 512, 1024], P(None, 'head', ('dp', 'seq'))
- grad_w_out: float32 [2, 1536, 1024], P(None, 'head', ('dp', 'seq'))
- grad_gain_ff: float32 [2, 1024], P(None, ('dp', 'seq'))
- grad_w_gu: float32 [2, 1024, 2, 2048], P(None, ('dp', 'seq'), None, 'head')
- grad_w_down: float32 [2, 2048, 1024], P(None, 'head', ('dp', 'seq'))
Inputs may be any that keep to these rules, and one draw needn't show every extreme that they name: `segment_ids`: never falling along a sequence; every sequence holds documents 0, 1 and 2.
All inputs are finite; a program needn't handle non-finite values.
Results may differ from a plain program's by a relative error of at most 0.03.
Values may be sent and summed in bfloat16 or wider, within the bound.
A program may use at most 320 MiB of HBM per device.

v0:
```python
import jax
import jax.numpy as jnp
from jax import lax
from jax.sharding import PartitionSpec as P

NS = 128
HD = 64
BLOCK = 64


highest = lax.Precision.HIGHEST
norm_eps = 1e-05
masked_score = -1e30


def from_behind(value, axis, steps):
    count = lax.axis_size(axis)
    initial, last = (max(0, -steps), min(count, count - steps))
    return lax.ppermute(value, axis, [(source, source + steps) for source in range(initial, last)])


def entering(array, axis, join, neutral, backward):
    count = lax.axis_size(axis)
    place = lax.axis_index(axis)
    ahead = count - 1 - place if backward else place
    gathered = jax.tree.map(
        lambda a, kind: lax.all_gather(a.astype(kind), axis), array, (jnp.bfloat16, jnp.bfloat16)
    )
    state = jax.tree.map(lambda a, e: jnp.zeros_like(a) + jnp.asarray(e, a.dtype), array, neutral)

    def one(step, state):
        source = count - 1 - step if backward else step
        return join(
            state,
            jax.tree.map(
                lambda a, own: lax.dynamic_index_in_dim(a, source, 0, False).astype(own.dtype),
                gathered,
                array,
            ),
        )

    return lax.fori_loop(0, ahead, one, state)


def product(left, right):
    return jnp.dot(left, right, preferred_element_type=jnp.float32)


def left_product(left, right):
    return lax.dot_general(
        left, right, (((0,), (0,)), ((), ())), preferred_element_type=jnp.float32
    )


def right_product(left, right):
    return lax.dot_general(
        left, right, (((1,), (1,)), ((), ())), preferred_element_type=jnp.float32
    )


def rms_scaled(hidden, gain):
    return hidden * lax.rsqrt(jnp.mean(hidden * hidden, axis=-1, keepdims=True) + norm_eps) * gain


def conv_silu(extended, weights, doc_ext):
    tap_count = weights.shape[0]
    row_count = extended.shape[0] - (tap_count - 1)
    current = doc_ext[tap_count - 1 :]
    running_sum = extended[tap_count - 1 :] * weights[0]
    for offset in range(1, tap_count):
        begin = tap_count - 1 - offset
        same_doc = (doc_ext[begin : begin + row_count] == current).astype(jnp.float32)[:, None]
        running_sum = running_sum + extended[begin : begin + row_count] * same_doc * weights[offset]
    return jax.nn.silu(running_sum)


def block_step(carry_in, inputs):
    memory, last_doc = carry_in
    values, b_rows, c_rows, step_sizes, log_decay, doc_ids = inputs
    running = jnp.cumsum(log_decay, axis=0)
    gaps_log = running[:, None, :] - running[None, :, :]
    ordered = jnp.arange(BLOCK)[:, None] >= jnp.arange(BLOCK)[None, :]
    linked = ordered & (doc_ids[:, None] == doc_ids[None, :])
    decays = jnp.exp(jnp.where(linked[:, :, None], gaps_log, 0.0)) * linked[:, :, None].astype(
        jnp.float32
    )
    intersection = jnp.dot(c_rows, b_rows.T, precision=highest)
    mixing = decays * intersection[:, :, None] * step_sizes[None, :, :]
    outputs = jnp.einsum("tsh,shp->thp", mixing, values, precision=highest)
    carried = (doc_ids == last_doc).astype(jnp.float32)[:, None] * jnp.exp(running)
    outputs = outputs + carried[:, :, None] * jnp.einsum(
        "tn,hpn->thp", c_rows, memory, precision=highest
    )
    fading = (
        jnp.exp(running[-1][None, :] - running)
        * (doc_ids == doc_ids[-1]).astype(jnp.float32)[:, None]
        * step_sizes
    )
    memory = carried[-1][:, None, None] * memory + jnp.einsum(
        "sh,shp,sn->hpn", fading, values, b_rows, precision=highest
    )
    return ((memory, doc_ids[-1]), outputs)


def ssm_scan(values, b_rows, c_rows, step_sizes, log_decay, doc_ids, start_memory, start_doc):
    block_count = values.shape[0] // BLOCK

    def into_blocks(tensor):
        return tensor.reshape((block_count, BLOCK) + tensor.shape[1:])

    final, scanned = lax.scan(
        block_step,
        (start_memory, start_doc),
        (
            into_blocks(values),
            into_blocks(b_rows),
            into_blocks(c_rows),
            into_blocks(step_sizes),
            into_blocks(log_decay),
            into_blocks(doc_ids),
        ),
    )
    return (final, scanned.reshape(values.shape))


def mamba_local(extended, dt_raw, conv_taps, head_vals, doc_ext, start_doc):
    mixed = conv_silu(extended, conv_taps, doc_ext)
    row_count, channel_count = mixed.shape
    heads_here = head_vals.shape[1]
    d_local = channel_count - 2 * NS
    values = mixed[:, :d_local].reshape(row_count, heads_here, d_local // heads_here)
    b_rows = mixed[:, d_local : d_local + NS]
    c_rows = mixed[:, d_local + NS :]
    step_sizes = jax.nn.softplus(dt_raw + head_vals[0])
    log_decay = -jnp.exp(head_vals[1]) * step_sizes
    doc_ids = doc_ext[conv_taps.shape[0] - 1 :]
    start_memory = jnp.zeros((heads_here, d_local // heads_here, NS), jnp.float32)
    final, scanned = ssm_scan(
        values, b_rows, c_rows, step_sizes, log_decay, doc_ids, start_memory, start_doc
    )
    skipped = scanned + head_vals[2][None, :, None] * values
    decay_in = (
        jnp.exp(jnp.cumsum(log_decay, axis=0)) * (doc_ids == start_doc).astype(jnp.float32)[:, None]
    )
    return (skipped, final[0], decay_in, c_rows)


def mamba_finish(skipped, decay_in, c_rows, gate_in, memory_in):
    row_count = skipped.shape[0]
    carried = decay_in[:, :, None] * jnp.einsum("tn,hpn->thp", c_rows, memory_in, precision=highest)
    return (skipped + carried).reshape(row_count, -1) * jax.nn.silu(gate_in)


def mamba_full(extended, gate_in, dt_raw, conv_taps, head_vals, memory_in, doc_ext, start_doc):
    skipped, local_memory, decay_in, c_rows = mamba_local(
        extended, dt_raw, conv_taps, head_vals, doc_ext, start_doc
    )
    gated_out = mamba_finish(skipped, decay_in, c_rows, gate_in, memory_in)
    memory_out = decay_in[-1][:, None, None] * memory_in + local_memory
    return (gated_out, memory_out)


def chain_combine(earlier, later):
    return (earlier[0] * later[0], later[0][:, None, None] * earlier[1] + later[1])


def block_span(row_count):
    return row_count // max(1, row_count // 512)


def masked_scores(block_q, keys_all, doc_all, first_pos, span):
    length_all = keys_all.shape[0]
    head_size = block_q.shape[-1]
    scores = jnp.einsum(
        "tgrd,kgd->grtk", block_q, keys_all, preferred_element_type=jnp.float32
    ) * head_size ** (-0.5)
    query_pos = first_pos + jnp.arange(span)
    query_doc = lax.dynamic_slice_in_dim(doc_all, first_pos, span)
    allowed = (jnp.arange(length_all)[None, :] <= query_pos[:, None]) & (
        doc_all[None, :] == query_doc[:, None]
    )
    return jnp.where(allowed[None, None], scores, masked_score)


def split_keyvals(keyvals_all):
    length_all = keyvals_all.shape[0]
    kv_heads = keyvals_all.shape[1] // (2 * HD)
    shaped = keyvals_all.reshape(length_all, kv_heads, 2, HD)
    return (shaped[:, :, 0], shaped[:, :, 1], kv_heads)


def attend_forward(queries, keyvals_all, doc_all, offset):
    row_count = queries.shape[0]
    keys_all, vals_all, kv_heads = split_keyvals(keyvals_all)
    group_size = queries.shape[1] // (kv_heads * HD)
    span = block_span(row_count)
    block_q = queries.reshape(span, kv_heads, group_size, HD)
    scores = masked_scores(block_q, keys_all, doc_all, offset + 0, span)
    peak = jnp.max(scores, axis=-1, keepdims=True)
    expo_scores = jnp.exp(scores - peak)
    denominator = jnp.sum(expo_scores, axis=-1, keepdims=True)
    weights_soft = (expo_scores / denominator).astype(jnp.bfloat16)
    totals_blocks = [peak + jnp.log(denominator)]
    mixed = jnp.einsum("grtk,kgd->tgrd", weights_soft, vals_all, preferred_element_type=jnp.float32)
    attended_blocks = mixed.reshape(span, -1).astype(jnp.bfloat16)
    return (attended_blocks, jnp.stack(totals_blocks))


def attend_backward(queries, keyvals_all, log_totals, grad_att, doc_all, offset):
    row_count = queries.shape[0]
    keys_all, vals_all, kv_heads = split_keyvals(keyvals_all)
    length_all = keys_all.shape[0]
    group_size = queries.shape[1] // (kv_heads * HD)
    span = block_span(row_count)
    score_scale = HD ** (-0.5)
    block_q = queries.reshape(span, kv_heads, group_size, HD)
    scores = masked_scores(block_q, keys_all, doc_all, offset + 0, span)
    weights_soft = jnp.exp(scores - log_totals[0])
    probs_low = weights_soft.astype(jnp.bfloat16)
    grad_block = grad_att.reshape(span, kv_heads, group_size, HD)
    grad_probs = jnp.einsum(
        "tgrd,kgd->grtk", grad_block, vals_all, preferred_element_type=jnp.float32
    )
    inner_sum = jnp.sum(grad_probs * weights_soft, axis=-1, keepdims=True)
    grad_scores = (weights_soft * (grad_probs - inner_sum)).astype(jnp.bfloat16)
    grad_query = (
        jnp.einsum("grtk,kgd->tgrd", grad_scores, keys_all, preferred_element_type=jnp.float32)
        * score_scale
    )
    query_blocks = grad_query.reshape(span, -1)
    grad_keys = (
        jnp.einsum("grtk,tgrd->kgd", grad_scores, block_q, preferred_element_type=jnp.float32)
        * score_scale
    )
    grad_vals = jnp.einsum(
        "grtk,tgrd->kgd", probs_low, grad_block, preferred_element_type=jnp.float32
    )
    grad_kv_all = jnp.stack([grad_keys, grad_vals], axis=2).reshape(length_all, -1)
    return (query_blocks, grad_kv_all)


def layer_forward(hidden, params, context):
    (
        gain_mix,
        w_zx,
        w_bc,
        w_dt,
        conv_x,
        conv_bc,
        ssm_head,
        w_q,
        w_kv,
        w_o,
        w_out,
        gain_ff,
        w_gu,
        w_down,
    ) = params
    doc_all, doc_ext, start_doc, offset = context
    row_count, model_width = hidden.shape
    d_local = w_zx.shape[2]
    ff_local = w_gu.shape[2]
    tap_count = conv_x.shape[0]
    normed = rms_scaled(hidden, gain_mix.astype(jnp.float32)).astype(jnp.bfloat16)
    zx_proj = product(normed, w_zx.reshape(model_width, 2 * d_local)).astype(jnp.bfloat16)
    bc_proj = product(normed, w_bc).astype(jnp.bfloat16)
    dt_raw = product(normed, w_dt).astype(jnp.bfloat16)
    stacked = jnp.concatenate([zx_proj[:, d_local:], bc_proj], axis=1)
    rim_rows = from_behind(stacked[row_count - (tap_count - 1) :], "seq", 1)
    extended = jnp.concatenate([rim_rows, stacked], axis=0)
    conv_taps = jnp.concatenate([conv_x.reshape(tap_count, d_local), conv_bc], axis=1).astype(
        jnp.float32
    )
    gate_in = zx_proj[:, :d_local].astype(jnp.float32)
    skipped, local_memory, decay_in, c_rows = mamba_local(
        extended.astype(jnp.float32),
        dt_raw.astype(jnp.float32),
        conv_taps,
        ssm_head,
        doc_ext,
        start_doc,
    )
    passed = entering(
        (decay_in[-1], local_memory),
        "seq",
        chain_combine,
        (jnp.ones_like(decay_in[-1]), jnp.zeros_like(local_memory)),
        False,
    )
    memory_in = passed[1]
    gated_out = mamba_finish(skipped, decay_in, c_rows, gate_in, memory_in).astype(jnp.bfloat16)
    queries = product(normed, w_q).astype(jnp.bfloat16)
    keyvals = product(normed, w_kv.reshape(model_width, -1)).astype(jnp.bfloat16)
    keyvals_all = lax.all_gather(keyvals, "seq", axis=0, tiled=True)
    attended, log_totals = attend_forward(queries, keyvals_all, doc_all, offset)
    partial_sum = product(gated_out, w_out) + product(attended, w_o)
    middle = hidden + lax.psum(partial_sum.astype(jnp.bfloat16), "head").astype(jnp.float32)
    normed_ff = rms_scaled(middle, gain_ff.astype(jnp.float32)).astype(jnp.bfloat16)
    gate_up = product(normed_ff, w_gu.reshape(model_width, -1)).astype(jnp.bfloat16)
    inner_act = (
        jax.nn.silu(gate_up[:, :ff_local].astype(jnp.float32))
        * gate_up[:, ff_local:].astype(jnp.float32)
    ).astype(jnp.bfloat16)
    output = middle + lax.psum(product(inner_act, w_down).astype(jnp.bfloat16), "head").astype(
        jnp.float32
    )
    saved_state = (
        hidden,
        normed,
        zx_proj,
        dt_raw,
        extended,
        memory_in,
        decay_in,
        c_rows,
        gated_out,
        queries,
        keyvals_all,
        attended,
        log_totals,
        middle,
        normed_ff,
        gate_up,
        inner_act,
    )
    return (output, saved_state)


def layer_backward(grad_out, params, saved_state, context):
    (
        gain_mix,
        w_zx,
        w_bc,
        w_dt,
        conv_x,
        conv_bc,
        ssm_head,
        w_q,
        w_kv,
        w_o,
        w_out,
        gain_ff,
        w_gu,
        w_down,
    ) = params
    (
        hidden,
        normed,
        zx_proj,
        dt_raw,
        extended,
        memory_in,
        decay_in,
        c_rows,
        gated_out,
        queries,
        keyvals_all,
        attended,
        log_totals,
        middle,
        normed_ff,
        gate_up,
        inner_act,
    ) = saved_state
    doc_all, doc_ext, start_doc, offset = context
    row_count, model_width = hidden.shape
    d_local = w_zx.shape[2]
    ff_local = w_gu.shape[2]
    tap_count = conv_x.shape[0]
    heads_here = ssm_head.shape[1]
    grad_ff = grad_out.astype(jnp.bfloat16)
    g_down = left_product(inner_act, grad_ff)
    grad_inner = right_product(grad_ff, w_down)

    def swiglu(gate_part, up_part):
        return jax.nn.silu(gate_part) * up_part

    _, swiglu_pull = jax.vjp(
        swiglu, gate_up[:, :ff_local].astype(jnp.float32), gate_up[:, ff_local:].astype(jnp.float32)
    )
    grad_gate, grad_up = swiglu_pull(grad_inner)
    grad_gu = jnp.concatenate([grad_gate, grad_up], axis=1).astype(jnp.bfloat16)
    g_gu = left_product(normed_ff, grad_gu).reshape(model_width, 2, ff_local)
    grad_nff = lax.psum(
        right_product(grad_gu, w_gu.reshape(model_width, -1)).astype(jnp.bfloat16), "head"
    ).astype(jnp.float32)
    _, ff_norm_pull = jax.vjp(rms_scaled, middle, gain_ff.astype(jnp.float32))
    grad_middle, g_gain_ff = ff_norm_pull(grad_nff)
    grad_middle = grad_middle + grad_out
    grad_branch = grad_middle.astype(jnp.bfloat16)
    g_out = left_product(gated_out, grad_branch)
    grad_gated = right_product(grad_branch, w_out)
    gate_in = zx_proj[:, :d_local].astype(jnp.float32)
    grad_ssm = (grad_gated * jax.nn.silu(gate_in)).reshape(row_count, heads_here, -1)
    pushed = jnp.einsum("th,thp,tn->hpn", decay_in, grad_ssm, c_rows, precision=highest)
    returned = entering(
        (decay_in[-1], pushed),
        "seq",
        chain_combine,
        (jnp.ones_like(decay_in[-1]), jnp.zeros_like(pushed)),
        True,
    )
    grad_memory = returned[1]
    conv_taps = jnp.concatenate([conv_x.reshape(tap_count, d_local), conv_bc], axis=1).astype(
        jnp.float32
    )

    def mamba_piece(ext_rows, gate_rows, raw_rows, taps_in, head_vals, memory_start):
        return mamba_full(
            ext_rows, gate_rows, raw_rows, taps_in, head_vals, memory_start, doc_ext, start_doc
        )

    _, mamba_pull = jax.vjp(
        mamba_piece,
        extended.astype(jnp.float32),
        gate_in,
        dt_raw.astype(jnp.float32),
        conv_taps,
        ssm_head,
        memory_in,
    )
    grad_ext, grad_gate_in, grad_raw, g_conv, g_head, _ = mamba_pull((grad_gated, grad_memory))
    rim_grad = from_behind(grad_ext[: tap_count - 1], "seq", -1)
    grad_stack = grad_ext[tap_count - 1 :] + jnp.concatenate(
        [jnp.zeros((row_count - (tap_count - 1), grad_ext.shape[1]), jnp.float32), rim_grad], axis=0
    )
    grad_zx = jnp.concatenate([grad_gate_in, grad_stack[:, :d_local]], axis=1).astype(jnp.bfloat16)
    grad_bc = grad_stack[:, d_local:]
    grad_dt = grad_raw.astype(jnp.bfloat16)
    g_o = left_product(attended, grad_branch)
    grad_att = right_product(grad_branch, w_o).astype(jnp.bfloat16)
    grad_query, grad_kv_all = attend_backward(
        queries, keyvals_all, log_totals, grad_att, doc_all, offset
    )
    grad_kv = lax.psum_scatter(
        grad_kv_all.astype(jnp.bfloat16), "seq", scatter_dimension=0, tiled=True
    )
    grad_query = grad_query.astype(jnp.bfloat16)
    normed_exact = normed.astype(jnp.float32)
    g_zx = left_product(normed, grad_zx).reshape(model_width, 2, d_local)
    g_bc = lax.dot_general(normed_exact, grad_bc, (((0,), (0,)), ((), ())), precision=highest)
    g_dt = left_product(normed, grad_dt)
    g_q = left_product(normed, grad_query)
    g_kv = left_product(normed, grad_kv).reshape(w_kv.shape)
    grad_normed = (
        right_product(grad_zx, w_zx.reshape(model_width, -1))
        + lax.dot_general(
            grad_bc, w_bc.astype(jnp.float32), (((1,), (1,)), ((), ())), precision=highest
        )
        + right_product(grad_dt, w_dt)
        + right_product(grad_query, w_q)
        + right_product(grad_kv, w_kv.reshape(model_width, -1))
    )
    grad_normed = lax.psum(grad_normed.astype(jnp.bfloat16), "head").astype(jnp.float32)
    _, mix_norm_pull = jax.vjp(rms_scaled, hidden, gain_mix.astype(jnp.float32))
    grad_hidden, g_gain_mix = mix_norm_pull(grad_normed)
    grad_hidden = grad_hidden + grad_middle
    g_conv_x = g_conv[:, :d_local].reshape(conv_x.shape)
    g_conv_bc = g_conv[:, d_local:]
    split_parts = (g_gain_mix, g_zx, g_dt, g_conv_x, g_q, g_kv, g_o, g_out, g_gain_ff, g_gu, g_down)
    shared_parts = (g_bc, g_conv_bc)
    return (grad_hidden, split_parts, shared_parts, g_head)


def reduce_grads(split_parts, shared_parts, head_part):
    (
        gain_a,
        zx_part,
        dt_part,
        convx_part,
        q_part,
        kv_part,
        o_part,
        out_part,
        gain_b,
        gu_part,
        down_part,
    ) = split_parts
    summed = (
        lax.psum_scatter(gain_a, ("dp", "seq"), scatter_dimension=1, tiled=True),
        lax.psum_scatter(zx_part, ("dp", "seq"), scatter_dimension=1, tiled=True),
        lax.psum_scatter(dt_part, ("dp", "seq"), scatter_dimension=1, tiled=True),
        lax.psum_scatter(convx_part, ("dp", "seq"), scatter_dimension=3, tiled=True),
        lax.psum_scatter(q_part, ("dp", "seq"), scatter_dimension=1, tiled=True),
        lax.psum_scatter(kv_part, ("dp", "seq"), scatter_dimension=1, tiled=True),
        lax.psum_scatter(o_part, ("dp", "seq"), scatter_dimension=2, tiled=True),
        lax.psum_scatter(out_part, ("dp", "seq"), scatter_dimension=2, tiled=True),
        lax.psum_scatter(gain_b, ("dp", "seq"), scatter_dimension=1, tiled=True),
        lax.psum_scatter(gu_part, ("dp", "seq"), scatter_dimension=1, tiled=True),
        lax.psum_scatter(down_part, ("dp", "seq"), scatter_dimension=2, tiled=True),
    )
    shared_sums = (
        lax.psum_scatter(shared_parts[0], ("dp", "seq", "head"), scatter_dimension=2, tiled=True),
        lax.psum_scatter(shared_parts[1], ("dp", "seq", "head"), scatter_dimension=2, tiled=True),
    )
    head_sum = lax.psum(head_part, ("dp", "seq"))
    return (tuple(summed), tuple(shared_sums), head_sum)


def on_device(
    hidden_in,
    segment_ids,
    gain_mix,
    w_zx,
    w_bc,
    w_dt,
    conv_x,
    conv_bc,
    ssm_head,
    w_q,
    w_kv,
    w_o,
    w_out,
    gain_ff,
    w_gu,
    w_down,
    cotangent,
):
    row_count = hidden_in.shape[0]
    tap_count = conv_x.shape[1]
    seq_index = lax.axis_index("seq")
    offset = seq_index * row_count
    doc_all = segment_ids[0]
    padded_docs = jnp.concatenate([jnp.full((tap_count - 1,), -1, jnp.int32), doc_all])
    doc_ext = lax.dynamic_slice_in_dim(padded_docs, offset, row_count + tap_count - 1)
    start_doc = doc_ext[tap_count - 2]
    context = (doc_all, doc_ext, start_doc, offset)
    layer_count = gain_mix.shape[0]
    params_all = (
        gain_mix,
        w_zx,
        w_bc,
        w_dt,
        conv_x,
        conv_bc,
        ssm_head,
        w_q,
        w_kv,
        w_o,
        w_out,
        gain_ff,
        w_gu,
        w_down,
    )
    hidden = hidden_in.astype(jnp.float32)
    saved_list = []
    output = hidden
    for layer_index in range(layer_count):
        params = tuple((weight[layer_index] for weight in params_all))
        output, saved_state = layer_forward(hidden, params, context)
        saved_list.append(saved_state)
        if layer_index + 1 < layer_count:
            hidden = output.astype(jnp.bfloat16).astype(jnp.float32)
    block_out = output.astype(jnp.bfloat16)
    gradient = cotangent.astype(jnp.float32)
    pending = []
    for layer_index in reversed(range(layer_count)):
        params = tuple((weight[layer_index] for weight in params_all))
        gradient, split_parts, shared_parts, head_part = layer_backward(
            gradient, params, saved_list[layer_index], context
        )
        leading = jax.tree.map(
            lambda grad_piece: grad_piece[None], (split_parts, shared_parts, head_part)
        )
        pending.append(leading)
    collected = pending[::-1]
    joined = jax.tree.map(lambda *layer_parts: jnp.concatenate(layer_parts, axis=0), *collected)
    summed, shared_sums, head_sum = reduce_grads(joined[0], joined[1], joined[2])
    return (
        block_out,
        gradient,
        summed[0],
        summed[1],
        shared_sums[0],
        summed[2],
        summed[3],
        shared_sums[1],
        head_sum,
        summed[4],
        summed[5],
        summed[6],
        summed[7],
        summed[8],
        summed[9],
        summed[10],
    )


def solution(mesh):
    in_specs = (
        P(("dp", "seq"), None),
        P("dp", None),
        P(),
        P(None, None, None, "head"),
        P(),
        P(None, None, "head"),
        P(None, None, "head", None),
        P(),
        P(None, None, "head"),
        P(None, None, "head"),
        P(None, None, "head", None),
        P(None, "head", None),
        P(None, "head", None),
        P(),
        P(None, None, None, "head"),
        P(None, "head", None),
        P(("dp", "seq"), None),
    )
    out_specs = (
        P(("dp", "seq"), None),
        P(("dp", "seq"), None),
        P(None, ("dp", "seq")),
        P(None, ("dp", "seq"), None, "head"),
        P(None, None, ("dp", "seq", "head")),
        P(None, ("dp", "seq"), "head"),
        P(None, None, "head", ("dp", "seq")),
        P(None, None, ("dp", "seq", "head")),
        P(None, None, "head"),
        P(None, ("dp", "seq"), "head"),
        P(None, ("dp", "seq"), "head", None),
        P(None, "head", ("dp", "seq")),
        P(None, "head", ("dp", "seq")),
        P(None, ("dp", "seq")),
        P(None, ("dp", "seq"), None, "head"),
        P(None, "head", ("dp", "seq")),
    )
    return jax.shard_map(
        on_device, mesh=mesh, in_specs=in_specs, out_specs=out_specs, check_vma=False
    )
```

profile of v0, /device:TPU:0, one launch (start us, length us, event | category | flops | bytes accessed | tf_op | source)
XLA Modules:
  0.0 2467.2 jit_solution(13823780685029302797)
XLA Ops:
  26.6 14.8 all_gather.45
  94.6 158.9 %while.252 = (s32[]{:T(128)}, f32[12,64,128]{2,1,0:T(8,128)S(1)}, s32[]{:T(128)}, f32[4,64,12,64]{1,0,3,2:T(4,128)}, pred[4,64,64,12]{2,1,3,0:T(32,128)(4,1)}, /...) while((s32[]{:T(128)}, f32[12,64,128]{2,1,0:T(8,128)S(1)}, ...), condition=%wide.region_28.30_spmd.clone.clone, body=%wide.region_26.29_spmd.clone.clone.sunk | while | flops 196302592 | bytes 7537263 | solution.py:111
  257.8 77.3 %while.250 = (s32[]{:T(128)}, f32[12,64,128]{2,1,0:T(8,128)S(1)}, s32[]{:T(128)}, f32[4,64,12,64]{1,0,3,2:T(4,128)}, s32[4,64]{1,0:T(4,128)}, /*index=5*/f32[4,6...) while((s32[]{:T(128)}, f32[12,64,128]{2,1,0:T(8,128)S(1)}, ...), condition=%wide.region_3.4_spmd.clone, body=%wide.region_1.3_spmd.clone.sunk | while | flops 195889664 | bytes 3486123 | solution.py:111
  338.3 16.8 all-gather
  375.9 16.5 all-reduce.56.cloned.1.call-done
  405.1 23.8 all-reduce.58.cloned.1.call-done
  432.7 13.9 all_gather.49
  500.1 190.4 %while.253 = (s32[]{:T(128)}, f32[12,64,128]{2,1,0:T(8,128)}, s32[]{:T(128)}, f32[4,64,12,64]{1,0,3,2:T(4,128)}, pred[4,64,64,12]{2,1,3,0:T(32,128)(4,1)}, /*ind...) while((s32[]{:T(128)}, f32[12,64,128]{2,1,0:T(8,128)}, ...), condition=%wide.region_33.35_spmd.clone.clone, body=%wide.region_31.34_spmd.clone.clone.sunk | while | flops 196302592 | bytes 8511259 | solution.py:111
  695.0 107.7 %while.251 = (s32[]{:T(128)}, f32[12,64,128]{2,1,0:T(8,128)S(1)}, s32[]{:T(128)}, f32[4,64,12,64]{1,0,3,2:T(4,128)}, s32[4,64]{1,0:T(4,128)}, /*index=5*/f32[4,6...) while((s32[]{:T(128)}, f32[12,64,128]{2,1,0:T(8,128)S(1)}, ...), condition=%wide.region_16.17_spmd.clone, body=%wide.region_14.16_spmd.clone.sunk | while | flops 195889664 | bytes 3474943 | solution.py:111
  805.7 17.4 all-gather.1
  838.5 20.7 all-reduce.60.cloned.1.call-done
  872.2 26.0 %all-reduce.62.cloned.1.call-done = bf16[256,1024]{1,0:T(8,128)(2,1)} async-done(((bf16[256,1024]{1,0:T(8,128)(2,1)}), bf16[256,1024]{1,0:T(8,128)(2,1)}) %all-reduce.62.cloned.1.call-update) | async-done | bytes 524304 | tf_op jit(solution)/shard_map/psum | solution.py:384
  914.2 19.6 all-gather.2
  949.7 112.5 %while.247 = (s32[]{:T(128)}, f32[12,64,128]{2,1,0:T(8,128)S(1)}, f32[4,64,12,64]{3,1,2,0:T(8,128)}, f32[4,64,128]{2,1,0:T(8,128)}, f32[4,64,128]{2,1,0:T(8,128)...) while((s32[]{:T(128)}, f32[12,64,128]{2,1,0:T(8,128)S(1)}, ...), condition=%wide.region_49.51_spmd, body=%wide.region_40.50_spmd.sunk | while | flops 391468032 | bytes 10571149 | solution.py:111
  1096.5 22.5 all-reduce.64.cloned.1.call-done
  1133.8 24.0 all-reduce.66.cloned.1.call-done
  1173.7 19.6 all-gather.3
  1209.4 112.4 %while.249 = (s32[]{:T(128)}, f32[12,64,128]{2,1,0:T(8,128)S(1)}, f32[4,64,12,64]{3,1,2,0:T(8,128)}, f32[4,64,128]{2,1,0:T(8,128)}, f32[4,64,128]{2,1,0:T(8,128)...) while((s32[]{:T(128)}, f32[12,64,128]{2,1,0:T(8,128)S(1)}, ...), condition=%wide.region_71.73_spmd, body=%wide.region_62.72_spmd.sunk | while | flops 391468032 | bytes 10571149 | solution.py:111
  1385.4 13.4 copy.727
  1464.7 16.4 reshape.2121
  1488.1 11.8 broadcast_in_dim_reshape.31
  1505.9 11.7 broadcast_in_dim_reshape.30
  1517.6 12.3 copy_bitcast_fusion.4
  1529.9 22.2 reshape.2129
  1564.1 67.4 %all-reduce.43 = (f32[2,4,12,64]{2,1,0,3:T(4,128)}, f32[2,3,12]{2,1,0:T(4,128)S(1)}) all-reduce(f32[2,4,12,64]{2,1,0,3:T(4,128)S(1)} %copy.724, f32[2,3,12]{2,1,0:T(4,128)S(1)} %pad_maximum_fusion.29), channel_id=12, replica_groups=mesh['dp'=4,'seq'=4,'head'=2] {'dp','seq'}, use_global_device_ids=true, to_apply=%region_94.96.clone | all-reduce | flops 6216 | bytes 49728
  1634.8 37.2 %all-reduce.39 = f32[2,4,256]{2,1,0:T(4,128)S(1)} all-reduce(f32[2,4,256]{2,1,0:T(4,128)S(1)} %pad_maximum_fusion.27), channel_id=13, replica_groups=mesh['dp'=4,'seq'=4,'head'=2] {'dp','seq','head'}, use_global_device_ids=true, to_apply=%region_95.97.clone | all-reduce | flops 2048 | bytes 16384
  1682.3 27.1 %reduce-scatter.31.cloned.1.call-done = f32[64,2]{1,0:T(8,128)} async-done(((f32[1024,2]{1,0:T(8,128)}), f32[64,2]{1,0:T(8,128)}) %reduce-scatter.31.cloned.1.call-update) | async-done | bytes 528
  1710.8 302.4 %all-reduce.70.cloned.1.call-done = (f32[2,256,1024]{1,0,2:T(2,128)}, f32[2,768,1024]{1,0,2:T(2,128)}, f32[2,1024,1024]{1,0,2:T(2,128)}) async-done(((f32[2,256,1024]{1,0,2:T(2,128)}, f32[2,768,1024]{1,0,2:T(2,128)}, f32[2,1024,1024]{1,0,2:T(2,128)}), (f32[2,256,1024]{1,0,2:T(2,128)}, f32[2,768,1024]{1,0,2:T(2,128)}, f32[2,1024,1024]{1,0,2:T(2,128)})) %all-reduce.70.cloned.1.call-update) | async-done | bytes 16777232
  2018.7 133.4 %reduce-scatter.33.cloned.1.call-done = f32[64,3072]{1,0:T(8,128)} async-done(((f32[1024,3072]{1,0:T(8,128)}), f32[64,3072]{1,0:T(8,128)}) %reduce-scatter.33.cloned.1.call-update) | async-done | bytes 786448
  2154.9 179.5 %reduce-scatter.39.cloned.1.call-done = f32[64,4096]{1,0:T(8,128)} async-done(((f32[1024,4096]{1,0:T(8,128)}), f32[64,4096]{1,0:T(8,128)}) %reduce-scatter.39.cloned.1.call-update) | async-done | bytes 1048592
  2337.5 57.8 %reduce-scatter.29.cloned.1.call-done = f32[2,64,1,128]{3,1,2,0:T(8,128)} async-done(((f32[2,1024,1,128]{3,1,2,0:T(8,128)}), f32[2,64,1,128]{3,1,2,0:T(8,128)}) %reduce-scatter.29.cloned.1.call-update) | async-done | bytes 65552 | tf_op jit(solution)/shard_map/reduce_scatter | solution.py:485
  2395.3 64.8 %reduce-scatter.27.cloned.1.call-done = f32[2,64,256]{2,1,0:T(8,128)} async-done(((f32[2,1024,256]{2,1,0:T(8,128)}), f32[2,64,256]{2,1,0:T(8,128)}) %reduce-scatter.27.cloned.1.call-update) | async-done | bytes 131088 | tf_op jit(solution)/shard_map/reduce_scatter | solution.py:484
  (1923 shorter events, 1241.2 us)
Async XLA Ops:
  7.2 385.1 %all-reduce.56.cloned.1.call-start = ((), (), s32[]{:S(2)}) async-start(), calls=%async_computation.9 | async-start | bytes 1048576 | tf_op jit(solution)/shard_map/psum | solution.py:297
  8.6 39.0 %copy-start.129 = (f32[1,1024]{1,0:T(1,128)}, f32[1,1024]{1,0:T(1,128)S(1)}, u32[]{:S(2)}) copy-start(f32[1,1024]{1,0:T(1,128)S(1)} %get-tuple-element.3940) | copy-start | bytes 12292
  9.8 37.8 %copy-start.190 = (f32[256]{0:T(256)}, f32[256]{0:T(256)S(1)}, u32[]{:S(2)}) copy-start(f32[256]{0:T(256)S(1)} %fusion.549) | copy-start | bytes 3076
  20.7 46.5 %collective-permute-start = (bf16[3,1024]{1,0:T(4,128)(2,1)S(1)}, bf16[3,1024]{1,0:T(4,128)(2,1)S(1)}, u32[]{:S(2)}, u32[]{:S(2)}) collective-permute-start(bf16[3,1024]{1,0:T(4,128)(2,1)S(1)} %pad_maximum_fusion.25), channel_id=1, source_target_pairs={{0,2},{2,4},{4,6},{1,3},{3,5},{5,7},{8,10},{10,12},{12,14},{9,11},... | collective-permute-start | bytes 18440 | tf_op jit(solution)/shard_map/ppermute | solution.py:19
  363.5 65.5 %all-reduce.58.cloned.1.call-start = ((), (), s32[]{:S(2)}) async-start(), calls=%async_computation.10 | async-start | bytes 1048576 | tf_op jit(solution)/shard_map/psum | solution.py:304
  400.2 459.0 %all-reduce.60.cloned.1.call-start = ((), (), s32[]{:S(2)}) async-start(), calls=%async_computation.11 | async-start | bytes 1048576 | tf_op jit(solution)/shard_map/psum | solution.py:297
  405.1 67.6 %copy-start.203 = (f32[1,1024]{1,0:T(1,128)}, f32[1,1024]{1,0:T(1,128)S(1)}, u32[]{:S(2)}) copy-start(f32[1,1024]{1,0:T(1,128)S(1)} %get-tuple-element.3923) | copy-start | bytes 12292
  405.1 67.6 %copy-start.205 = (f32[1,1024]{1,0:T(1,128)}, f32[1,1024]{1,0:T(1,128)S(1)}, u32[]{:S(2)}) copy-start(f32[1,1024]{1,0:T(1,128)S(1)} %get-tuple-element.3925) | copy-start | bytes 12292
  405.1 67.6 %copy-start.207 = (f32[1,1024]{1,0:T(1,128)}, f32[1,1024]{1,0:T(1,128)S(1)}, u32[]{:S(2)}) copy-start(f32[1,1024]{1,0:T(1,128)S(1)} %get-tuple-element.3926) | copy-start | bytes 12292
  405.1 67.6 %copy-start.225 = (f32[1,1024]{1,0:T(1,128)}, f32[1,1024]{1,0:T(1,128)S(1)}, u32[]{:S(2)}) copy-start(f32[1,1024]{1,0:T(1,128)S(1)} %get-tuple-element.3924) | copy-start | bytes 12292
  454.0 18.6 collective-permute-start.1
  823.2 111.2 %copy-start.12 = (f32[12,64,128]{2,1,0:T(8,128)}, f32[12,64,128]{2,1,0:T(8,128)S(1)}, u32[]{:S(2)}) copy-start(f32[12,64,128]{2,1,0:T(8,128)S(1)} %get-tuple-element.2183) | copy-start | bytes 1179652
  832.8 65.5 %all-reduce.62.cloned.1.call-start = ((), (), s32[]{:S(2)}) async-start(), calls=%async_computation.12 | async-start | bytes 1048576 | tf_op jit(solution)/shard_map/psum | solution.py:384
  860.5 40.0 %copy-start.242 = (f32[256]{0:T(256)}, f32[256]{0:T(256)S(1)}, u32[]{:S(2)}) copy-start(f32[256]{0:T(256)S(1)} %fusion.552) | copy-start | bytes 3076
  869.5 217.9 %reduce-scatter.23.cloned.1.call-start = ((), (), s32[]{:S(2)}) async-start(), calls=%async_computation.13 | async-start | bytes 327680 | tf_op jit(solution)/shard_map/reduce_scatter | solution.py:435
  872.2 29.9 %copy-start.97 = (bf16[2,256,1024]{2,1,0:T(8,128)(2,1)S(1)}, bf16[2,256,1024]{2,1,0:T(8,128)(2,1)}, u32[]{:S(2)}) copy-start(bf16[2,256,1024]{2,1,0:T(8,128)(2,1)} %param.49) | copy-start | bytes 3145732
  942.2 176.8 %all-reduce.64.cloned.1.call-start = ((), (), s32[]{:S(2)}) async-start(), calls=%async_computation.14 | async-start | bytes 1048576 | tf_op jit(solution)/shard_map/psum | solution.py:454
  1074.5 9.5 collective-permute-start.2
  1090.9 66.9 %all-reduce.66.cloned.1.call-start = ((), (), s32[]{:S(2)}) async-start(), calls=%async_computation.15 | async-start | bytes 1048576 | tf_op jit(solution)/shard_map/psum | solution.py:384
  1123.2 36.8 %copy-start.29 = (f32[256,1024]{1,0:T(8,128)}, f32[256,1024]{1,0:T(8,128)S(1)}, u32[]{:S(2)}) copy-start(f32[256,1024]{1,0:T(8,128)S(1)} %fusion.435) | copy-start | bytes 3145732
  1129.1 220.4 %reduce-scatter.25.cloned.1.call-start = ((), (), s32[]{:S(2)}) async-start(), calls=%async_computation.16 | async-start | bytes 327680 | tf_op jit(solution)/shard_map/reduce_scatter | solution.py:435
  1201.9 203.5 %all-reduce.72.cloned.1.call-start = ((), (), s32[]{:S(2)}) async-start(), calls=%async_computation.26 | async-start | bytes 2097152 | tf_op jit(solution)/shard_map/psum | solution.py:304
  1336.7 9.5 collective-permute-start.3
  1353.0 319.7 %reduce-scatter.37.cloned.1.call-start = ((), (), s32[]{:S(2)}) async-start(), calls=%async_computation.22 | async-start | bytes 557056
  1365.2 308.9 %reduce-scatter.35.cloned.1.call-start = ((), (), s32[]{:S(2)}) async-start(), calls=%async_computation.21 | async-start | bytes 557056
  1368.8 306.9 %all-reduce.68.cloned.1.call-start = ((), (), s32[]{:S(2)}) async-start(), calls=%async_computation.24 | async-start | bytes 4194304
  1376.3 333.1 %reduce-scatter.31.cloned.1.call-start = ((), (), s32[]{:S(2)}) async-start(), calls=%async_computation.19 | async-start | bytes 557056
  1410.7 602.6 %all-reduce.70.cloned.1.call-start = ((), (), s32[]{:S(2)}) async-start(), calls=%async_computation.25 | async-start | bytes 33554432
  1428.1 724.0 %reduce-scatter.33.cloned.1.call-start = ((), (), s32[]{:S(2)}) async-start(), calls=%async_computation.20 | async-start | bytes 13369344
  1481.2 853.2 %reduce-scatter.39.cloned.1.call-start = ((), (), s32[]{:S(2)}) async-start(), calls=%async_computation.23 | async-start | bytes 17825792
  1552.1 843.1 %reduce-scatter.29.cloned.1.call-start = ((), (), s32[]{:S(2)}) async-start(), calls=%async_computation.18 | async-start | bytes 1114112 | tf_op jit(solution)/shard_map/reduce_scatter | solution.py:485
  1555.0 905.1 %reduce-scatter.27.cloned.1.call-start = ((), (), s32[]{:S(2)}) async-start(), calls=%async_computation.17 | async-start | bytes 2228224 | tf_op jit(solution)/shard_map/reduce_scatter | solution.py:484
  (357 other events, 2091.7 us)
Sparse Core Ops, SparseCore 0:
  363.6 28.6 all-reduce.55
  400.3 28.5 all-reduce.57
  832.9 26.2 all-reduce.59
  869.6 28.5 all-reduce.61
  942.3 17.4 reduce-scatter.22
  1091.1 27.9 all-reduce.63
  1129.2 28.5 all-reduce.65
  1202.0 17.9 reduce-scatter.24
  1353.2 39.7 all-reduce.71
  1396.8 55.7 reduce-scatter.36
  1456.7 54.7 reduce-scatter.34
  1517.6 132.9 all-reduce.67
  1654.7 54.6 reduce-scatter.30
  1714.5 298.6 all-reduce.69
  2017.7 134.3 reduce-scatter.32
  2156.6 177.6 reduce-scatter.38
  2338.8 56.3 reduce-scatter.28
  2399.4 60.5 reduce-scatter.26
where the time goes:
time: 2500 us; the launch traced here: 2470 us
  waiting for transfers between devices  899 us (36%)
  local copies, waits for them, and re-layouts  698 us (28%)
  matrix products  338 us (14%)
  other arithmetic  259 us (10%)
  blocking collectives  224 us (9%)
    unnamed x25, waiting for transfers between devices  643 us
    dynamic_update_slice x144, local copies, waits for them, and re-layouts, ssm_scan(): lax.scan(block_step, (start_memory, start_doc), (into_blocks(values), int...  246 us
    unnamed x593, local copies, waits for them, and re-layouts  114 us
    unnamed x2, blocking collectives  105 us
    all_gather x6, blocking collectives, entering(): lax.all_gather(a.astype(kind), axis)  90.9 us
    dot_general x32, matrix products, block_step(): outputs = jnp.einsum('tsh,shp->thp', mixing, values, precision=highest)  68.7 us
    dynamic_update_slice x48, other arithmetic, ssm_scan(): lax.scan(block_step, (start_memory, start_doc), (into_blocks(values), int...  65 us
    reduce_scatter x1, waiting for transfers between devices, reduce_grads(): lax.psum_scatter(q_part, ('dp', 'seq'), scatter_dimension=1, tiled=True)  64.8 us
  transfers between devices with their start and end apart: 22, of which 12 were waited for; matrix products, arithmetic and copies ran while one was open for 23% of the time, Pallas kernels for 0%

commit v1 on v0

v1 whole, which is shorter than its diff:
```python
import functools

import jax
import jax.numpy as jnp
from jax import lax
from jax.experimental import pallas as pl
from jax.experimental.pallas import tpu as pltpu
from jax.sharding import PartitionSpec as P

NS = 128
HD = 64
RIM = 16

highest = lax.Precision.HIGHEST
norm_eps = 1e-05
masked_score = -1e30
bf16 = jnp.bfloat16
f32 = jnp.float32
VMEM_LIMIT = 56 * 1024 * 1024


def nn(left, right):
    return jnp.dot(left, right, preferred_element_type=f32)


def tn(left, right):
    return lax.dot_general(left, right, (((0,), (0,)), ((), ())), preferred_element_type=f32)


def nt(left, right):
    return lax.dot_general(left, right, (((1,), (1,)), ((), ())), preferred_element_type=f32)


def exact(left, right, contract=(1, 0)):
    return lax.dot_general(
        left,
        right,
        (((contract[0],), (contract[1],)), ((), ())),
        precision=highest,
        preferred_element_type=f32,
    )


def sigmoid(v):
    return 1.0 / (1.0 + jnp.exp(-v))


def softplus(v):
    return jnp.maximum(v, 0.0) + jnp.log(1.0 + jnp.exp(-jnp.abs(v)))


def head_map(heads, width):
    rows = lax.broadcasted_iota(jnp.int32, (128, heads * width), 0)
    columns = lax.broadcasted_iota(jnp.int32, (128, heads * width), 1)
    return (columns // width == rows).astype(f32)


def call(kernel, outs, scratch=(), **extra):
    return pl.pallas_call(
        kernel,
        out_shape=[jax.ShapeDtypeStruct(shape, kind) for shape, kind in outs],
        scratch_shapes=list(scratch),
        compiler_params=pltpu.CompilerParams(vmem_limit_bytes=VMEM_LIMIT),
        **extra,
    )


def rms_scaled(hidden, gain):
    return hidden * lax.rsqrt(jnp.mean(hidden * hidden, axis=-1, keepdims=True) + norm_eps) * gain


def project_kernel(h_ref, gain_ref, wzx_ref, wbc_ref, wdt_ref, wq_ref, wkv_ref,
                   normed_ref, gate_ref, stack_ref, dt_ref, q_ref, kv_ref):
    d_local = gate_ref.shape[1]
    normed_ref[...] = rms_scaled(h_ref[...], gain_ref[...]).astype(bf16)
    normed = normed_ref[...]
    q_ref[...] = nn(normed, wq_ref[...]).astype(bf16)
    kv_ref[...] = nn(normed, wkv_ref[...]).astype(bf16)
    dt_ref[...] = nn(normed, wdt_ref[...]).astype(bf16).astype(f32)
    stack_ref[:, d_local:] = nn(normed, wbc_ref[...]).astype(bf16)
    gate_ref[...] = nn(normed, wzx_ref[:, :d_local]).astype(bf16)
    stack_ref[:, :d_local] = nn(normed, wzx_ref[:, d_local:]).astype(bf16)


def ssm_scalars(dt_ref, heads_ref):
    rows = dt_ref.shape[0]
    raw = dt_ref[...] + heads_ref[0:1, :]
    step = softplus(raw)
    log_decay = -jnp.exp(heads_ref[1:2, :]) * step
    place_t = lax.broadcasted_iota(jnp.int32, (rows, rows), 0)
    place_s = lax.broadcasted_iota(jnp.int32, (rows, rows), 1)
    lower = (place_s <= place_t).astype(f32)
    running = exact(lower, log_decay)
    running_t = jnp.transpose(running)
    return raw, step, log_decay, running, running_t, place_t >= place_s


def spread(scalars, mapping):
    return exact(scalars, mapping)


def mix_local_kernel(heads, ext_ref, dt_ref, dcol_ref, dloc_ref, drow_ref, taps_ref, heads_ref,
                     q_ref, kv_ref,
                     y_ref, pre_ref, state_ref, dec_ref, crow_ref, att_ref, lse_ref, ext):
    rows = dt_ref.shape[0]
    d_local = y_ref.shape[1]
    ext[...] = ext_ref[...].astype(f32)
    pre = ext[RIM:RIM + rows, :] * taps_ref[0:1, :]
    for k in range(1, 4):
        pre = pre + ext[RIM - k:RIM - k + rows, :] * dcol_ref[:, k:k + 1] * taps_ref[k:k + 1, :]
    pre_ref[...] = pre
    raw, step, log_decay, running, running_t, ordered = ssm_scalars(dt_ref, heads_ref)
    mapping = head_map(heads, d_local // heads)
    last = running[rows - 1:rows, :]
    fade = jnp.exp(last - running) * dcol_ref[:, 5:6]
    dec = jnp.exp(running) * dcol_ref[:, 4:5]
    dec_ref[...] = dec
    mixed = pre_ref[...] * sigmoid(pre_ref[...])
    values = mixed[:, :d_local]
    b_rows = mixed[:, d_local:d_local + NS].astype(bf16)
    c_rows = mixed[:, d_local + NS:].astype(bf16)
    crow_ref[...] = c_rows
    stepped = values * spread(step, mapping)
    state_ref[...] = tn((stepped * spread(fade, mapping)).astype(bf16), b_rows)
    y_ref[...] = values * spread(heads_ref[2:3, :] + jnp.zeros((8, 128), f32), mapping)[0:1, :]
    linked = ordered & (dcol_ref[:, 0:1] == dloc_ref[0:1, :])
    cb = jnp.where(linked, nt(c_rows, b_rows), 0.0)
    stepped = stepped.astype(bf16)
    lane = lax.broadcasted_iota(jnp.int32, (rows, 128), 1)
    for pair in range(heads // 2):
        span = slice(pair * 128, pair * 128 + 128)
        sides = []
        for h in (2 * pair, 2 * pair + 1):
            gap = running[:, h:h + 1] - running_t[h:h + 1, :]
            mixing = (jnp.exp(jnp.minimum(gap, 0.0)) * cb).astype(bf16)
            sides.append(nn(mixing, stepped[:, span]))
        y_ref[:, span] += jnp.where(lane < 64, sides[0], sides[1])
    allowed = score_mask(dcol_ref, drow_ref)
    keyvals = kv_ref[...]
    keys, vals = keyvals[:, :HD], keyvals[:, HD:]
    totals = jnp.zeros((rows, 128), f32)
    for h in range(q_ref.shape[1] // HD):
        query = q_ref[:, h * HD:(h + 1) * HD] * jnp.asarray(HD ** -0.5, bf16)
        scores = jnp.where(allowed, nt(query, keys), masked_score)
        peak = jnp.max(scores, axis=1, keepdims=True)
        expo = jnp.exp(scores - peak)
        total = jnp.sum(expo, axis=1, keepdims=True)
        probs = (expo * (1.0 / total)).astype(bf16)
        att_ref[:, h * HD:(h + 1) * HD] = nn(probs, vals).astype(bf16)
        totals = jnp.where(lane == h, peak + jnp.log(total), totals)
    lse_ref[...] = totals


def score_mask(dcol_ref, drow_ref):
    rows, length = dcol_ref.shape[0], drow_ref.shape[1]
    query_pos = lax.broadcasted_iota(jnp.int32, (rows, length), 0) + lax.axis_index("seq") * rows
    key_pos = lax.broadcasted_iota(jnp.int32, (rows, length), 1)
    return (key_pos <= query_pos) & (dcol_ref[:, 0:1] == drow_ref[0:1, :])


def mix_finish_kernel(heads, y_ref, dec_ref, crow_ref, gate_ref, mem_ref, att_ref, wout_ref, wo_ref,
                      gated_ref, part_ref):
    d_local = y_ref.shape[1]
    mapping = head_map(heads, d_local // heads)
    carried = spread(dec_ref[...], mapping) * nt(crow_ref[...], mem_ref[...])
    gate = gate_ref[...].astype(f32)
    gated_ref[...] = ((y_ref[...] + carried) * (gate * sigmoid(gate))).astype(bf16)
    part_ref[...] = (nn(gated_ref[...], wout_ref[...]) + nn(att_ref[...], wo_ref[...])).astype(bf16)


def back_push_kernel(heads, branch_ref, wout_ref, wo_ref, gate_ref, dec_ref, crow_ref, q_ref, kv_ref,
                     att_ref, lse_ref, dcol_ref, drow_ref,
                     gg_ref, push_ref, dq_ref, dkv_ref, acc):
    d_local = gg_ref.shape[1]
    rows = gg_ref.shape[0]
    mapping = head_map(heads, d_local // heads)
    branch = branch_ref[...]
    gg_ref[...] = nt(branch, wout_ref[...])
    gate = gate_ref[...].astype(f32)
    grad_ssm = gg_ref[...] * (gate * sigmoid(gate))
    push_ref[...] = tn((grad_ssm * spread(dec_ref[...], mapping)).astype(bf16), crow_ref[...])
    grad_att = nt(branch, wo_ref[...])
    allowed = score_mask(dcol_ref, drow_ref)
    keyvals = kv_ref[...]
    keys, vals = keyvals[:, :HD], keyvals[:, HD:]
    scale = jnp.asarray(HD ** -0.5, bf16)
    for h in range(q_ref.shape[1] // HD):
        span = slice(h * HD, (h + 1) * HD)
        query = q_ref[:, span] * scale
        grad = grad_att[:, span].astype(bf16)
        delta = jnp.sum(grad.astype(f32) * att_ref[:, span].astype(f32), axis=1, keepdims=True)
        scores = jnp.where(allowed, nt(query, keys), masked_score)
        probs = jnp.exp(scores - lse_ref[:, h:h + 1])
        low = probs.astype(bf16)
        grad_scores = (probs * (nt(grad, vals) - delta)).astype(bf16)
        dq_ref[:, span] = (nn(grad_scores, keys) * HD ** -0.5).astype(bf16)
        dk = tn(grad_scores, query)
        dv = tn(low, grad)
        if h == 0:
            acc[:, :HD] = dk
            acc[:, HD:] = dv
        else:
            acc[:, :HD] += dk
            acc[:, HD:] += dv
    dkv_ref[...] = acc[...].astype(bf16)


def back_ssm_kernel(heads, ext_ref, pre_ref, dt_ref, dcol_ref, dloc_ref, taps_ref, heads_ref, gate_ref,
                    gg_ref, mem_ref, gmem_ref,
                    dgate_ref, dext_ref, draw_ref, dtaps_ref, dheads_ref, ext, dy_s, dxs_s, u_s, pad):
    rows = dt_ref.shape[0]
    d_local = gate_ref.shape[1]
    width = pre_ref.shape[1]
    mapping = head_map(heads, d_local // heads)
    raw, step, log_decay, running, running_t, ordered = ssm_scalars(dt_ref, heads_ref)
    last = running[rows - 1:rows, :]
    fade = spread(jnp.exp(last - running) * dcol_ref[:, 5:6], mapping)
    dec = jnp.exp(running) * dcol_ref[:, 4:5]
    steps = spread(step, mapping)
    skip = spread(heads_ref[2:3, :] + jnp.zeros((8, 128), f32), mapping)[0:1, :]
    pre_v = pre_ref[:, :d_local]
    values = pre_v * sigmoid(pre_v)
    pre_n = pre_ref[:, d_local:]
    maps = (pre_n * sigmoid(pre_n)).astype(bf16)
    b_rows, c_rows = maps[:, :NS], maps[:, NS:]
    stepped = (values * steps).astype(bf16)
    gate = gate_ref[...].astype(f32)
    gate_sig = sigmoid(gate)
    grad_ssm = gg_ref[...] * (gate * gate_sig)
    dy_s[...] = grad_ssm.astype(bf16)
    memory = mem_ref[...]
    gmem = gmem_ref[...]
    decs = spread(dec, mapping)
    carried = decs * nt(c_rows, memory)
    back = fade * nt(b_rows, gmem)
    linked = ordered & (dcol_ref[:, 0:1] == dloc_ref[0:1, :])
    cb = jnp.where(linked, nt(c_rows, b_rows), 0.0)
    dcb = jnp.zeros((rows, rows), f32)
    lane = lax.broadcasted_iota(jnp.int32, (rows, 128), 1)
    for pair in range(heads // 2):
        span = slice(pair * 128, pair * 128 + 128)
        stepped_p = stepped[:, span]
        dy_p = dy_s[:, span]
        ys, dxs = [], []
        for side, h in enumerate((2 * pair, 2 * pair + 1)):
            gap = running[:, h:h + 1] - running_t[h:h + 1, :]
            decay = jnp.exp(jnp.minimum(gap, 0.0))
            mixing = (decay * cb).astype(bf16)
            ys.append(nn(mixing, stepped_p))
            dxs.append(tn(mixing, dy_p))
            half = jnp.where((lane < 64) == (side == 0), dy_p, jnp.zeros_like(dy_p))
            dcb = dcb + nt(half, stepped_p) * decay
        u_s[:, span] = jnp.where(lane < 64, ys[0], ys[1])
        dxs_s[:, span] = jnp.where(lane < 64, dxs[0], dxs[1])
    dy_low = dy_s[...].astype(f32)
    stepped_f = stepped.astype(f32)
    scanned = u_s[...] + carried
    dxs_all = dxs_s[...] + back
    drun = exact(dy_low * scanned - stepped_f * dxs_all, mapping, (1, 1))
    ssm_out = scanned + skip * values
    dgate_ref[...] = (gg_ref[...] * ssm_out * (gate_sig * (1.0 + gate * (1.0 - gate_sig)))).astype(bf16)
    gstep = exact(values * dxs_all, mapping, (1, 1))
    ones = jnp.ones((8, 128), f32)
    moved = exact(ones, gmem.astype(f32) * memory.astype(f32), (1, 1))
    end = exact(jnp.sum(stepped_f * back, axis=0, keepdims=True) + jnp.zeros((8, 1), f32), mapping, (1, 1))
    end = end + exact(moved, mapping, (1, 1)) * dec[rows - 1:rows, :]
    upper = (lax.broadcasted_iota(jnp.int32, (rows, rows), 1)
             >= lax.broadcasted_iota(jnp.int32, (rows, rows), 0)).astype(f32)
    dlog = exact(upper, drun) + end[0:1, :]
    draw = (gstep - jnp.exp(heads_ref[1:2, :]) * dlog) * sigmoid(raw)
    draw_ref[...] = draw.astype(bf16)
    dskip = exact(jnp.sum(grad_ssm * values, axis=0, keepdims=True) + jnp.zeros((8, 1), f32), mapping, (1, 1))
    dheads_ref[...] = jnp.zeros((8, 128), f32)
    dheads_ref[0:1, :] = jnp.sum(draw, axis=0, keepdims=True)
    dheads_ref[1:2, :] = jnp.sum(dlog * log_decay, axis=0, keepdims=True)
    dheads_ref[2:3, :] = dskip[0:1, :]
    dcb = jnp.where(linked, dcb, 0.0).astype(bf16)
    dc = nn(dcb, b_rows) + nn((dy_low * decs).astype(bf16), memory)
    db = tn(dcb, c_rows) + nn((stepped_f * fade).astype(bf16), gmem)
    dvalues = steps * dxs_all + skip * grad_ssm

    pad[0:8, :] = jnp.zeros((8, width), f32)
    pad[8 + rows:, :] = jnp.zeros((8, width), f32)
    sig = sigmoid(pre_v)
    pad[8:8 + rows, :d_local] = dvalues * (sig * (1.0 + pre_v * (1.0 - sig)))
    sig = sigmoid(pre_n)
    slope = sig * (1.0 + pre_n * (1.0 - sig))
    pad[8:8 + rows, d_local:d_local + NS] = db * slope[:, :NS]
    pad[8:8 + rows, d_local + NS:] = dc * slope[:, NS:]
    ext[...] = ext_ref[...].astype(f32)
    dpre = pad[8:8 + rows, :]
    total = pad[0:8 + rows, :] * taps_ref[0:1, :]
    dext_ref[...] = total
    dtaps_ref[...] = jnp.zeros((8, width), f32)
    dtaps_ref[0:1, :] = jnp.sum(dpre * ext[RIM:RIM + rows, :], axis=0, keepdims=True)
    for k in range(1, 4):
        masked = dpre * dcol_ref[:, k:k + 1]
        pad[8:8 + rows, :] = masked
        dtaps_ref[k:k + 1, :] = jnp.sum(masked * ext[RIM - k:RIM - k + rows, :], axis=0, keepdims=True)
        dext_ref[...] += pad[k:k + 8 + rows, :] * taps_ref[k:k + 1, :]


def wgrad_kernel(terms, *refs):
    out_ref = refs[-1]
    at = 0
    for i, count in enumerate(terms):
        left = refs[at][...]
        at += 1
        for right in refs[at:at + count]:
            begin = right_offset(refs, terms, at, right)
            out_ref[:, begin:begin + right.shape[1]] = tn(left, right[...]).astype(out_ref.dtype)
        at += count


def right_offset(refs, terms, at, right):
    begin, place = 0, 0
    for count in terms:
        place += 1
        for ref in refs[place:place + count]:
            if ref is right:
                return begin
            begin += ref.shape[1]
        place += count
    return begin


def weight_grads(groups, blocks=8):
    operands, specs, columns, terms = [], [], 0, []
    for left, rights in groups:
        rows, width = left.shape
        operands.append(left)
        specs.append(pl.BlockSpec((rows, width // blocks), lambda i: (0, i)))
        for right in rights:
            operands.append(right)
            specs.append(pl.BlockSpec(right.shape, lambda i: (0, 0)))
            columns += right.shape[1]
        terms.append(len(rights))
    return pl.pallas_call(
        functools.partial(wgrad_kernel, tuple(terms)),
        grid=(blocks,),
        in_specs=specs,
        out_specs=pl.BlockSpec((width // blocks, columns), lambda i: (i, 0)),
        out_shape=jax.ShapeDtypeStruct((width, columns), bf16),
        compiler_params=pltpu.CompilerParams(vmem_limit_bytes=VMEM_LIMIT),
    )(*operands)


def pass_states(state, dec_last, heads, backward):
    count = lax.axis_size("seq")
    place = lax.axis_index("seq")
    states = lax.all_gather(state.astype(bf16), "seq")
    decays = lax.all_gather(dec_last, "seq")
    total = jnp.zeros(state.shape, f32)
    size = state.shape[0] // heads
    order = range(count) if not backward else range(count - 1, -1, -1)
    for source in order:
        ahead = source > place if backward else source < place
        decay = jnp.repeat(decays[source][:heads], size)[:, None]
        total = jnp.where(ahead, decay * total + states[source].astype(f32), total)
    return total.astype(bf16)


def from_behind(value, steps):
    count = lax.axis_size("seq")
    initial, last = (max(0, -steps), min(count, count - steps))
    return lax.ppermute(value, "seq", [(source, source + steps) for source in range(initial, last)])


def layer_forward(hidden, weights, context):
    dcol, dloc, drow = context
    rows, model_width = hidden.shape
    heads = weights["heads"]
    d_local = weights["out"].shape[0]
    ff_local = weights["down"].shape[0]
    width = d_local + 2 * NS
    normed, gate, stack, dt, queries, keyvals = call(
        project_kernel,
        [((rows, model_width), bf16), ((rows, d_local), bf16), ((rows, width), bf16),
         ((rows, 128), f32), ((rows, weights["q"].shape[1]), bf16), ((rows, 128), bf16)],
    )(hidden, weights["gain_mix"], weights["zx"], weights["bc"], weights["dt"], weights["q"], weights["kv"])
    ext = jnp.concatenate([from_behind(stack[rows - RIM:], 1), stack], axis=0)
    keyvals_all = lax.all_gather(keyvals, "seq", axis=0, tiled=True)
    local, pre, state, dec, crow, att, lse = call(
        functools.partial(mix_local_kernel, heads),
        [((rows, d_local), f32), ((rows, width), f32), ((d_local, NS), f32), ((rows, 128), f32),
         ((rows, NS), bf16), ((rows, weights["q"].shape[1]), bf16), ((rows, 128), f32)],
        [pltpu.VMEM((rows + RIM, width), f32)],
    )(ext, dt, dcol, dloc, drow, weights["taps"], weights["head_vals"], queries, keyvals_all)
    memory = pass_states(state, dec[-1], heads, False)
    gated, part = call(
        functools.partial(mix_finish_kernel, heads),
        [((rows, d_local), bf16), ((rows, model_width), bf16)],
    )(local, dec, crow, gate, memory, att, weights["out"], weights["o"])
    middle = hidden + lax.psum(part, "head").astype(f32)
    normed_ff = rms_scaled(middle, weights["gain_ff"]).astype(bf16)
    gate_up = nn(normed_ff, weights["gu"]).astype(bf16)
    inner = (jax.nn.silu(gate_up[:, :ff_local].astype(f32)) * gate_up[:, ff_local:].astype(f32)).astype(bf16)
    output = middle + lax.psum(nn(inner, weights["down"]).astype(bf16), "head").astype(f32)
    saved = (hidden, normed, gate, ext, pre, dt, queries, keyvals_all, dec, crow, att, lse, memory,
             gated, middle, normed_ff, gate_up, inner)
    return output, saved


def layer_backward(grad_out, weights, saved, context):
    dcol, dloc, drow = context
    (hidden, normed, gate, ext, pre, dt, queries, keyvals_all, dec, crow, att, lse, memory,
     gated, middle, normed_ff, gate_up, inner) = saved
    rows, model_width = hidden.shape
    heads = weights["heads"]
    d_local = gate.shape[1]
    ff_local = inner.shape[1]
    width = d_local + 2 * NS
    grad_ff = grad_out.astype(bf16)
    grad_inner = nt(grad_ff, weights["down"])
    gate_f = gate_up[:, :ff_local].astype(f32)
    up_f = gate_up[:, ff_local:].astype(f32)
    sig = jax.nn.sigmoid(gate_f)
    grad_gu = jnp.concatenate(
        [grad_inner * up_f * (sig * (1.0 + gate_f * (1.0 - sig))), grad_inner * gate_f * sig], axis=1
    ).astype(bf16)
    grad_nff = lax.psum(nt(grad_gu, weights["gu"]).astype(bf16), "head").astype(f32)
    ff_grads = weight_grads([(grad_ff, [inner]), (normed_ff, [grad_gu])])
    ff_sum = lax.psum_scatter(ff_grads, ("dp", "seq"), scatter_dimension=0, tiled=True)
    _, pull = jax.vjp(rms_scaled, middle, weights["gain_ff"])
    grad_middle, g_gain_ff = pull(grad_nff)
    grad_middle = grad_middle + grad_out
    branch = grad_middle.astype(bf16)
    gg, push, dq, dkv = call(
        functools.partial(back_push_kernel, heads),
        [((rows, d_local), f32), ((d_local, NS), f32), (queries.shape, bf16), (keyvals_all.shape, bf16)],
        [pltpu.VMEM(keyvals_all.shape, f32)],
    )(branch, weights["out"], weights["o"], gate, dec, crow, queries, keyvals_all, att, lse, dcol, drow)
    gmem = pass_states(push, dec[-1], heads, True)
    grad_kv = lax.psum_scatter(dkv, "seq", scatter_dimension=0, tiled=True)
    dgate, dext, draw, dtaps, dheads = call(
        functools.partial(back_ssm_kernel, heads),
        [((rows, d_local), bf16), ((rows + 8, width), f32), ((rows, 128), bf16), ((8, width), f32),
         ((8, 128), f32)],
        [pltpu.VMEM((rows + RIM, width), f32), pltpu.VMEM((rows, d_local), bf16),
         pltpu.VMEM((rows, d_local), f32), pltpu.VMEM((rows, d_local), f32),
         pltpu.VMEM((rows + 16, width), f32)],
    )(ext, pre, dt, dcol, dloc, weights["taps"], weights["head_vals"], gate, gg, memory, gmem)
    rim = from_behind(dext[:8], -1)
    dstack = dext[8:] + jnp.concatenate([jnp.zeros((rows - 8, width), f32), rim], axis=0)
    dx = dstack[:, :d_local].astype(bf16)
    dbc = dstack[:, d_local:].astype(bf16)
    grad_normed = (
        nt(dgate, weights["zx"][:, :d_local]) + nt(dx, weights["zx"][:, d_local:]) + nt(dbc, weights["bc"])
        + nt(draw, weights["dt"]) + nt(dq, weights["q"]) + nt(grad_kv, weights["kv"])
    )
    grad_normed = lax.psum(grad_normed.astype(bf16), "head").astype(f32)
    mix_grads = weight_grads([(normed, [dgate, dx, dq, grad_kv, draw]), (branch, [gated, att])])
    mix_sum = lax.psum_scatter(mix_grads, ("dp", "seq"), scatter_dimension=0, tiled=True)
    _, pull = jax.vjp(rms_scaled, hidden, weights["gain_mix"])
    grad_hidden, g_gain_mix = pull(grad_normed)
    grad_hidden = grad_hidden + grad_middle
    g_bc = jnp.concatenate(
        [tn(dbc, normed), jnp.pad(jnp.transpose(dtaps[:4, d_local:]), ((0, 0), (0, 124)))], axis=1
    )
    shards = lax.axis_size("dp") * lax.axis_size("seq")
    taps = dtaps[:4, :d_local].reshape(4, heads, shards, -1)
    small = jnp.concatenate(
        [g_gain_mix.reshape(shards, -1), g_gain_ff.reshape(shards, -1),
         jnp.transpose(taps, (2, 0, 1, 3)).reshape(shards, -1),
         jnp.broadcast_to(dheads[:3, :heads].reshape(1, -1), (shards, 3 * heads))], axis=1
    )
    return grad_hidden, ff_sum, mix_sum, g_bc, small


def on_device(hidden_in, segment_ids, gain_mix, w_zx, w_bc, w_dt, conv_x, conv_bc, ssm_head, w_q, w_kv,
              w_o, w_out, gain_ff, w_gu, w_down, cotangent):
    rows, model_width = hidden_in.shape
    taps_count = conv_x.shape[1]
    place = lax.axis_index("seq")
    offset = place * rows
    doc_all = segment_ids[0]
    padded = jnp.concatenate([jnp.full((taps_count - 1,), -1, jnp.int32), doc_all])
    doc_ext = lax.dynamic_slice_in_dim(padded, offset, rows + taps_count - 1)
    docs = doc_ext[taps_count - 1:]
    columns = [docs.astype(f32)]
    for k in range(1, taps_count):
        columns.append((doc_ext[taps_count - 1 - k:taps_count - 1 - k + rows] == docs).astype(f32))
    columns.append((docs == doc_ext[taps_count - 2]).astype(f32))
    columns.append((docs == docs[-1]).astype(f32))
    dcol = jnp.pad(jnp.stack(columns, axis=1), ((0, 0), (0, 128 - len(columns))))
    dloc = jnp.broadcast_to(docs.astype(f32)[None], (8, rows))
    drow = jnp.broadcast_to(doc_all.astype(f32)[None], (8, doc_all.shape[0]))
    context = (dcol, dloc, drow)
    layers = gain_mix.shape[0]
    heads = ssm_head.shape[2]
    d_local = w_zx.shape[3]
    all_weights = []
    for l in range(layers):
        all_weights.append(dict(
            heads=heads,
            gain_mix=gain_mix[l][None].astype(f32),
            gain_ff=gain_ff[l][None].astype(f32),
            zx=w_zx[l].reshape(model_width, -1),
            bc=w_bc[l],
            dt=jnp.pad(w_dt[l], ((0, 0), (0, 128 - heads))),
            q=w_q[l],
            kv=w_kv[l].reshape(model_width, -1),
            o=w_o[l],
            out=w_out[l],
            gu=w_gu[l].reshape(model_width, -1),
            down=w_down[l],
            taps=jnp.pad(jnp.concatenate([conv_x[l].reshape(taps_count, -1), conv_bc[l]], axis=1).astype(f32),
                         ((0, 8 - taps_count), (0, 0))),
            head_vals=jnp.pad(ssm_head[l], ((0, 5), (0, 128 - heads))),
        ))
    hidden = hidden_in.astype(f32)
    saved = []
    output = hidden
    for l in range(layers):
        output, kept = layer_forward(hidden, all_weights[l], context)
        saved.append(kept)
        hidden = output.astype(bf16).astype(f32)
    block_out = output.astype(bf16)
    gradient = cotangent.astype(f32)
    parts = [None] * layers
    for l in reversed(range(layers)):
        gradient, *parts[l] = layer_backward(gradient, all_weights[l], saved[l], context)
    g_bc = lax.psum_scatter(jnp.concatenate([p[2] for p in parts], axis=1), ("dp", "seq", "head"),
                            scatter_dimension=0, tiled=True)
    small = lax.psum_scatter(jnp.concatenate([p[3] for p in parts], axis=1), ("dp", "seq"),
                             scatter_dimension=0, tiled=True)
    ff_local = w_down.shape[1]
    q_width = w_q.shape[2]
    part = model_width // (lax.axis_size("dp") * lax.axis_size("seq"))

    def both(pieces):
        return jnp.stack(pieces, axis=0).astype(f32)

    def cut(index, begin, size):
        return [p[index][:, begin:begin + size] for p in parts]

    down = both([jnp.transpose(a) for a in cut(0, 0, ff_local)])
    gu = both(cut(0, ff_local, 2 * ff_local)).reshape(layers, part, 2, ff_local)
    at = 2 * d_local
    zx = both(cut(1, 0, at)).reshape(layers, part, 2, d_local)
    q = both(cut(1, at, q_width))
    at += q_width
    kv = both(cut(1, at, 128)).reshape(layers, part, 1, 128)
    at += 128
    dt = both(cut(1, at, heads))
    at += 128
    out = both([jnp.transpose(a) for a in cut(1, at, d_local)])
    at += d_local
    o = both([jnp.transpose(a) for a in cut(1, at, q_width)])
    g_bc = g_bc.reshape(g_bc.shape[0], layers, -1)
    w_bc_grad = jnp.transpose(g_bc[:, :, :model_width], (1, 2, 0))
    conv_bc_grad = jnp.transpose(g_bc[:, :, model_width:model_width + taps_count], (1, 2, 0))
    small = small.reshape(layers, -1)
    gain_a = small[:, :part]
    gain_b = small[:, part:2 * part]
    taps_end = 2 * part + taps_count * d_local // (model_width // part)
    conv_x_grad = small[:, 2 * part:taps_end].reshape(layers, taps_count, heads, -1)
    head_grad = small[:, taps_end:].reshape(layers, 3, heads)
    return (block_out, gradient, gain_a, zx, w_bc_grad, dt, conv_x_grad, conv_bc_grad, head_grad, q, kv,
            o, out, gain_b, gu, down)


def solution(mesh):
    in_specs = (
        P(("dp", "seq"), None),
        P("dp", None),
        P(),
        P(None, None, None, "head"),
        P(),
        P(None, None, "head"),
        P(None, None, "head", None),
        P(),
        P(None, None, "head"),
        P(None, None, "head"),
        P(None, None, "head", None),
        P(None, "head", None),
        P(None, "head", None),
        P(),
        P(None, None, None, "head"),
        P(None, "head", None),
        P(("dp", "seq"), None),
    )
    out_specs = (
        P(("dp", "seq"), None),
        P(("dp", "seq"), None),
        P(None, ("dp", "seq")),
        P(None, ("dp", "seq"), None, "head"),
        P(None, None, ("dp", "seq", "head")),
        P(None, ("dp", "seq"), "head"),
        P(None, None, "head", ("dp", "seq")),
        P(None, None, ("dp", "seq", "head")),
        P(None, None, "head"),
        P(None, ("dp", "seq"), "head"),
        P(None, ("dp", "seq"), "head", None),
        P(None, "head", ("dp", "seq")),
        P(None, "head", ("dp", "seq")),
        P(None, ("dp", "seq")),
        P(None, ("dp", "seq"), None, "head"),
        P(None, "head", ("dp", "seq")),
    )
    return jax.shard_map(
        on_device, mesh=mesh, in_specs=in_specs, out_specs=out_specs, check_vma=False
    )
```

time: 2500 us -> 1030 us (0.41); the launches traced: 2470 us -> 1020 us
  local copies, waits for them, and re-layouts: 698 us -> 99.3 us
  waiting for transfers between devices: 899 us -> 492 us
  matrix products: 338 us -> 46.6 us
  other arithmetic: 259 us -> 52.2 us
  Pallas kernels: 0 us -> 108 us
  blocking collectives: 224 us -> 197 us
    unnamed x25 -> x14, waiting for transfers between devices: 643 us -> 0.23 us
    dot_general x200 -> x22, matrix products: 338 us -> 46.6 us  [the longest x16 31.7 us: nt(): lax.dot_general(left, right, (((1,), (1,)), ((), ())), preferred_element_...]
    dynamic_update_slice x144 -> x0, local copies, waits for them, and re-layouts: 246 us -> none  [ssm_scan(): lax.scan(block_step, (start_memory, start_doc), (into_blocks(values), int...]
    reduce_scatter x4 -> x7, waiting for transfers between devices: 123 us -> 349 us  [the longest x2 171 us: layer_backward(): lax.psum_scatter(mix_grads, ('dp', 'seq'), scatter_dimension=0, tiled=True)]
    pallas_call x0 -> x14, Pallas kernels: none -> 108 us  [the longest x4 32.3 us: weight_grads(): pl.pallas_call(functools.partial(wgrad_kernel, tuple(terms)), grid=(block...]
    another operation x115 -> x21, local copies, waits for them, and re-layouts: 99.2 us -> 10.9 us  [the longest x16 8.72 us: both(): return jnp.stack(pieces, axis=0).astype(f32)]
    unnamed x593 -> x147, local copies, waits for them, and re-layouts: 114 us -> 31.6 us
    dynamic_update_slice x48 -> x0, other arithmetic: 65 us -> none  [ssm_scan(): lax.scan(block_step, (start_memory, start_doc), (into_blocks(values), int...]
  transfers between devices with their start and end apart: 22 -> 18, of which waited for: 12 -> 13; matrix products, arithmetic and copies ran while one was open for 23% -> 10% of each run, Pallas kernels for 0% -> 6%
where the time goes in v1:
time: 1030 us; the launch traced here: 1020 us
  waiting for transfers between devices  492 us (48%)
  blocking collectives  197 us (19%)
  Pallas kernels  108 us (10%)
  local copies, waits for them, and re-layouts  99.3 us (10%)
  other arithmetic  52.2 us (5%)
  matrix products  46.6 us (5%)
  between operations  15.2 us (1%)
  starting transfers between devices  12.3 us (1%)
    reduce_scatter x2, waiting for transfers between devices, layer_backward(): lax.psum_scatter(mix_grads, ('dp', 'seq'), scatter_dimension=0, tiled=True)  171 us
    reduce_scatter x2, waiting for transfers between devices, layer_backward(): lax.psum_scatter(ff_grads, ('dp', 'seq'), scatter_dimension=0, tiled=True)  170 us
    all_gather x4, blocking collectives, pass_states(): states = lax.all_gather(state.astype(bf16), 'seq')  82.2 us
    unnamed x1, blocking collectives  66.8 us
    psum x2, waiting for transfers between devices, layer_backward(): lax.psum(nt(grad_gu, weights['gu']).astype(bf16), 'head').astype(f32)  52.6 us
    psum x2, waiting for transfers between devices, layer_forward(): middle = hidden + lax.psum(part, 'head').astype(f32)  37.1 us
    pallas_call x4, Pallas kernels, weight_grads(): pl.pallas_call(functools.partial(wgrad_kernel, tuple(terms)), grid=(block...  32.3 us
    dot_general x16, matrix products, nt(): lax.dot_general(left, right, (((1,), (1,)), ((), ())), preferred_element_...  31.7 us
  transfers between devices with their start and end apart: 18, of which 13 were waited for; matrix products, arithmetic and copies ran while one was open for 10% of the time, Pallas kernels for 6%

profile of v1, /device:TPU:0, one launch (start us, length us, event | category | flops | bytes accessed | tf_op | source)
XLA Modules:
  0.0 1022.6 jit_solution(13657050765748482651)
XLA Ops:
  13.8 7.9 fusion.164
  44.8 15.1 %all_gather.38.kv_ref = bf16[1024,128]{1,0:T(8,128)(2,1)} all-gather(bf16[256,128]{1,0:T(8,128)(2,1)S(1)} %copy-done.51), channel_id=1, replica_groups=mesh['dp'=4,'seq'=4,'head'=2] {'seq'}, dimensions={0}, use_global_device_ids=true | all-gather | bytes 327680 | tf_op jit(solution)/shard_map/all_gather | solution.py:382
  62.7 8.1 shard_map.289
  71.5 8.7 all-gather.4
  81.8 17.8 %all-gather = bf16[3072,128]{1,0:T(8,128)(2,1)S(1)} all-gather(bf16[768,128]{1,0:T(8,128)(2,1)S(1)} %convert_element_type.301), channel_id=2, replica_groups=mesh['dp'=4,'seq'=4,'head'=2] {'seq'}, dimensions={0}, use_global_device_ids=true | all-gather | bytes 983040 | tf_op jit(solution)/shard_map/all_gather | solution.py:351
  105.4 8.1 fusion.163
  116.9 16.3 %all-reduce.22.cloned.1.call-done = bf16[256,1024]{1,0:T(8,128)(2,1)} async-done(((bf16[256,1024]{1,0:T(8,128)(2,1)}), bf16[256,1024]{1,0:T(8,128)(2,1)}) %all-reduce.22.cloned.1.call-update) | async-done | bytes 524304 | tf_op jit(solution)/shard_map/psum | solution.py:394
  149.7 22.2 %all-reduce.24.cloned.1.call-done = bf16[256,1024]{1,0:T(8,128)(2,1)} async-done(((bf16[256,1024]{1,0:T(8,128)(2,1)}), bf16[256,1024]{1,0:T(8,128)(2,1)}) %all-reduce.24.cloned.1.call-update) | async-done | bytes 524304 | tf_op jit(solution)/shard_map/psum | solution.py:398
  183.3 15.1 %all_gather.42.kv_ref = bf16[1024,128]{1,0:T(8,128)(2,1)} all-gather(bf16[256,128]{1,0:T(8,128)(2,1)} %get-tuple-element.78), channel_id=1, replica_groups=mesh['dp'=4,'seq'=4,'head'=2] {'seq'}, dimensions={0}, use_global_device_ids=true | all-gather | bytes 327680 | tf_op jit(solution)/shard_map/all_gather | solution.py:382
  200.4 8.1 shard_map.292
  209.1 9.0 all-gather.5
  219.7 17.3 %all-gather.1 = bf16[3072,128]{1,0:T(8,128)(2,1)S(1)} all-gather(bf16[768,128]{1,0:T(8,128)(2,1)S(1)} %convert_element_type.322), channel_id=3, replica_groups=mesh['dp'=4,'seq'=4,'head'=2] {'seq'}, dimensions={0}, use_global_device_ids=true | all-gather | bytes 983040 | tf_op jit(solution)/shard_map/all_gather | solution.py:351
  248.7 20.8 %all-reduce.26.cloned.1.call-done = bf16[256,1024]{1,0:T(8,128)(2,1)} async-done(((bf16[256,1024]{1,0:T(8,128)(2,1)}), bf16[256,1024]{1,0:T(8,128)(2,1)}) %all-reduce.26.cloned.1.call-update) | async-done | bytes 524304 | tf_op jit(solution)/shard_map/psum | solution.py:394
  281.1 28.7 %all-reduce.28.cloned.1.call-done = bf16[256,1024]{1,0:T(8,128)(2,1)} async-done(((bf16[256,1024]{1,0:T(8,128)(2,1)}), bf16[256,1024]{1,0:T(8,128)(2,1)}) %all-reduce.28.cloned.1.call-update) | async-done | bytes 524304 | tf_op jit(solution)/shard_map/psum | solution.py:421
  313.7 8.1 shard_map.294
  323.0 23.5 %all-gather.2 = bf16[3072,128]{1,0:T(8,128)(2,1)S(1)} all-gather(bf16[768,128]{1,0:T(8,128)(2,1)S(1)} %convert_element_type.345), channel_id=4, replica_groups=mesh['dp'=4,'seq'=4,'head'=2] {'seq'}, dimensions={0}, use_global_device_ids=true | all-gather | bytes 983040 | tf_op jit(solution)/shard_map/all_gather | solution.py:351
  347.6 12.1 %shard_map.295 = (bf16[256,768]{1,0:T(8,128)(2,1)}, f32[264,1024]{1,0:T(8,128)}, bf16[256,128]{1,0:T(8,128)(2,1)}, f32[8,1024]{1,0:T(8,128)}, f32[8,128]{1,0:T(8,128)}) custom-call(bf16[272,1024]{1,0:T(8,128)(2,1)} %copy-done.21, f32[256,1024]{1,0:T(8,128)} %get-tuple-element.87.pre_ref, f32[256,128]{1,0:T(8,128)} %get-tuple-element.76.dt_ref, ...), custom_call_target="tpu_custom_call" | custom-call | tf_op jit(solution)/shard_map/pallas_call | solution.py:435
  375.4 27.9 %all-reduce.30.cloned.1.call-done = bf16[256,1024]{1,0:T(8,128)(2,1)} async-done(((bf16[256,1024]{1,0:T(8,128)(2,1)}), bf16[256,1024]{1,0:T(8,128)(2,1)}) %all-reduce.30.cloned.1.call-update) | async-done | bytes 524304 | tf_op jit(solution)/shard_map/psum | solution.py:451
  417.5 23.9 %all-reduce.32.cloned.1.call-done = bf16[256,1024]{1,0:T(8,128)(2,1)} async-done(((bf16[256,1024]{1,0:T(8,128)(2,1)}), bf16[256,1024]{1,0:T(8,128)(2,1)}) %all-reduce.32.cloned.1.call-update) | async-done | bytes 524304 | tf_op jit(solution)/shard_map/psum | solution.py:421
  447.1 8.2 shard_map.296
  456.4 23.5 %all-gather.3 = bf16[3072,128]{1,0:T(8,128)(2,1)S(1)} all-gather(bf16[768,128]{1,0:T(8,128)(2,1)S(1)} %convert_element_type.361), channel_id=5, replica_groups=mesh['dp'=4,'seq'=4,'head'=2] {'seq'}, dimensions={0}, use_global_device_ids=true | all-gather | bytes 983040 | tf_op jit(solution)/shard_map/all_gather | solution.py:351
  481.0 12.1 %shard_map.297 = (bf16[256,768]{1,0:T(8,128)(2,1)}, f32[264,1024]{1,0:T(8,128)}, bf16[256,128]{1,0:T(8,128)(2,1)}, f32[8,1024]{1,0:T(8,128)}, f32[8,128]{1,0:T(8,128)}) custom-call(bf16[272,1024]{1,0:T(8,128)(2,1)} %copy-done.20, f32[256,1024]{1,0:T(8,128)} %get-tuple-element.86.pre_ref, f32[256,128]{1,0:T(8,128)} %get-tuple-element.65.dt_ref, ...), custom_call_target="tpu_custom_call" | custom-call | tf_op jit(solution)/shard_map/pallas_call | solution.py:435
  515.3 8.0 shard_map.301
  524.2 8.1 shard_map.299
  534.6 8.0 shard_map.300
  544.4 8.1 shard_map.298
  568.7 66.8 %all-reduce.12 = f32[16,712]{0,1:T(8,128)} all-reduce(f32[16,712]{0,1:T(8,128)S(1)} %concatenate.53), channel_id=8, replica_groups=mesh['dp'=4,'seq'=4,'head'=2] {'dp','seq'}, use_global_device_ids=true, to_apply=%region_22.23.clone | all-reduce | flops 11392 | bytes 91136
  643.8 8.5 reduce-scatter.17.cloned.1.call-done
  655.1 85.4 %reduce-scatter.21.cloned.1.call-done = bf16[64,3072]{1,0:T(8,128)(2,1)} async-done(((bf16[1024,3072]{1,0:T(8,128)(2,1)}), bf16[64,3072]{1,0:T(8,128)(2,1)}) %reduce-scatter.21.cloned.1.call-update) | async-done | bytes 393232 | tf_op jit(solution)/shard_map/reduce_scatter | solution.py:423
  742.5 86.8 %reduce-scatter.15.cloned.1.call-done = bf16[64,3072]{1,0:T(8,128)(2,1)} async-done(((bf16[1024,3072]{1,0:T(8,128)(2,1)}), bf16[64,3072]{1,0:T(8,128)(2,1)}) %reduce-scatter.15.cloned.1.call-update) | async-done | bytes 393232 | tf_op jit(solution)/shard_map/reduce_scatter | solution.py:453
  833.5 84.3 %reduce-scatter.19.cloned.1.call-done = bf16[64,3072]{1,0:T(8,128)(2,1)} async-done(((bf16[1024,3072]{1,0:T(8,128)(2,1)}), bf16[64,3072]{1,0:T(8,128)(2,1)}) %reduce-scatter.19.cloned.1.call-update) | async-done | bytes 393232 | tf_op jit(solution)/shard_map/reduce_scatter | solution.py:423
  922.3 84.3 %reduce-scatter.13.cloned.1.call-done = bf16[64,3072]{1,0:T(8,128)(2,1)} async-done(((bf16[1024,3072]{1,0:T(8,128)(2,1)}), bf16[64,3072]{1,0:T(8,128)(2,1)}) %reduce-scatter.13.cloned.1.call-update) | async-done | bytes 393232 | tf_op jit(solution)/shard_map/reduce_scatter | solution.py:453
  (368 shorter events, 216.7 us)
Async XLA Ops:
  7.2 126.0 %all-reduce.22.cloned.1.call-start = ((), (), s32[]{:S(2)}) async-start(), calls=%async_computation.7 | async-start | bytes 1048576 | tf_op jit(solution)/shard_map/psum | solution.py:394
  26.1 11.7 %copy-start.36 = (bf16[2,256,1024]{2,1,0:T(8,128)(2,1)S(1)}, bf16[2,256,1024]{2,1,0:T(8,128)(2,1)}, u32[]{:S(2)}) copy-start(bf16[2,256,1024]{2,1,0:T(8,128)(2,1)} %param.28) | copy-start | bytes 3145732
  32.0 29.4 %collective-permute-start = (bf16[16,1024]{1,0:T(8,128)(2,1)S(1)}, bf16[16,1024]{1,0:T(8,128)(2,1)S(1)}, u32[]{:S(2)}, u32[]{:S(2)}) collective-permute-start(bf16[16,1024]{1,0:T(8,128)(2,1)S(1)} %slice.391), channel_id=1, source_target_pairs={{0,2},{2,4},{4,6},{1,3},{3,5},{5,7},{8,10},{10,12},{12,14},{9,11},... | collective-permute-start | bytes 98312 | tf_op jit(solution)/shard_map/ppermute | solution.py:366
  38.9 22.4 %copy-start.37 = (bf16[256,1024]{1,0:T(8,128)(2,1)S(1)}, bf16[256,1024]{1,0:T(8,128)(2,1)}, u32[]{:S(2)}) copy-start(bf16[256,1024]{1,0:T(8,128)(2,1)} %get-tuple-element.64) | copy-start | bytes 1572868
  105.3 66.5 %all-reduce.24.cloned.1.call-start = ((), (), s32[]{:S(2)}) async-start(), calls=%async_computation.8 | async-start | bytes 1048576 | tf_op jit(solution)/shard_map/psum | solution.py:398
  113.5 19.7 %copy-start = (bf16[256,1024]{1,0:T(8,128)(2,1)S(1)}, bf16[256,1024]{1,0:T(8,128)(2,1)}, u32[]{:S(2)}) copy-start(bf16[256,1024]{1,0:T(8,128)(2,1)} %param.17) | copy-start | bytes 1572868
  143.1 126.4 %all-reduce.26.cloned.1.call-start = ((), (), s32[]{:S(2)}) async-start(), calls=%async_computation.9 | async-start | bytes 1048576 | tf_op jit(solution)/shard_map/psum | solution.py:394
  144.9 27.0 %copy-start.4 = (bf16[256,1024]{1,0:T(8,128)(2,1)S(1)}, bf16[256,1024]{1,0:T(8,128)(2,1)}, u32[]{:S(2)}) copy-start(bf16[256,1024]{1,0:T(8,128)(2,1)} %all-reduce.22.cloned.1.call-done) | copy-start | bytes 1572868
  179.9 18.5 %collective-permute-start.1 = (bf16[16,1024]{1,0:T(8,128)(2,1)S(1)}, bf16[16,1024]{1,0:T(8,128)(2,1)S(1)}, u32[]{:S(2)}, u32[]{:S(2)}) collective-permute-start(bf16[16,1024]{1,0:T(8,128)(2,1)S(1)} %slice.427), channel_id=1, source_target_pairs={{0,2},{2,4},{4,6},{1,3},{3,5},{5,7},{8,10},{10,12},{12,14},{9,11},... | collective-permute-start | bytes 98312 | tf_op jit(solution)/shard_map/ppermute | solution.py:366
  242.8 67.0 %all-reduce.28.cloned.1.call-start = ((), (), s32[]{:S(2)}) async-start(), calls=%async_computation.10 | async-start | bytes 1048576 | tf_op jit(solution)/shard_map/psum | solution.py:421
  278.9 30.9 %copy-start.1 = (bf16[256,1024]{1,0:T(8,128)(2,1)S(1)}, bf16[256,1024]{1,0:T(8,128)(2,1)}, u32[]{:S(2)}) copy-start(bf16[256,1024]{1,0:T(8,128)(2,1)} %all-reduce.26.cloned.1.call-done) | copy-start | bytes 1572868
  281.0 88.5 %reduce-scatter.9.cloned.1.call-start = ((), (), s32[]{:S(2)}) async-start(), calls=%async_computation.11 | async-start | bytes 327680 | tf_op jit(solution)/shard_map/reduce_scatter | solution.py:434
  321.9 81.4 %all-reduce.30.cloned.1.call-start = ((), (), s32[]{:S(2)}) async-start(), calls=%async_computation.12 | async-start | bytes 1048576 | tf_op jit(solution)/shard_map/psum | solution.py:451
  346.5 15.5 %copy-start.10 = (bf16[2,1024,256]{2,1,0:T(8,128)(2,1)S(1)}, bf16[2,1024,256]{2,1,0:T(8,128)(2,1)}, u32[]{:S(2)}) copy-start(bf16[2,1024,256]{2,1,0:T(8,128)(2,1)} %param.26) | copy-start | bytes 3145732
  346.5 15.5 %copy-start.38 = (bf16[256,256]{1,0:T(8,128)(2,1)S(1)}, bf16[256,256]{1,0:T(8,128)(2,1)}, u32[]{:S(2)}) copy-start(bf16[256,256]{1,0:T(8,128)(2,1)} %get-tuple-element.94.refs_3_) | copy-start | bytes 393220
  347.6 15.7 %copy-start.23 = (bf16[1,1024,12]{2,1,0:T(8,128)(2,1)S(1)}, bf16[1,1024,12]{2,1,0:T(8,128)(2,1)}, u32[]{:S(2)}) copy-start(bf16[1,1024,12]{2,1,0:T(8,128)(2,1)} %copy-done.22) | copy-start | bytes 73732
  360.6 5.9 collective-permute-start.2
  370.7 32.6 %copy-start.49 = (f32[1,1024]{1,0:T(1,128)S(1)}, f32[1,1024]{1,0:T(1,128)}, u32[]{:S(2)}) copy-start(f32[1,1024]{1,0:T(1,128)} %get-tuple-element.239.gain_ref) | copy-start | bytes 12292
  370.7 34.2 %copy-start.6 = (bf16[256,1024]{1,0:T(8,128)(2,1)S(1)}, bf16[256,1024]{1,0:T(8,128)(2,1)}, u32[]{:S(2)}) copy-start(bf16[256,1024]{1,0:T(8,128)(2,1)} %all-reduce.28.cloned.1.call-done) | copy-start | bytes 1572868
  375.1 66.3 %all-reduce.32.cloned.1.call-start = ((), (), s32[]{:S(2)}) async-start(), calls=%async_computation.13 | async-start | bytes 1048576 | tf_op jit(solution)/shard_map/psum | solution.py:421
  412.7 90.2 %reduce-scatter.11.cloned.1.call-start = ((), (), s32[]{:S(2)}) async-start(), calls=%async_computation.14 | async-start | bytes 327680 | tf_op jit(solution)/shard_map/reduce_scatter | solution.py:434
  455.3 103.9 %all-reduce.34.cloned.1.call-start = ((), (), s32[]{:S(2)}) async-start(), calls=%async_computation.20 | async-start | bytes 2097152 | tf_op jit(solution)/shard_map/psum | solution.py:398
  479.9 15.5 %copy-start.11 = (bf16[2,1024,256]{2,1,0:T(8,128)(2,1)S(1)}, bf16[2,1024,256]{2,1,0:T(8,128)(2,1)}, u32[]{:S(2)}) copy-start(bf16[2,1024,256]{2,1,0:T(8,128)(2,1)} %param.26) | copy-start | bytes 3145732
  479.9 15.5 %copy-start.39 = (bf16[256,256]{1,0:T(8,128)(2,1)S(1)}, bf16[256,256]{1,0:T(8,128)(2,1)}, u32[]{:S(2)}) copy-start(bf16[256,256]{1,0:T(8,128)(2,1)} %get-tuple-element.102.refs_3_) | copy-start | bytes 393220
  494.0 5.9 collective-permute-start.3
  508.1 144.1 %reduce-scatter.17.cloned.1.call-start = ((), (), s32[]{:S(2)}) async-start(), calls=%async_computation.17 | async-start | bytes 2433024 | tf_op jit(solution)/shard_map/reduce_scatter | solution.py:523
  513.0 227.4 %reduce-scatter.21.cloned.1.call-start = ((), (), s32[]{:S(2)}) async-start(), calls=%async_computation.19 | async-start | bytes 6684672 | tf_op jit(solution)/shard_map/reduce_scatter | solution.py:423
  523.3 306.0 %reduce-scatter.15.cloned.1.call-start = ((), (), s32[]{:S(2)}) async-start(), calls=%async_computation.16 | async-start | bytes 6684672 | tf_op jit(solution)/shard_map/reduce_scatter | solution.py:453
  532.3 385.5 %reduce-scatter.19.cloned.1.call-start = ((), (), s32[]{:S(2)}) async-start(), calls=%async_computation.18 | async-start | bytes 6684672 | tf_op jit(solution)/shard_map/reduce_scatter | solution.py:423
  542.6 464.0 %reduce-scatter.13.cloned.1.call-start = ((), (), s32[]{:S(2)}) async-start(), calls=%async_computation.15 | async-start | bytes 6684672 | tf_op jit(solution)/shard_map/reduce_scatter | solution.py:453
  560.8 81.7 %copy-start.15 = (f32[256,1024]{1,0:T(8,128)S(1)}, f32[256,1024]{1,0:T(8,128)}, u32[]{:S(2)}) copy-start(f32[256,1024]{1,0:T(8,128)} %get-tuple-element.205) | copy-start | bytes 3145732
  560.8 81.7 %copy-start.30 = (bf16[256,1024]{1,0:T(8,128)(2,1)S(1)}, bf16[256,1024]{1,0:T(8,128)(2,1)}, u32[]{:S(2)}) copy-start(bf16[256,1024]{1,0:T(8,128)(2,1)} %get-tuple-element.203) | copy-start | bytes 1572868
  (50 other events, 187.2 us)
Sparse Core Ops, SparseCore 0:
  105.5 27.6 all-reduce.21
  143.2 28.5 all-reduce.23
  242.9 26.5 all-reduce.25
  281.2 28.5 all-reduce.27
  322.0 21.2 reduce-scatter.8
  375.3 27.9 all-reduce.29
  412.8 28.5 all-reduce.31
  455.4 21.1 reduce-scatter.10
  508.2 38.3 all-reduce.33
  552.6 99.5 reduce-scatter.16
  656.2 84.2 reduce-scatter.20
  744.8 84.4 reduce-scatter.14
  833.2 84.5 reduce-scatter.18
  922.1 84.4 reduce-scatter.12

commit v2 on v1

--- a/solution.py
+++ b/solution.py
@@ -366,45 +366,270 @@
     return lax.ppermute(value, "seq", [(source, source + steps) for source in range(initial, last)])
 
 
-def layer_forward(hidden, weights, context):
+MESH_ID = pl.DeviceIdType.MESH
+CHUNK = 128
+
+
+def remote(src, dst, send, recv, axis, target):
+    return pltpu.make_async_remote_copy(
+        src_ref=src, dst_ref=dst, send_sem=send, recv_sem=recv,
+        device_id={axis: target}, device_id_type=MESH_ID,
+    )
+
+
+def meet(count, later_sends):
+    place = lax.axis_index("seq")
+    barrier = pltpu.get_barrier_semaphore()
+    for j in range(1, count):
+        here = place - j if not later_sends else place + j
+
+        @pl.when((here >= 0) & (here < count))
+        def _():
+            pl.semaphore_signal(barrier, inc=1, device_id={"seq": here}, device_id_type=MESH_ID)
+    heads_axis = lax.axis_size("head")
+    partner = lax.rem(lax.axis_index("head") + 1, heads_axis)
+    pl.semaphore_signal(barrier, inc=1, device_id={"head": partner}, device_id_type=MESH_ID)
+    waits = (place if later_sends else count - 1 - place) + 1
+    pl.semaphore_wait(barrier, waits)
+    return partner
+
+
+def layer_forward_kernel(heads, h_ref, gain_mix_ref, gain_ff_ref, wzx_ref, wbc_ref, wdt_ref, wq_ref, wkv_ref,
+                         taps_ref, heads_ref, dcol_ref, dloc_ref, drow_ref,
+                         wo_hbm, wout_hbm, wgu_hbm, wdown_hbm,
+                         h_out, normed_ref, gate_ref, stack_ref, rim_ref, pre_ref, dt_ref, q_ref, kvall_ref,
+                         att_ref, lse_ref, mem_ref, gated_ref, middle_ref, nff_ref, gu_ref, inner_ref,
+                         ext, y, wo_ref, wout_ref, wgu_ref, wdown_ref, rim_in, kv_in, chain_in, chain_out,
+                         part_out, part_in, down_out, down_in,
+                         load_sem, kv_send, kv_recv, rim_send, rim_recv, chain_send, chain_recv,
+                         part_send, part_recv, down_send, down_recv):
+    rows = dt_ref.shape[0]
+    d_local = gate_ref.shape[1]
+    ff_local = inner_ref.shape[1]
+    count = lax.axis_size("seq")
+    place = lax.axis_index("seq")
+    loads = [
+        pltpu.make_async_copy(src, dst, load_sem.at[i])
+        for i, (src, dst) in enumerate(((wout_hbm, wout_ref), (wo_hbm, wo_ref), (wgu_hbm, wgu_ref),
+                                        (wdown_hbm, wdown_ref)))
+    ]
+    for load in loads:
+        load.start()
+    partner = meet(count, False)
+
+    normed_ref[...] = rms_scaled(h_ref[...].astype(f32), gain_mix_ref[...]).astype(bf16)
+    normed = normed_ref[...]
+    own = pl.ds(pl.multiple_of(place * rows, rows), rows)
+    for j in range(count):
+        @pl.when(j > place)
+        def _():
+            kv_in[j * rows:(j + 1) * rows, :] = jnp.zeros((rows, 2 * HD), bf16)
+    kv_in[own, :] = nn(normed, wkv_ref[...]).astype(bf16)
+    kv_copies = [
+        remote(kv_in.at[own], kv_in.at[own], kv_send.at[j - 1], kv_recv.at[j - 1], "seq", place + j)
+        for j in range(1, count)
+    ]
+    for j in range(1, count):
+        @pl.when(place + j < count)
+        def _():
+            kv_copies[j - 1].start()
+    stack_ref[:, d_local:] = nn(normed, wbc_ref[...]).astype(bf16)
+    stack_ref[:, :d_local] = nn(normed, wzx_ref[:, d_local:]).astype(bf16)
+    rim_copy = remote(stack_ref.at[pl.ds(rows - RIM, RIM)], rim_in, rim_send, rim_recv, "seq", place + 1)
+
+    @pl.when(place + 1 < count)
+    def _():
+        rim_copy.start()
+
+    @pl.when(place == 0)
+    def _():
+        rim_in[...] = jnp.zeros(rim_in.shape, bf16)
+        chain_in[...] = jnp.zeros(chain_in.shape, bf16)
+    dt_ref[...] = nn(normed, wdt_ref[...]).astype(bf16).astype(f32)
+    gate_ref[...] = nn(normed, wzx_ref[:, :d_local]).astype(bf16)
+    q_ref[...] = nn(normed, wq_ref[...]).astype(bf16)
+    raw, step, log_decay, running, running_t, ordered = ssm_scalars(dt_ref, heads_ref)
+    mapping = head_map(heads, d_local // heads)
+    last = running[rows - 1:rows, :]
+    fade = jnp.exp(last - running) * dcol_ref[:, 5:6]
+    dec = jnp.exp(running) * dcol_ref[:, 4:5]
+    ends = jnp.exp(running_t[:, rows - 1:rows]) * dcol_ref[rows - 1:rows, 4:5] + jnp.zeros((128, NS), f32)
+    ends = exact(mapping, ends, (0, 0))
+    steps = spread(step, mapping)
+    ext[RIM:, :] = stack_ref[...].astype(f32)
+
+    @pl.when(place > 0)
+    def _():
+        rim_copy.wait_recv()
+    rim_ref[...] = rim_in[...]
+    ext[0:RIM, :] = rim_in[...].astype(f32)
+    pre = ext[RIM:RIM + rows, :] * taps_ref[0:1, :]
+    for k in range(1, 4):
+        pre = pre + ext[RIM - k:RIM - k + rows, :] * dcol_ref[:, k:k + 1] * taps_ref[k:k + 1, :]
+    pre_ref[...] = pre
+    mixed = pre_ref[...] * sigmoid(pre_ref[...])
+    values = mixed[:, :d_local]
+    b_rows = mixed[:, d_local:d_local + NS].astype(bf16)
+    c_rows = mixed[:, d_local + NS:].astype(bf16)
+    stepped = values * steps
+    state = tn((stepped * spread(fade, mapping)).astype(bf16), b_rows)
+    y[...] = values * spread(heads_ref[2:3, :] + jnp.zeros((8, 128), f32), mapping)[0:1, :]
+    linked = ordered & (dcol_ref[:, 0:1] == dloc_ref[0:1, :])
+    cb = jnp.where(linked, nt(c_rows, b_rows), 0.0)
+    stepped = stepped.astype(bf16)
+    lane = lax.broadcasted_iota(jnp.int32, (rows, 128), 1)
+
+    for j in range(1, count):
+        @pl.when(place - j >= 0)
+        def _():
+            kv_copies[j - 1].wait_recv()
+    allowed = score_mask(dcol_ref, drow_ref)
+    keyvals = kv_in[...]
+    kvall_ref[...] = keyvals
+    keys, vals = keyvals[:, :HD], keyvals[:, HD:]
+    totals = jnp.zeros((rows, 128), f32)
+    pairs = heads // 2
+    query_heads = q_ref.shape[1] // HD
+    chain_copies = []
+    for pair in range(pairs):
+        span = slice(pair * 128, pair * 128 + 128)
+        copy = remote(chain_out.at[pl.ds(pair * 128, 128)], chain_in.at[pl.ds(pair * 128, 128)],
+                      chain_send.at[pair], chain_recv.at[pair], "seq", place + 1)
+        chain_copies.append(copy)
+
+        @pl.when(place > 0)
+        def _():
+            copy.wait_recv()
+        chain_out[span, :] = (ends[span] * chain_in[span, :].astype(f32) + state[span]).astype(bf16)
+
+        @pl.when(place + 1 < count)
+        def _():
+            copy.start()
+        sides = []
+        for h in (2 * pair, 2 * pair + 1):
+            gap = running[:, h:h + 1] - running_t[h:h + 1, :]
+            mixing = (jnp.exp(jnp.minimum(gap, 0.0)) * cb).astype(bf16)
+            sides.append(nn(mixing, stepped[:, span]))
+        y[:, span] += jnp.where(lane < 64, sides[0], sides[1])
+        for h in range(query_heads * pair // pairs, query_heads * (pair + 1) // pairs):
+            query = q_ref[:, h * HD:(h + 1) * HD] * jnp.asarray(HD ** -0.5, bf16)
+            scores = jnp.where(allowed, nt(query, keys), masked_score)
+            peak = jnp.max(scores, axis=1, keepdims=True)
+            expo = jnp.exp(scores - peak)
+            total = jnp.sum(expo, axis=1, keepdims=True)
+            probs = (expo * (1.0 / total)).astype(bf16)
+            att_ref[:, h * HD:(h + 1) * HD] = nn(probs, vals).astype(bf16)
+            totals = jnp.where(lane == h, peak + jnp.log(total), totals)
+    lse_ref[...] = totals
+    mem_ref[...] = chain_in[...]
+    decs = spread(dec, mapping)
+    carried = decs * nt(c_rows, mem_ref[...])
+    gate = gate_ref[...].astype(f32)
+    gated_ref[...] = ((y[...] + carried) * (gate * sigmoid(gate))).astype(bf16)
+    loads[0].wait()
+    loads[1].wait()
+    chunks = [pl.ds(begin, CHUNK) for begin in range(0, rows, CHUNK)]
+    part_copies, down_copies = [], []
+    for i, chunk in enumerate(chunks):
+        part_out[chunk, :] = (nn(gated_ref[chunk, :], wout_ref[...])
+                              + nn(att_ref[chunk, :], wo_ref[...])).astype(bf16)
+        copy = remote(part_out.at[chunk], part_in.at[chunk], part_send.at[i], part_recv.at[i], "head", partner)
+        copy.start()
+        part_copies.append(copy)
+    loads[2].wait()
+    loads[3].wait()
+    for i, chunk in enumerate(chunks):
+        part_copies[i].wait_recv()
+        middle_ref[chunk, :] = h_ref[chunk, :].astype(f32) + (
+            part_out[chunk, :].astype(f32) + part_in[chunk, :].astype(f32))
+        nff_ref[chunk, :] = rms_scaled(middle_ref[chunk, :], gain_ff_ref[...]).astype(bf16)
+        gu_ref[chunk, :] = nn(nff_ref[chunk, :], wgu_ref[...]).astype(bf16)
+        gate = gu_ref[chunk, :ff_local].astype(f32)
+        inner_ref[chunk, :] = (gate * sigmoid(gate) * gu_ref[chunk, ff_local:].astype(f32)).astype(bf16)
+        down_out[chunk, :] = nn(inner_ref[chunk, :], wdown_ref[...]).astype(bf16)
+        copy = remote(down_out.at[chunk], down_in.at[chunk], down_send.at[i], down_recv.at[i], "head", partner)
+        copy.start()
+        down_copies.append(copy)
+    for i, chunk in enumerate(chunks):
+        down_copies[i].wait_recv()
+        h_out[chunk, :] = (middle_ref[chunk, :] + (
+            down_out[chunk, :].astype(f32) + down_in[chunk, :].astype(f32))).astype(bf16)
+    for i in range(len(chunks)):
+        part_copies[i].wait_send()
+        down_copies[i].wait_send()
+
+    @pl.when(place + 1 < count)
+    def _():
+        rim_copy.wait_send()
+        for copy in chain_copies:
+            copy.wait_send()
+    for j in range(1, count):
+        @pl.when(place + j < count)
+        def _():
+            kv_copies[j - 1].wait_send()
+
+
+VM = pl.BlockSpec(memory_space=pltpu.VMEM)
+ANY = pl.BlockSpec(memory_space=pl.ANY)
+DMA = pltpu.SemaphoreType.DMA
+
+
+def layer_forward(hidden, w, context):
     dcol, dloc, drow = context
     rows, model_width = hidden.shape
-    heads = weights["heads"]
-    d_local = weights["out"].shape[0]
-    ff_local = weights["down"].shape[0]
+    heads = w["heads"]
+    d_local = w["out"].shape[0]
+    ff_local = w["down"].shape[0]
+    q_width = w["q"].shape[1]
     width = d_local + 2 * NS
-    normed, gate, stack, dt, queries, keyvals = call(
-        project_kernel,
-        [((rows, model_width), bf16), ((rows, d_local), bf16), ((rows, width), bf16),
-         ((rows, 128), f32), ((rows, weights["q"].shape[1]), bf16), ((rows, 128), bf16)],
-    )(hidden, weights["gain_mix"], weights["zx"], weights["bc"], weights["dt"], weights["q"], weights["kv"])
-    ext = jnp.concatenate([from_behind(stack[rows - RIM:], 1), stack], axis=0)
-    keyvals_all = lax.all_gather(keyvals, "seq", axis=0, tiled=True)
-    local, pre, state, dec, crow, att, lse = call(
-        functools.partial(mix_local_kernel, heads),
-        [((rows, d_local), f32), ((rows, width), f32), ((d_local, NS), f32), ((rows, 128), f32),
-         ((rows, NS), bf16), ((rows, weights["q"].shape[1]), bf16), ((rows, 128), f32)],
-        [pltpu.VMEM((rows + RIM, width), f32)],
-    )(ext, dt, dcol, dloc, drow, weights["taps"], weights["head_vals"], queries, keyvals_all)
-    memory = pass_states(state, dec[-1], heads, False)
-    gated, part = call(
-        functools.partial(mix_finish_kernel, heads),
-        [((rows, d_local), bf16), ((rows, model_width), bf16)],
-    )(local, dec, crow, gate, memory, att, weights["out"], weights["o"])
-    middle = hidden + lax.psum(part, "head").astype(f32)
-    normed_ff = rms_scaled(middle, weights["gain_ff"]).astype(bf16)
-    gate_up = nn(normed_ff, weights["gu"]).astype(bf16)
-    inner = (jax.nn.silu(gate_up[:, :ff_local].astype(f32)) * gate_up[:, ff_local:].astype(f32)).astype(bf16)
-    output = middle + lax.psum(nn(inner, weights["down"]).astype(bf16), "head").astype(f32)
-    saved = (hidden, normed, gate, ext, pre, dt, queries, keyvals_all, dec, crow, att, lse, memory,
-             gated, middle, normed_ff, gate_up, inner)
-    return output, saved
+    count = lax.axis_size("seq")
+    length = count * rows
+    parts = rows // CHUNK
+    outs = [
+        ((rows, model_width), bf16), ((rows, model_width), bf16), ((rows, d_local), bf16), ((rows, width), bf16),
+        ((RIM, width), bf16), ((rows, width), f32), ((rows, 128), f32), ((rows, q_width), bf16),
+        ((length, 2 * HD), bf16), ((rows, q_width), bf16), ((rows, 128), f32), ((d_local, NS), bf16),
+        ((rows, d_local), bf16), ((rows, model_width), f32), ((rows, model_width), bf16),
+        ((rows, 2 * ff_local), bf16), ((rows, ff_local), bf16),
+    ]
+    full = (rows, model_width)
+    result = pl.pallas_call(
+        functools.partial(layer_forward_kernel, heads),
+        out_shape=[jax.ShapeDtypeStruct(shape, kind) for shape, kind in outs],
+        in_specs=[VM] * 13 + [ANY] * 4,
+        out_specs=[VM] * len(outs),
+        scratch_shapes=[
+            pltpu.VMEM((rows + RIM, width), f32), pltpu.VMEM((rows, d_local), f32),
+            pltpu.VMEM(w["o"].shape, bf16), pltpu.VMEM(w["out"].shape, bf16),
+            pltpu.VMEM(w["gu"].shape, bf16), pltpu.VMEM(w["down"].shape, bf16),
+            pltpu.VMEM((RIM, width), bf16), pltpu.VMEM((length, 2 * HD), bf16),
+            pltpu.VMEM((d_local, NS), bf16), pltpu.VMEM((d_local, NS), bf16),
+            pltpu.VMEM(full, bf16), pltpu.VMEM(full, bf16), pltpu.VMEM(full, bf16), pltpu.VMEM(full, bf16),
+            DMA((4,)), DMA((count - 1,)), DMA((count - 1,)), DMA, DMA, DMA((heads // 2,)), DMA((heads // 2,)),
+            DMA((parts,)), DMA((parts,)), DMA((parts,)), DMA((parts,)),
+        ],
+        compiler_params=pltpu.CompilerParams(
+            vmem_limit_bytes=VMEM_LIMIT, collective_id=0, has_side_effects=True),
+    )(hidden, w["gain_mix"], w["gain_ff"], w["zx"], w["bc"], w["dt"], w["q"], w["kv"], w["taps"],
+      w["head_vals"], dcol, dloc, drow, w["o"], w["out"], w["gu"], w["down"])
+    names = ("out", "normed", "gate", "stack", "rim", "pre", "dt", "q", "kv", "att", "lse", "memory",
+             "gated", "middle", "nff", "gu", "inner")
+    saved = dict(zip(names, result))
+    saved["hidden"] = hidden
+    return saved.pop("out"), saved
 
 
 def layer_backward(grad_out, weights, saved, context):
     dcol, dloc, drow = context
-    (hidden, normed, gate, ext, pre, dt, queries, keyvals_all, dec, crow, att, lse, memory,
-     gated, middle, normed_ff, gate_up, inner) = saved
+    hidden, normed, gate, pre, dt = (saved[name] for name in ("hidden", "normed", "gate", "pre", "dt"))
+    queries, keyvals_all, att, lse, memory = (saved[name] for name in ("q", "kv", "att", "lse", "memory"))
+    gated, middle, normed_ff, gate_up, inner = (saved[name] for name in ("gated", "middle", "nff", "gu", "inner"))
+    hidden = hidden.astype(f32)
+    ext = jnp.concatenate([saved["rim"], saved["stack"]], axis=0)
+    step = jax.nn.softplus(dt + weights["head_vals"][0:1])
+    dec = jnp.exp(jnp.cumsum(-jnp.exp(weights["head_vals"][1:2]) * step, axis=0)) * dcol[:, 4:5]
+    crow = pre[:, pre.shape[1] - NS:]
+    crow = (crow * jax.nn.sigmoid(crow)).astype(bf16)
     rows, model_width = hidden.shape
     heads = weights["heads"]
     d_local = gate.shape[1]
@@ -508,14 +733,12 @@
                          ((0, 8 - taps_count), (0, 0))),
             head_vals=jnp.pad(ssm_head[l], ((0, 5), (0, 128 - heads))),
         ))
-    hidden = hidden_in.astype(f32)
+    hidden = hidden_in
     saved = []
-    output = hidden
     for l in range(layers):
-        output, kept = layer_forward(hidden, all_weights[l], context)
+        hidden, kept = layer_forward(hidden, all_weights[l], context)
         saved.append(kept)
-        hidden = output.astype(bf16).astype(f32)
-    block_out = output.astype(bf16)
+    block_out = hidden
     gradient = cotangent.astype(f32)
     parts = [None] * layers
     for l in reversed(range(layers)):

time: 1030 us -> 927 us (0.900)
  waiting for transfers between devices: 492 us -> 423 us
  blocking collectives: 197 us -> 133 us
  Pallas kernels: 108 us -> 170 us
  local copies, waits for them, and re-layouts: 99.3 us -> 86.9 us
    pallas_call x6 -> x2, Pallas kernels: 35.4 us -> 97 us  [layer_forward(): pl.pallas_call(functools.partial(layer_forward_kernel, heads), out_shape=...]
    psum x4 -> x0, waiting for transfers between devices: 59.3 us -> none  [the longest x2 37.1 us: layer_forward(): middle = hidden + lax.psum(part, 'head').astype(f32)]
    all_gather x4 -> x2, blocking collectives: 82.2 us -> 39.8 us  [pass_states(): states = lax.all_gather(state.astype(bf16), 'seq')]
    all_gather x2 -> x0, blocking collectives: 30.2 us -> none  [layer_forward(): keyvals_all = lax.all_gather(keyvals, 'seq', axis=0, tiled=True)]
    reduce_scatter x2, waiting for transfers between devices: 0.01 us -> 22.4 us  [layer_backward(): grad_kv = lax.psum_scatter(dkv, 'seq', scatter_dimension=0, tiled=True)]
    psum x2, waiting for transfers between devices: 52.6 us -> 31.4 us  [layer_backward(): lax.psum(nt(grad_gu, weights['gu']).astype(bf16), 'head').astype(f32)]
    dot_general x4 -> x0, matrix products: 12 us -> none  [nn(): return jnp.dot(left, right, preferred_element_type=f32)]
    psum x1 -> x2, waiting for transfers between devices: 27.9 us -> 17.2 us  [layer_backward(): grad_normed = lax.psum(grad_normed.astype(bf16), 'head').astype(f32)]
  transfers between devices with their start and end apart: 18 -> 13, of which waited for: 13 -> 11; matrix products, arithmetic and copies ran while one was open for 10% -> 7% of each run, Pallas kernels for 6% -> 4%
where the time goes in v2:
time: 927 us; the launch traced here: 916 us
  waiting for transfers between devices  423 us (46%)
  Pallas kernels  170 us (18%)
  blocking collectives  133 us (14%)
  local copies, waits for them, and re-layouts  86.9 us (9%)
  other arithmetic  46.5 us (5%)
  matrix products  39.2 us (4%)
  between operations  15.2 us (2%)
    reduce_scatter x2, waiting for transfers between devices, layer_backward(): lax.psum_scatter(ff_grads, ('dp', 'seq'), scatter_dimension=0, tiled=True)  170 us
    reduce_scatter x2, waiting for transfers between devices, layer_backward(): lax.psum_scatter(mix_grads, ('dp', 'seq'), scatter_dimension=0, tiled=True)  170 us
    pallas_call x2, Pallas kernels, layer_forward(): pl.pallas_call(functools.partial(layer_forward_kernel, heads), out_shape=...  97 us
    unnamed x1, blocking collectives  66 us
    all_gather x2, blocking collectives, pass_states(): states = lax.all_gather(state.astype(bf16), 'seq')  39.8 us
    dot_general x16, matrix products, nt(): lax.dot_general(left, right, (((1,), (1,)), ((), ())), preferred_element_...  35.3 us
    pallas_call x4, Pallas kernels, weight_grads(): pl.pallas_call(functools.partial(wgrad_kernel, tuple(terms)), grid=(block...  32.4 us
    psum x2, waiting for transfers between devices, layer_backward(): lax.psum(nt(grad_gu, weights['gu']).astype(bf16), 'head').astype(f32)  31.4 us
  transfers between devices with their start and end apart: 13, of which 11 were waited for; matrix products, arithmetic and copies ran while one was open for 7% of the time, Pallas kernels for 4%

profile of v2, /device:TPU:0, one launch (start us, length us, event | category | flops | bytes accessed | tf_op | source)
XLA Modules:
  0.0 916.3 jit_solution(3054450079591951375)
XLA Ops:
  15.1 6.8 fusion.148
  24.2 6.8 fusion.147
  31.0 3.4 copy.155
  37.8 4.7 slice_bitcast_fusion
  47.3 3.5 copy.157
  56.3 47.7 %shard_map.288 = (bf16[256,1024]{1,0:T(8,128)(2,1)}, bf16[256,1024]{1,0:T(8,128)(2,1)}, bf16[256,768]{1,0:T(8,128)(2,1)}, bf16[256,1024]{1,0:T(8,128)(2,1)}, bf1...) custom-call(bf16[256,1024]{1,0:T(8,128)(2,1)} %h_ref.1, ...), custom_call_target="tpu_custom_call" | custom-call | tf_op jit(solution)/shard_map/pallas_call | solution.py:596
  104.0 49.3 %shard_map.289 = (bf16[256,1024]{1,0:T(8,128)(2,1)}, bf16[256,1024]{1,0:T(8,128)(2,1)}, bf16[256,768]{1,0:T(8,128)(2,1)}, bf16[256,1024]{1,0:T(8,128)(2,1)}, bf1...) custom-call(bf16[256,1024]{1,0:T(8,128)(2,1)} %get-tuple-element.68., ...), custom_call_target="tpu_custom_call" | custom-call | tf_op jit(solution)/shard_map/pallas_call | solution.py:596
  162.8 18.7 %all-gather.2 = f32[4,1,128]{2,1,0:T(1,128)S(1)} all-gather(f32[1,1,128]{2,1,0:T(1,128)S(1)} %slice_bitcast_fusion.32), channel_id=1, replica_groups=mesh['dp'=4,'seq'=4,'head'=2] {'seq'}, dimensions={0}, use_global_device_ids=true | all-gather | bytes 2560 | tf_op jit(solution)/shard_map/all_gather | solution.py:352
  186.3 9.3 %all-reduce.18.cloned.1.call-done = bf16[256,1024]{1,0:T(8,128)(2,1)} async-done(((bf16[256,1024]{1,0:T(8,128)(2,1)}), bf16[256,1024]{1,0:T(8,128)(2,1)}) %all-reduce.18.cloned.1.call-update) | async-done | bytes 524304 | tf_op jit(solution)/shard_map/psum | solution.py:646
  199.5 8.2 shard_map.290
  208.7 20.0 %all-gather = bf16[3072,128]{1,0:T(8,128)(2,1)S(1)} all-gather(bf16[768,128]{1,0:T(8,128)(2,1)S(1)} %convert_element_type.217), channel_id=2, replica_groups=mesh['dp'=4,'seq'=4,'head'=2] {'seq'}, dimensions={0}, use_global_device_ids=true | all-gather | bytes 983040 | tf_op jit(solution)/shard_map/all_gather | solution.py:351
  229.8 12.0 %shard_map.291 = (bf16[256,768]{1,0:T(8,128)(2,1)}, f32[264,1024]{1,0:T(8,128)}, bf16[256,128]{1,0:T(8,128)(2,1)}, f32[8,1024]{1,0:T(8,128)}, f32[8,128]{1,0:T(8,128)}) custom-call(bf16[272,1024]{1,0:T(8,128)(2,1)} %pad_maximum_fusion.3.ext_ref, f32[256,1024]{1,0:T(8,128)} %get-tuple-element.77.pre_ref, f32[256,128]{1,0:T(8,128)} %get-tuple-element.78.dt_ref, ...), custom_call_target="tpu_custom_call" | custom-call | tf_op jit(solution)/shard_map/pallas_call | solution.py:660
  255.5 13.0 %reduce-scatter.9.cloned.1.call-done.refs_4_ = bf16[256,128]{1,0:T(8,128)(2,1)} async-done(((bf16[1024,128]{1,0:T(8,128)(2,1)}), bf16[256,128]{1,0:T(8,128)(2,1)}) %reduce-scatter.9.cloned.1.call-update) | async-done | bytes 65552 | tf_op jit(solution)/shard_map/reduce_scatter | solution.py:659
  269.9 3.9 fusion.43
  273.8 8.2 all-gather.3
  283.6 17.1 %all-reduce.20.cloned.1.call-done = bf16[256,1024]{1,0:T(8,128)(2,1)} async-done(((bf16[256,1024]{1,0:T(8,128)(2,1)}), bf16[256,1024]{1,0:T(8,128)(2,1)}) %all-reduce.20.cloned.1.call-update) | async-done | bytes 524304 | tf_op jit(solution)/shard_map/psum | solution.py:676
  316.8 22.1 %all-reduce.22.cloned.1.call-done = bf16[256,1024]{1,0:T(8,128)(2,1)} async-done(((bf16[256,1024]{1,0:T(8,128)(2,1)}), bf16[256,1024]{1,0:T(8,128)(2,1)}) %all-reduce.22.cloned.1.call-update) | async-done | bytes 524304 | tf_op jit(solution)/shard_map/psum | solution.py:646
  343.1 8.2 shard_map.292
  352.2 19.8 %all-gather.1 = bf16[3072,128]{1,0:T(8,128)(2,1)S(1)} all-gather(bf16[768,128]{1,0:T(8,128)(2,1)S(1)} %convert_element_type.237), channel_id=3, replica_groups=mesh['dp'=4,'seq'=4,'head'=2] {'seq'}, dimensions={0}, use_global_device_ids=true | all-gather | bytes 983040 | tf_op jit(solution)/shard_map/all_gather | solution.py:351
  373.2 12.1 %shard_map.293 = (bf16[256,768]{1,0:T(8,128)(2,1)}, f32[264,1024]{1,0:T(8,128)}, bf16[256,128]{1,0:T(8,128)(2,1)}, f32[8,1024]{1,0:T(8,128)}, f32[8,128]{1,0:T(8,128)}) custom-call(bf16[272,1024]{1,0:T(8,128)(2,1)} %pad_maximum_fusion.2.ext_ref, f32[256,1024]{1,0:T(8,128)} %get-tuple-element.72.pre_ref, f32[256,128]{1,0:T(8,128)} %get-tuple-element.73.dt_ref, ...), custom_call_target="tpu_custom_call" | custom-call | tf_op jit(solution)/shard_map/pallas_call | solution.py:660
  398.7 9.3 %reduce-scatter.11.cloned.1.call-done.refs_4_ = bf16[256,128]{1,0:T(8,128)(2,1)} async-done(((bf16[1024,128]{1,0:T(8,128)(2,1)}), bf16[256,128]{1,0:T(8,128)(2,1)}) %reduce-scatter.11.cloned.1.call-update) | async-done | bytes 65552 | tf_op jit(solution)/shard_map/reduce_scatter | solution.py:659
  409.3 3.9 fusion.40
  418.7 8.1 shard_map.297
  428.6 8.2 shard_map.295
  439.0 8.0 shard_map.296
  448.9 8.1 shard_map.294
  464.8 66.0 %all-reduce.12 = f32[16,712]{0,1:T(8,128)S(1)} all-reduce(f32[16,712]{0,1:T(8,128)S(1)} %concatenate.53), channel_id=6, replica_groups=mesh['dp'=4,'seq'=4,'head'=2] {'dp','seq'}, use_global_device_ids=true, to_apply=%region_22.23.clone | all-reduce | flops 11392 | bytes 91136
  535.3 9.8 %reduce-scatter.17.cloned.1.call-done = f32[8,2304]{1,0:T(8,128)} async-done(((f32[256,2304]{1,0:T(8,128)}), f32[8,2304]{1,0:T(8,128)}) %reduce-scatter.17.cloned.1.call-update) | async-done | bytes 73744 | tf_op jit(solution)/shard_map/reduce_scatter | solution.py:746
  547.9 85.9 %reduce-scatter.21.cloned.1.call-done = bf16[64,3072]{1,0:T(8,128)(2,1)} async-done(((bf16[1024,3072]{1,0:T(8,128)(2,1)}), bf16[64,3072]{1,0:T(8,128)(2,1)}) %reduce-scatter.21.cloned.1.call-update) | async-done | bytes 393232 | tf_op jit(solution)/shard_map/reduce_scatter | solution.py:648
  635.9 86.4 %reduce-scatter.15.cloned.1.call-done = bf16[64,3072]{1,0:T(8,128)(2,1)} async-done(((bf16[1024,3072]{1,0:T(8,128)(2,1)}), bf16[64,3072]{1,0:T(8,128)(2,1)}) %reduce-scatter.15.cloned.1.call-update) | async-done | bytes 393232 | tf_op jit(solution)/shard_map/reduce_scatter | solution.py:678
  726.6 84.6 %reduce-scatter.19.cloned.1.call-done = bf16[64,3072]{1,0:T(8,128)(2,1)} async-done(((bf16[1024,3072]{1,0:T(8,128)(2,1)}), bf16[64,3072]{1,0:T(8,128)(2,1)}) %reduce-scatter.19.cloned.1.call-update) | async-done | bytes 393232 | tf_op jit(solution)/shard_map/reduce_scatter | solution.py:648
  815.7 83.9 %reduce-scatter.13.cloned.1.call-done = bf16[64,3072]{1,0:T(8,128)(2,1)} async-done(((bf16[1024,3072]{1,0:T(8,128)(2,1)}), bf16[64,3072]{1,0:T(8,128)(2,1)}) %reduce-scatter.13.cloned.1.call-update) | async-done | bytes 393232 | tf_op jit(solution)/shard_map/reduce_scatter | solution.py:678
  (356 shorter events, 144.1 us)
Async XLA Ops:
  7.2 188.4 %all-reduce.18.cloned.1.call-start = ((), (), s32[]{:S(2)}) async-start(), calls=%async_computation.7 | async-start | bytes 1048576 | tf_op jit(solution)/shard_map/psum | solution.py:646
  104.0 49.4 %copy-start.17 = (bf16[2,1024,1024]{2,1,0:T(8,128)(2,1)S(1)}, bf16[2,1024,1024]{2,1,0:T(8,128)(2,1)}, u32[]{:S(2)}) copy-start(bf16[2,1024,1024]{2,1,0:T(8,128)(2,1)} %param.32) | copy-start | bytes 12582916
  104.0 49.4 %copy-start.27 = (bf16[256,1024]{1,0:T(8,128)(2,1)S(1)}, bf16[256,1024]{1,0:T(8,128)(2,1)}, u32[]{:S(2)}) copy-start(bf16[256,1024]{1,0:T(8,128)(2,1)} %refs_0_) | copy-start | bytes 1572868
  158.9 23.2 %copy-start.7 = (f32[256,1024]{1,0:T(8,128)S(1)}, f32[256,1024]{1,0:T(8,128)}, u32[]{:S(2)}) copy-start(f32[256,1024]{1,0:T(8,128)} %get-tuple-element.95) | copy-start | bytes 3145732
  158.9 109.6 %reduce-scatter.9.cloned.1.call-start = ((), (), s32[]{:S(2)}) async-start(), calls=%async_computation.8 | async-start | bytes 327680 | tf_op jit(solution)/shard_map/reduce_scatter | solution.py:659
  160.2 22.1 %copy-start.57 = (f32[256]{0:T(256)}, f32[256]{0:T(256)S(1)}, u32[]{:S(2)}) copy-start(f32[256]{0:T(256)S(1)} %fusion.80) | copy-start | bytes 3076
  162.4 33.3 %copy-start.53 = (f32[1,1024]{1,0:T(1,128)S(1)}, f32[1,1024]{1,0:T(1,128)}, u32[]{:S(2)}) copy-start(f32[1,1024]{1,0:T(1,128)} %get-tuple-element.242.gain_ff_ref) | copy-start | bytes 12292
  162.8 36.8 %copy-start.36 = (f32[128,256]{0,1:T(8,128)}, f32[128,256]{0,1:T(8,128)S(1)}, u32[]{:S(2)}) copy-start(f32[128,256]{0,1:T(8,128)S(1)} %get-tuple-element.269) | copy-start | bytes 393220
  162.8 36.8 %copy-start.37 = (f32[128,256]{0,1:T(8,128)}, f32[128,256]{0,1:T(8,128)S(1)}, u32[]{:S(2)}) copy-start(f32[128,256]{0,1:T(8,128)S(1)} %get-tuple-element.270) | copy-start | bytes 393220
  182.3 91.5 %copy-start.59 = (f32[256]{0:T(256)}, f32[256]{0:T(256)S(1)}, u32[]{:S(2)}) copy-start(f32[256]{0:T(256)S(1)} %multiply_reduce_fusion) | copy-start | bytes 3076
  245.9 6.1 collective-permute-start
  248.6 52.2 %all-reduce.20.cloned.1.call-start = ((), (), s32[]{:S(2)}) async-start(), calls=%async_computation.9 | async-start | bytes 1048576 | tf_op jit(solution)/shard_map/psum | solution.py:676
  269.8 30.9 %copy-start.50 = (f32[1,1024]{1,0:T(1,128)S(1)}, f32[1,1024]{1,0:T(1,128)}, u32[]{:S(2)}) copy-start(f32[1,1024]{1,0:T(1,128)} %get-tuple-element.278.gain_mix_ref) | copy-start | bytes 12292
  269.9 32.6 %copy-start.58 = (f32[256]{0:T(256)S(1)}, f32[256]{0:T(256)}, u32[]{:S(2)}) copy-start(f32[256]{0:T(256)} %copy-done.57) | copy-start | bytes 3076
  273.7 28.7 %copy-start.10 = (f32[256,1024]{1,0:T(8,128)S(1)}, f32[256,1024]{1,0:T(8,128)}, u32[]{:S(2)}) copy-start(f32[256,1024]{1,0:T(8,128)} %get-tuple-element.211) | copy-start | bytes 3145732
  273.7 65.1 %all-reduce.22.cloned.1.call-start = ((), (), s32[]{:S(2)}) async-start(), calls=%async_computation.10 | async-start | bytes 1048576 | tf_op jit(solution)/shard_map/psum | solution.py:646
  310.1 28.8 %copy-start.8 = (f32[256,1024]{1,0:T(8,128)S(1)}, f32[256,1024]{1,0:T(8,128)}, u32[]{:S(2)}) copy-start(f32[256,1024]{1,0:T(8,128)} %get-tuple-element.95) | copy-start | bytes 3145732
  310.1 28.8 %copy-start.52 = (f32[1,1024]{1,0:T(1,128)S(1)}, f32[1,1024]{1,0:T(1,128)}, u32[]{:S(2)}) copy-start(f32[1,1024]{1,0:T(1,128)} %get-tuple-element.243.gain_ff_ref) | copy-start | bytes 12292
  310.1 30.1 %copy-start.60 = (f32[256]{0:T(256)S(1)}, f32[256]{0:T(256)}, u32[]{:S(2)}) copy-start(f32[256]{0:T(256)} %copy-done.59) | copy-start | bytes 3076
  310.1 30.1 %copy-start.6 = (bf16[256,1024]{1,0:T(8,128)(2,1)S(1)}, bf16[256,1024]{1,0:T(8,128)(2,1)}, u32[]{:S(2)}) copy-start(bf16[256,1024]{1,0:T(8,128)(2,1)} %get-tuple-element.68.h_ref) | copy-start | bytes 1572868
  310.1 30.1 %copy-start.12 = (bf16[256,1024]{1,0:T(8,128)(2,1)S(1)}, bf16[256,1024]{1,0:T(8,128)(2,1)}, u32[]{:S(2)}) copy-start(bf16[256,1024]{1,0:T(8,128)(2,1)} %all-reduce.20.cloned.1.call-done) | copy-start | bytes 1572868
  310.2 97.9 %reduce-scatter.11.cloned.1.call-start = ((), (), s32[]{:S(2)}) async-start(), calls=%async_computation.11 | async-start | bytes 327680 | tf_op jit(solution)/shard_map/reduce_scatter | solution.py:659
  386.7 7.5 collective-permute-start.1
  388.0 74.1 %all-reduce.24.cloned.1.call-start = ((), (), s32[]{:S(2)}) async-start(), calls=%async_computation.12 | async-start | bytes 1048576 | tf_op jit(solution)/shard_map/psum | solution.py:676
  413.2 131.9 %reduce-scatter.17.cloned.1.call-start = ((), (), s32[]{:S(2)}) async-start(), calls=%async_computation.15 | async-start | bytes 2433024 | tf_op jit(solution)/shard_map/reduce_scatter | solution.py:746
  416.4 217.4 %reduce-scatter.21.cloned.1.call-start = ((), (), s32[]{:S(2)}) async-start(), calls=%async_computation.17 | async-start | bytes 6684672 | tf_op jit(solution)/shard_map/reduce_scatter | solution.py:648
  426.8 295.5 %reduce-scatter.15.cloned.1.call-start = ((), (), s32[]{:S(2)}) async-start(), calls=%async_computation.14 | async-start | bytes 6684672 | tf_op jit(solution)/shard_map/reduce_scatter | solution.py:678
  436.8 374.4 %reduce-scatter.19.cloned.1.call-start = ((), (), s32[]{:S(2)}) async-start(), calls=%async_computation.16 | async-start | bytes 6684672 | tf_op jit(solution)/shard_map/reduce_scatter | solution.py:648
  447.1 452.5 %reduce-scatter.13.cloned.1.call-start = ((), (), s32[]{:S(2)}) async-start(), calls=%async_computation.13 | async-start | bytes 6684672 | tf_op jit(solution)/shard_map/reduce_scatter | solution.py:678
  459.6 74.5 %copy-start.22 = (f32[256,1024]{1,0:T(8,128)S(1)}, f32[256,1024]{1,0:T(8,128)}, u32[]{:S(2)}) copy-start(f32[256,1024]{1,0:T(8,128)} %get-tuple-element.209) | copy-start | bytes 3145732
  462.1 71.9 %copy-start.30 = (bf16[256,1024]{1,0:T(8,128)(2,1)S(1)}, bf16[256,1024]{1,0:T(8,128)(2,1)}, u32[]{:S(2)}) copy-start(bf16[256,1024]{1,0:T(8,128)(2,1)} %all-reduce.24.cloned.1.call-done) | copy-start | bytes 1572868
  814.1 94.5 %copy-start.35 = (bf16[256,1024]{1,0:T(8,128)(2,1)S(1)}, bf16[256,1024]{1,0:T(8,128)(2,1)}, u32[]{:S(2)}) copy-start(bf16[256,1024]{1,0:T(8,128)(2,1)} %get-tuple-element.295) | copy-start | bytes 1572868
  (49 other events, 193.9 us)
Sparse Core Ops, SparseCore 0:
  159.0 36.5 all-reduce.17
  248.7 19.8 reduce-scatter.8
  273.9 26.8 all-reduce.19
  310.2 28.5 all-reduce.21
  388.1 19.8 reduce-scatter.10
  413.4 26.7 all-reduce.23
  445.5 99.5 reduce-scatter.16
  549.5 84.2 reduce-scatter.20
  637.8 84.4 reduce-scatter.14
  726.6 84.4 reduce-scatter.18
  815.1 84.4 reduce-scatter.12

commit v3 on v2

v3 whole, which is shorter than its diff:
```python
import functools

import jax
import jax.numpy as jnp
from jax import lax
from jax.experimental import pallas as pl
from jax.experimental.pallas import tpu as pltpu
from jax.sharding import PartitionSpec as P

NS = 128
HD = 64
RIM = 16

highest = lax.Precision.HIGHEST
norm_eps = 1e-05
masked_score = -1e30
bf16 = jnp.bfloat16
f32 = jnp.float32
VMEM_LIMIT = 61 * 1024 * 1024


def nn(left, right):
    return jnp.dot(left, right, preferred_element_type=f32)


def tn(left, right):
    return lax.dot_general(left, right, (((0,), (0,)), ((), ())), preferred_element_type=f32)


def nt(left, right):
    return lax.dot_general(left, right, (((1,), (1,)), ((), ())), preferred_element_type=f32)


def exact(left, right, contract=(1, 0)):
    return lax.dot_general(
        left,
        right,
        (((contract[0],), (contract[1],)), ((), ())),
        precision=highest,
        preferred_element_type=f32,
    )


def sigmoid(v):
    return 1.0 / (1.0 + jnp.exp(-v))


def softplus(v):
    return jnp.maximum(v, 0.0) + jnp.log(1.0 + jnp.exp(-jnp.abs(v)))


def head_map(heads, width):
    rows = lax.broadcasted_iota(jnp.int32, (128, heads * width), 0)
    columns = lax.broadcasted_iota(jnp.int32, (128, heads * width), 1)
    return (columns // width == rows).astype(f32)


def rms_scaled(hidden, gain):
    return hidden * lax.rsqrt(jnp.mean(hidden * hidden, axis=-1, keepdims=True) + norm_eps) * gain


def ssm_scalars(dt_ref, heads_ref):
    rows = dt_ref.shape[0]
    raw = dt_ref[...] + heads_ref[0:1, :]
    step = softplus(raw)
    log_decay = -jnp.exp(heads_ref[1:2, :]) * step
    place_t = lax.broadcasted_iota(jnp.int32, (rows, rows), 0)
    place_s = lax.broadcasted_iota(jnp.int32, (rows, rows), 1)
    lower = (place_s <= place_t).astype(f32)
    running = exact(lower, log_decay)
    running_t = jnp.transpose(running)
    return raw, step, log_decay, running, running_t, place_t >= place_s


def spread(scalars, mapping):
    return exact(scalars, mapping)


def score_mask(dcol_ref, drow_ref):
    rows, length = dcol_ref.shape[0], drow_ref.shape[1]
    query_pos = lax.broadcasted_iota(jnp.int32, (rows, length), 0) + lax.axis_index("seq") * rows
    key_pos = lax.broadcasted_iota(jnp.int32, (rows, length), 1)
    return (key_pos <= query_pos) & (dcol_ref[:, 0:1] == drow_ref[0:1, :])


MESH_ID = pl.DeviceIdType.MESH
CHUNK = 128


def remote(src, dst, send, recv, axis, target):
    return pltpu.make_async_remote_copy(
        src_ref=src, dst_ref=dst, send_sem=send, recv_sem=recv,
        device_id={axis: target}, device_id_type=MESH_ID,
    )


def meet(count, later_sends):
    place = lax.axis_index("seq")
    barrier = pltpu.get_barrier_semaphore()
    for j in range(1, count):
        here = place - j if not later_sends else place + j

        @pl.when((here >= 0) & (here < count))
        def _():
            pl.semaphore_signal(barrier, inc=1, device_id={"seq": here}, device_id_type=MESH_ID)
    heads_axis = lax.axis_size("head")
    partner = lax.rem(lax.axis_index("head") + 1, heads_axis)
    pl.semaphore_signal(barrier, inc=1, device_id={"head": partner}, device_id_type=MESH_ID)
    waits = (place if later_sends else count - 1 - place) + 1
    pl.semaphore_wait(barrier, waits)
    return partner


def layer_forward_kernel(heads, layer, h_ref, gain_mix_ref, gain_ff_ref, wdt_ref,
                         taps_ref, heads_ref, dcol_ref, dloc_ref, drow_ref,
                         wkv_hbm, wbc_hbm, wx_hbm, wz_hbm, wq_hbm, wout_hbm, wo_hbm, wg_hbm, wu_hbm, wdown_hbm,
                         h_out, normed_ref, gate_ref, stack_ref, rim_ref, pre_ref, dt_ref, q_ref, kvall_ref,
                         att_ref, lse_ref, mem_ref, gated_ref, middle_ref, nff_ref, gu_ref, inner_ref,
                         ext, y, wkv_ref, wbc_ref, wzx_ref, wq_ref, wo_ref, wout_ref, wgu_ref, wdown_ref, rim_in, kv_in, chain_in, chain_out,
                         part_out, part_in, down_out, down_in,
                         load_sem, kv_send, kv_recv, rim_send, rim_recv, chain_send, chain_recv,
                         part_send, part_recv, down_send, down_recv):
    rows = dt_ref.shape[0]
    d_local = gate_ref.shape[1]
    ff_local = inner_ref.shape[1]
    count = lax.axis_size("seq")
    place = lax.axis_index("seq")
    loads = {}
    for name, src, dst in (
        ("kv", wkv_hbm, wkv_ref), ("bc", wbc_hbm, wbc_ref), ("x", wx_hbm, wzx_ref.at[:, pl.ds(d_local, d_local)]),
        ("z", wz_hbm, wzx_ref.at[:, pl.ds(0, d_local)]), ("q", wq_hbm, wq_ref), ("out", wout_hbm, wout_ref),
        ("o", wo_hbm, wo_ref), ("g", wg_hbm, wgu_ref.at[:, pl.ds(0, ff_local)]),
        ("u", wu_hbm, wgu_ref.at[:, pl.ds(ff_local, ff_local)]), ("down", wdown_hbm, wdown_ref),
    ):
        loads[name] = pltpu.make_async_copy(src.at[layer], dst, load_sem.at[len(loads)])
    for load in loads.values():
        load.start()
    partner = meet(count, False)

    normed_ref[...] = rms_scaled(h_ref[...].astype(f32), gain_mix_ref[...]).astype(bf16)
    normed = normed_ref[...]
    own = pl.ds(pl.multiple_of(place * rows, rows), rows)
    for j in range(count):
        @pl.when(j > place)
        def _():
            kv_in[j * rows:(j + 1) * rows, :] = jnp.zeros((rows, 2 * HD), bf16)
    loads["kv"].wait()
    kv_in[own, :] = nn(normed, wkv_ref[...]).astype(bf16)
    kv_copies = [
        remote(kv_in.at[own], kv_in.at[own], kv_send.at[j - 1], kv_recv.at[j - 1], "seq", place + j)
        for j in range(1, count)
    ]
    for j in range(1, count):
        @pl.when(place + j < count)
        def _():
            kv_copies[j - 1].start()
    loads["bc"].wait()
    stack_ref[:, d_local:] = nn(normed, wbc_ref[...]).astype(bf16)
    loads["x"].wait()
    stack_ref[:, :d_local] = nn(normed, wzx_ref[:, d_local:]).astype(bf16)
    rim_copy = remote(stack_ref.at[pl.ds(rows - RIM, RIM)], rim_in, rim_send, rim_recv, "seq", place + 1)

    @pl.when(place + 1 < count)
    def _():
        rim_copy.start()

    @pl.when(place == 0)
    def _():
        rim_in[...] = jnp.zeros(rim_in.shape, bf16)
        chain_in[...] = jnp.zeros(chain_in.shape, bf16)
    dt_ref[...] = nn(normed, wdt_ref[...]).astype(bf16).astype(f32)
    loads["z"].wait()
    gate_ref[...] = nn(normed, wzx_ref[:, :d_local]).astype(bf16)
    loads["q"].wait()
    q_ref[...] = nn(normed, wq_ref[...]).astype(bf16)
    raw, step, log_decay, running, running_t, ordered = ssm_scalars(dt_ref, heads_ref)
    mapping = head_map(heads, d_local // heads)
    last = running[rows - 1:rows, :]
    fade = jnp.exp(last - running) * dcol_ref[:, 5:6]
    dec = jnp.exp(running) * dcol_ref[:, 4:5]
    ends = jnp.exp(running_t[:, rows - 1:rows]) * dcol_ref[rows - 1:rows, 4:5] + jnp.zeros((128, NS), f32)
    ends = exact(mapping, ends, (0, 0))
    steps = spread(step, mapping)
    ext[RIM:, :] = stack_ref[...].astype(f32)

    @pl.when(place > 0)
    def _():
        rim_copy.wait_recv()
    rim_ref[...] = rim_in[...]
    ext[0:RIM, :] = rim_in[...].astype(f32)
    pre = ext[RIM:RIM + rows, :] * taps_ref[0:1, :]
    for k in range(1, 4):
        pre = pre + ext[RIM - k:RIM - k + rows, :] * dcol_ref[:, k:k + 1] * taps_ref[k:k + 1, :]
    pre_ref[...] = pre
    mixed = pre_ref[...] * sigmoid(pre_ref[...])
    values = mixed[:, :d_local]
    b_rows = mixed[:, d_local:d_local + NS].astype(bf16)
    c_rows = mixed[:, d_local + NS:].astype(bf16)
    stepped = values * steps
    state = tn((stepped * spread(fade, mapping)).astype(bf16), b_rows)
    y[...] = values * spread(heads_ref[2:3, :] + jnp.zeros((8, 128), f32), mapping)[0:1, :]
    linked = ordered & (dcol_ref[:, 0:1] == dloc_ref[0:1, :])
    cb = jnp.where(linked, nt(c_rows, b_rows), 0.0)
    stepped = stepped.astype(bf16)
    lane = lax.broadcasted_iota(jnp.int32, (rows, 128), 1)

    for j in range(1, count):
        @pl.when(place - j >= 0)
        def _():
            kv_copies[j - 1].wait_recv()
    allowed = score_mask(dcol_ref, drow_ref)
    keyvals = kv_in[...]
    kvall_ref[...] = keyvals
    keys, vals = keyvals[:, :HD], keyvals[:, HD:]
    totals = jnp.zeros((rows, 128), f32)
    pairs = heads // 2
    query_heads = q_ref.shape[1] // HD
    chain_copies = []
    for pair in range(pairs):
        span = slice(pair * 128, pair * 128 + 128)
        copy = remote(chain_out.at[pl.ds(pair * 128, 128)], chain_in.at[pl.ds(pair * 128, 128)],
                      chain_send.at[pair], chain_recv.at[pair], "seq", place + 1)
        chain_copies.append(copy)

        @pl.when(place > 0)
        def _():
            copy.wait_recv()
        chain_out[span, :] = (ends[span] * chain_in[span, :].astype(f32) + state[span]).astype(bf16)

        @pl.when(place + 1 < count)
        def _():
            copy.start()
        sides = []
        for h in (2 * pair, 2 * pair + 1):
            gap = running[:, h:h + 1] - running_t[h:h + 1, :]
            mixing = (jnp.exp(jnp.minimum(gap, 0.0)) * cb).astype(bf16)
            sides.append(nn(mixing, stepped[:, span]))
        y[:, span] += jnp.where(lane < 64, sides[0], sides[1])
        for h in range(query_heads * pair // pairs, query_heads * (pair + 1) // pairs):
            query = q_ref[:, h * HD:(h + 1) * HD] * jnp.asarray(HD ** -0.5, bf16)
            scores = jnp.where(allowed, nt(query, keys), masked_score)
            peak = jnp.max(scores, axis=1, keepdims=True)
            expo = jnp.exp(scores - peak)
            total = jnp.sum(expo, axis=1, keepdims=True)
            probs = (expo * (1.0 / total)).astype(bf16)
            att_ref[:, h * HD:(h + 1) * HD] = nn(probs, vals).astype(bf16)
            totals = jnp.where(lane == h, peak + jnp.log(total), totals)
    lse_ref[...] = totals
    mem_ref[...] = chain_in[...]
    decs = spread(dec, mapping)
    carried = decs * nt(c_rows, mem_ref[...])
    gate = gate_ref[...].astype(f32)
    gated_ref[...] = ((y[...] + carried) * (gate * sigmoid(gate))).astype(bf16)
    loads["out"].wait()
    loads["o"].wait()
    chunks = [pl.ds(begin, CHUNK) for begin in range(0, rows, CHUNK)]
    part_copies, down_copies = [], []
    for i, chunk in enumerate(chunks):
        part_out[chunk, :] = (nn(gated_ref[chunk, :], wout_ref[...])
                              + nn(att_ref[chunk, :], wo_ref[...])).astype(bf16)
        copy = remote(part_out.at[chunk], part_in.at[chunk], part_send.at[i], part_recv.at[i], "head", partner)
        copy.start()
        part_copies.append(copy)
    loads["g"].wait()
    loads["u"].wait()
    loads["down"].wait()
    for i, chunk in enumerate(chunks):
        part_copies[i].wait_recv()
        middle_ref[chunk, :] = h_ref[chunk, :].astype(f32) + (
            part_out[chunk, :].astype(f32) + part_in[chunk, :].astype(f32))
        nff_ref[chunk, :] = rms_scaled(middle_ref[chunk, :], gain_ff_ref[...]).astype(bf16)
        gu_ref[chunk, :] = nn(nff_ref[chunk, :], wgu_ref[...]).astype(bf16)
        gate = gu_ref[chunk, :ff_local].astype(f32)
        inner_ref[chunk, :] = (gate * sigmoid(gate) * gu_ref[chunk, ff_local:].astype(f32)).astype(bf16)
        down_out[chunk, :] = nn(inner_ref[chunk, :], wdown_ref[...]).astype(bf16)
        copy = remote(down_out.at[chunk], down_in.at[chunk], down_send.at[i], down_recv.at[i], "head", partner)
        copy.start()
        down_copies.append(copy)
    for i, chunk in enumerate(chunks):
        down_copies[i].wait_recv()
        h_out[chunk, :] = (middle_ref[chunk, :] + (
            down_out[chunk, :].astype(f32) + down_in[chunk, :].astype(f32))).astype(bf16)
    for i in range(len(chunks)):
        part_copies[i].wait_send()
        down_copies[i].wait_send()

    @pl.when(place + 1 < count)
    def _():
        rim_copy.wait_send()
        for copy in chain_copies:
            copy.wait_send()
    for j in range(1, count):
        @pl.when(place + j < count)
        def _():
            kv_copies[j - 1].wait_send()


VM = pl.BlockSpec(memory_space=pltpu.VMEM)
ANY = pl.BlockSpec(memory_space=pl.ANY)
DMA = pltpu.SemaphoreType.DMA


def layer_forward(layer, hidden, w, context):
    dcol, dloc, drow = context
    rows, model_width = hidden.shape
    heads = w["heads"]
    d_local = w["out"].shape[1]
    ff_local = w["down"].shape[1]
    q_width = w["q"].shape[2]
    width = d_local + 2 * NS
    count = lax.axis_size("seq")
    length = count * rows
    parts = rows // CHUNK
    outs = [
        ((rows, model_width), bf16), ((rows, model_width), bf16), ((rows, d_local), bf16), ((rows, width), bf16),
        ((RIM, width), bf16), ((rows, width), f32), ((rows, 128), f32), ((rows, q_width), bf16),
        ((length, 2 * HD), bf16), ((rows, q_width), bf16), ((rows, 128), f32), ((d_local, NS), bf16),
        ((rows, d_local), bf16), ((rows, model_width), f32), ((rows, model_width), bf16),
        ((rows, 2 * ff_local), bf16), ((rows, ff_local), bf16),
    ]
    full = (rows, model_width)
    result = pl.pallas_call(
        functools.partial(layer_forward_kernel, heads, layer),
        out_shape=[jax.ShapeDtypeStruct(shape, kind) for shape, kind in outs],
        in_specs=[VM] * 9 + [ANY] * 10,
        out_specs=[VM] * len(outs),
        scratch_shapes=[
            pltpu.VMEM((rows + RIM, width), f32), pltpu.VMEM((rows, d_local), f32),
            pltpu.VMEM((model_width, 2 * HD), bf16), pltpu.VMEM((model_width, 2 * NS), bf16),
            pltpu.VMEM((model_width, 2 * d_local), bf16), pltpu.VMEM((model_width, q_width), bf16),
            pltpu.VMEM((q_width, model_width), bf16), pltpu.VMEM((d_local, model_width), bf16),
            pltpu.VMEM((model_width, 2 * ff_local), bf16), pltpu.VMEM((ff_local, model_width), bf16),
            pltpu.VMEM((RIM, width), bf16), pltpu.VMEM((length, 2 * HD), bf16),
            pltpu.VMEM((d_local, NS), bf16), pltpu.VMEM((d_local, NS), bf16),
            pltpu.VMEM(full, bf16), pltpu.VMEM(full, bf16), pltpu.VMEM(full, bf16), pltpu.VMEM(full, bf16),
            DMA((10,)), DMA((count - 1,)), DMA((count - 1,)), DMA, DMA, DMA((heads // 2,)), DMA((heads // 2,)),
            DMA((parts,)), DMA((parts,)), DMA((parts,)), DMA((parts,)),
        ],
        compiler_params=pltpu.CompilerParams(
            vmem_limit_bytes=VMEM_LIMIT, collective_id=layer, has_side_effects=True),
    )(hidden, w["gain_mix"][layer], w["gain_ff"][layer], w["dt"][layer], w["taps"][layer], w["head_vals"][layer],
      dcol, dloc, drow, w["kv"], w["bc"], w["x"], w["z"], w["q"], w["out"], w["o"], w["g"], w["u"], w["down"])
    names = ("out", "normed", "gate", "stack", "rim", "pre", "dt", "q", "kv", "att", "lse", "memory",
             "gated", "middle", "nff", "gu", "inner")
    saved = dict(zip(names, result))
    saved["hidden"] = hidden
    return saved.pop("out"), saved


def norm_back(hidden, gain, grad):
    inverse = lax.rsqrt(jnp.mean(hidden * hidden, axis=-1, keepdims=True) + norm_eps)
    scaled = grad * gain
    lean = jnp.mean(scaled * hidden, axis=-1, keepdims=True)
    grad_gain = jnp.sum(grad * hidden * inverse, axis=0, keepdims=True)
    return inverse * (scaled - hidden * (inverse * inverse * lean)), grad_gain


def store_blocks(compute, slots, out, sems):
    columns = out.shape[1]

    def copy(i, slot):
        rows = pl.ds(pl.multiple_of(i * 256, 256), 256)
        return pltpu.make_async_copy(slots.at[slot, :, pl.ds(0, columns)], out.at[rows], sems.at[slot])
    blocks = out.shape[0] // 256

    def one(i, carry):
        slot = lax.rem(i, 2)

        @pl.when(i >= 2)
        def _():
            copy(i - 2, slot).wait()
        compute(pl.ds(pl.multiple_of(i * 256, 256), 256), slot)
        copy(i, slot).start()
        return carry
    lax.fori_loop(0, blocks, one, 0)
    for i in range(max(0, blocks - 2), blocks):
        copy(i, i % 2).wait()


def layer_backward_kernel(heads, layer, grad_ref, h_ref, normed_ref, gate_ref, stack_ref, rim_ref, pre_ref, dt_ref,
                          q_ref, kv_ref, att_ref, lse_ref, mem_ref, gated_ref, middle_ref, nff_ref, gu_ref,
                          inner_ref, gain_mix_ref, gain_ff_ref, wdt_ref,
                          taps_ref, heads_ref, dcol_ref, dloc_ref, drow_ref,
                          wdown_hbm, wg_hbm, wu_hbm, wout_hbm, wo_hbm, wz_hbm, wx_hbm, wbc_hbm, wq_hbm, wkv_hbm,
                          g_out, gff_out, gmix_out, gbc_out, dtaps_ref, dheads_ref, gains_ref,
                          wdown_ref, wide_ref, wout_ref, wo_ref, wbc_ref, wq_ref, wkv_ref,
                          gff, dgu, one_out, one_in, two_out, two_in, gmid, branch, gg, datt, dy_s, dxs_s, u_s,
                          decay_s, probs_s, acc, dkv_out, dkv_in, chain_in, chain_out, rim_in,
                          ext, pad, dext, dgate, dstack, dq, dkv, draw_s,
                          load_sem, one_send, one_recv, two_send, two_recv, chain_send, chain_recv,
                          rim_send, rim_recv, kv_send, kv_recv, gblk, grad_sem):
    rows = dt_ref.shape[0]
    d_local = gate_ref.shape[1]
    ff_local = inner_ref.shape[1]
    q_width = q_ref.shape[1]
    model_width = h_ref.shape[1]
    width = pre_ref.shape[1]
    length = kv_ref.shape[0]
    count = lax.axis_size("seq")
    place = lax.axis_index("seq")
    wgu_ref = wide_ref.at[:, pl.ds(0, 2 * ff_local)]
    wzx_ref = wide_ref.at[:, pl.ds(0, 2 * d_local)]
    loads = {}
    for name, src, dst in (
        ("down", wdown_hbm, wdown_ref), ("g", wg_hbm, wide_ref.at[:, pl.ds(0, ff_local)]),
        ("u", wu_hbm, wide_ref.at[:, pl.ds(ff_local, ff_local)]), ("out", wout_hbm, wout_ref),
        ("o", wo_hbm, wo_ref), ("bc", wbc_hbm, wbc_ref), ("q", wq_hbm, wq_ref), ("kv", wkv_hbm, wkv_ref),
        ("z", wz_hbm, wide_ref.at[:, pl.ds(0, d_local)]), ("x", wx_hbm, wide_ref.at[:, pl.ds(d_local, d_local)]),
    ):
        loads[name] = pltpu.make_async_copy(src.at[layer], dst, load_sem.at[len(loads)])
    for name in ("down", "g", "u", "out", "o", "bc", "q", "kv"):
        loads[name].start()
    partner = meet(count, True)
    chunks = [pl.ds(begin, CHUNK) for begin in range(0, rows, CHUNK)]

    gff[...] = grad_ref[...].astype(bf16)
    loads["down"].wait()
    loads["g"].wait()
    loads["u"].wait()
    one_copies, two_copies = [], []
    for i, chunk in enumerate(chunks):
        grad_inner = nt(gff[chunk, :], wdown_ref[...])
        gate = gu_ref[chunk, :ff_local].astype(f32)
        up = gu_ref[chunk, ff_local:].astype(f32)
        sig = sigmoid(gate)
        dgu[chunk, :ff_local] = (grad_inner * up * (sig * (1.0 + gate * (1.0 - sig)))).astype(bf16)
        dgu[chunk, ff_local:] = (grad_inner * (gate * sig)).astype(bf16)
        one_out[chunk, :] = nt(dgu[chunk, :], wgu_ref[...]).astype(bf16)
        copy = remote(one_out.at[chunk], one_in.at[chunk], one_send.at[i], one_recv.at[i], "head", partner)
        copy.start()
        one_copies.append(copy)
    loads["z"].start()
    loads["x"].start()

    @pl.when(place == count - 1)
    def _():
        rim_in[...] = jnp.zeros(rim_in.shape, f32)
        chain_in[...] = jnp.zeros(chain_in.shape, bf16)
    for j in range(1, count):
        @pl.when(place + j >= count)
        def _():
            dkv_in[(j - 1) * rows:j * rows, :] = jnp.zeros((rows, 2 * HD), bf16)

    def ff_weights(block, slot):
        gblk[slot, :, :ff_local] = tn(gff[:, block], inner_ref[...]).astype(bf16)
        gblk[slot, :, ff_local:3 * ff_local] = tn(nff_ref[:, block], dgu[...]).astype(bf16)
    store_blocks(ff_weights, gblk, gff_out, grad_sem)

    raw, step, log_decay, running, running_t, ordered = ssm_scalars(dt_ref, heads_ref)
    mapping = head_map(heads, d_local // heads)
    last = running[rows - 1:rows, :]
    fade = spread(jnp.exp(last - running) * dcol_ref[:, 5:6], mapping)
    dec = jnp.exp(running) * dcol_ref[:, 4:5]
    decs = spread(dec, mapping)
    ends = jnp.exp(running_t[:, rows - 1:rows]) * dcol_ref[rows - 1:rows, 4:5] + jnp.zeros((128, NS), f32)
    ends = exact(mapping, ends, (0, 0))
    steps = spread(step, mapping)
    skip = spread(heads_ref[2:3, :] + jnp.zeros((8, 128), f32), mapping)[0:1, :]
    pre_v = pre_ref[:, :d_local]
    values = pre_v * sigmoid(pre_v)
    pre_n = pre_ref[:, d_local:]
    maps = (pre_n * sigmoid(pre_n)).astype(bf16)
    b_rows, c_rows = maps[:, :NS], maps[:, NS:]
    stepped = (values * steps).astype(bf16)
    linked = ordered & (dcol_ref[:, 0:1] == dloc_ref[0:1, :])
    cb = jnp.where(linked, nt(c_rows, b_rows), 0.0)
    lane = lax.broadcasted_iota(jnp.int32, (rows, 128), 1)
    pairs = heads // 2
    for pair in range(pairs):
        span = slice(pair * 128, pair * 128 + 128)
        sides = []
        for h in (2 * pair, 2 * pair + 1):
            at = slice(h * rows, (h + 1) * rows)
            gap = running[:, h:h + 1] - running_t[h:h + 1, :]
            decay = jnp.exp(jnp.minimum(gap, 0.0))
            decay_s[:, at] = decay.astype(bf16)
            mixing = (decay_s[:, at].astype(f32) * cb).astype(bf16)
            sides.append(nn(mixing, stepped[:, span]))
        u_s[:, span] = jnp.where(lane < 64, sides[0], sides[1])
    allowed = score_mask(dcol_ref, drow_ref)
    keyvals = kv_ref[...]
    keys, vals = keyvals[:, :HD], keyvals[:, HD:]
    scale = jnp.asarray(HD ** -0.5, bf16)
    query_heads = q_width // HD
    for h in range(query_heads):
        query = q_ref[:, h * HD:(h + 1) * HD] * scale
        scores = jnp.where(allowed, nt(query, keys), masked_score)
        probs_s[:, h * length:(h + 1) * length] = jnp.exp(scores - lse_ref[:, h:h + 1]).astype(bf16)
    ext[0:RIM, :] = rim_ref[...].astype(f32)
    ext[RIM:, :] = stack_ref[...].astype(f32)
    gate = gate_ref[...].astype(f32)
    gate_sig = sigmoid(gate)
    gate_act = gate * gate_sig
    loads["out"].wait()
    loads["o"].wait()
    gains_ref[...] = jnp.zeros(gains_ref.shape, f32)
    for i, chunk in enumerate(chunks):
        one_copies[i].wait_recv()
        grad = one_out[chunk, :].astype(f32) + one_in[chunk, :].astype(f32)
        moved, gain = norm_back(middle_ref[chunk, :], gain_ff_ref[...], grad)
        gains_ref[1:2, :] += gain
        gmid[chunk, :] = grad_ref[chunk, :] + moved
        branch[chunk, :] = gmid[chunk, :].astype(bf16)
        gg[chunk, :] = nt(branch[chunk, :], wout_ref[...])
        datt[chunk, :] = nt(branch[chunk, :], wo_ref[...]).astype(bf16)
    grad_ssm = gg[...] * gate_act
    dy_s[...] = grad_ssm.astype(bf16)
    push = tn((grad_ssm * decs).astype(bf16), c_rows)
    dcb = jnp.zeros((rows, rows), f32)
    chain_copies = []
    for pair in range(pairs):
        span = slice(pair * 128, pair * 128 + 128)
        copy = remote(chain_out.at[pl.ds(pair * 128, 128)], chain_in.at[pl.ds(pair * 128, 128)],
                      chain_send.at[pair], chain_recv.at[pair], "seq", place - 1)
        chain_copies.append(copy)

        @pl.when(place < count - 1)
        def _():
            copy.wait_recv()
        chain_out[span, :] = (ends[span] * chain_in[span, :].astype(f32) + push[span]).astype(bf16)

        @pl.when(place > 0)
        def _():
            copy.start()
        stepped_p = stepped[:, span]
        dy_p = dy_s[:, span]
        dxs = []
        for side, h in enumerate((2 * pair, 2 * pair + 1)):
            at = slice(h * rows, (h + 1) * rows)
            decay = decay_s[:, at].astype(f32)
            dxs.append(tn((decay * cb).astype(bf16), dy_p))
            half = jnp.where((lane < 64) == (side == 0), dy_p, jnp.zeros_like(dy_p))
            dcb = dcb + nt(half, stepped_p) * decay
        dxs_s[:, span] = jnp.where(lane < 64, dxs[0], dxs[1])
        for h in range(query_heads * pair // pairs, query_heads * (pair + 1) // pairs):
            part = slice(h * HD, (h + 1) * HD)
            query = q_ref[:, part] * scale
            grad = datt[:, part]
            delta = jnp.sum(grad.astype(f32) * att_ref[:, part].astype(f32), axis=1, keepdims=True)
            probs = probs_s[:, h * length:(h + 1) * length]
            grad_scores = (probs.astype(f32) * (nt(grad, vals) - delta)).astype(bf16)
            dq[:, part] = (nn(grad_scores, keys) * HD ** -0.5).astype(bf16)
            dk = tn(grad_scores, query)
            dv = tn(probs, grad)
            if h == 0:
                acc[:, :HD] = dk
                acc[:, HD:] = dv
            else:
                acc[:, :HD] += dk
                acc[:, HD:] += dv
    dkv_out[...] = acc[...].astype(bf16)
    kv_copies = []
    for j in range(1, count):
        target = jnp.maximum(place - j, 0)
        theirs = pl.ds(pl.multiple_of(target * rows, rows), rows)
        copy = remote(dkv_out.at[theirs], dkv_in.at[pl.ds((j - 1) * rows, rows)], kv_send.at[j - 1],
                      kv_recv.at[j - 1], "seq", place - j)
        kv_copies.append(copy)

        @pl.when(place >= j)
        def _():
            copy.start()
    memory = mem_ref[...]
    gmem = chain_in[...]
    carried = decs * nt(c_rows, memory)
    back = fade * nt(b_rows, gmem)
    dy_low = dy_s[...].astype(f32)
    stepped_f = stepped.astype(f32)
    dxs_all = dxs_s[...] + back
    dxs_s[...] = dxs_all
    dcb = jnp.where(linked, dcb, 0.0).astype(bf16)
    dc = nn(dcb, b_rows) + nn((dy_low * decs).astype(bf16), memory)
    db = tn(dcb, c_rows) + nn((stepped_f * fade).astype(bf16), gmem)
    dvalues = steps * dxs_all + skip * grad_ssm
    pad[0:8, :] = jnp.zeros((8, width), f32)
    pad[8 + rows:, :] = jnp.zeros((8, width), f32)
    sig = sigmoid(pre_v)
    pad[8:8 + rows, :d_local] = dvalues * (sig * (1.0 + pre_v * (1.0 - sig)))
    sig = sigmoid(pre_n)
    slope = sig * (1.0 + pre_n * (1.0 - sig))
    pad[8:8 + rows, d_local:d_local + NS] = db * slope[:, :NS]
    pad[8:8 + rows, d_local + NS:] = dc * slope[:, NS:]
    dpre = pad[8:8 + rows, :]
    dext[...] = pad[0:8 + rows, :] * taps_ref[0:1, :]
    dtaps_ref[...] = jnp.zeros((8, width), f32)
    dtaps_ref[0:1, :] = jnp.sum(dpre * ext[RIM:RIM + rows, :], axis=0, keepdims=True)
    for k in range(1, 4):
        masked = dpre * dcol_ref[:, k:k + 1]
        pad[8:8 + rows, :] = masked
        dtaps_ref[k:k + 1, :] = jnp.sum(masked * ext[RIM - k:RIM - k + rows, :], axis=0, keepdims=True)
        dext[...] += pad[k:k + 8 + rows, :] * taps_ref[k:k + 1, :]
    rim_copy = remote(dext.at[pl.ds(0, 8)], rim_in, rim_send, rim_recv, "seq", place - 1)

    @pl.when(place > 0)
    def _():
        rim_copy.start()
    scanned = u_s[...] + carried
    drun = exact(dy_low * scanned - stepped_f * dxs_all, mapping, (1, 1))
    ssm_out = scanned + skip * values
    dgate[...] = (gg[...] * ssm_out * (gate_sig * (1.0 + gate * (1.0 - gate_sig)))).astype(bf16)
    gstep = exact(values * dxs_all, mapping, (1, 1))
    ones = jnp.ones((8, 128), f32)
    moved = exact(ones, gmem.astype(f32) * memory.astype(f32), (1, 1))
    end = exact(jnp.sum(stepped_f * back, axis=0, keepdims=True) + jnp.zeros((8, 1), f32), mapping, (1, 1))
    end = end + exact(moved, mapping, (1, 1)) * dec[rows - 1:rows, :]
    upper = (lax.broadcasted_iota(jnp.int32, (rows, rows), 1)
             >= lax.broadcasted_iota(jnp.int32, (rows, rows), 0)).astype(f32)
    dlog = exact(upper, drun) + end[0:1, :]
    draw = (gstep - jnp.exp(heads_ref[1:2, :]) * dlog) * sigmoid(raw)
    draw_s[...] = draw.astype(bf16)
    dskip = exact(jnp.sum(grad_ssm * values, axis=0, keepdims=True) + jnp.zeros((8, 1), f32), mapping, (1, 1))
    dheads_ref[...] = jnp.zeros((8, 128), f32)
    dheads_ref[0:1, :] = jnp.sum(draw, axis=0, keepdims=True)
    dheads_ref[1:2, :] = jnp.sum(dlog * log_decay, axis=0, keepdims=True)
    dheads_ref[2:3, :] = dskip[0:1, :]
    for name in ("z", "x", "bc", "q", "kv"):
        loads[name].wait()

    for j in range(1, count):
        @pl.when(place + j < count)
        def _():
            kv_copies[j - 1].wait_recv()
    own = pl.ds(pl.multiple_of(place * rows, rows), rows)
    total = acc[own, :]
    for j in range(1, count):
        total = total + dkv_in[(j - 1) * rows:j * rows, :].astype(f32)
    dkv[...] = total.astype(bf16)

    for i, chunk in enumerate(chunks):
        if i == len(chunks) - 1:
            @pl.when(place < count - 1)
            def _():
                rim_copy.wait_recv()
            dext[rows:rows + 8, :] += rim_in[...]
        dstack[chunk, :] = dext[8 + i * CHUNK:8 + (i + 1) * CHUNK, :].astype(bf16)
        two_out[chunk, :] = (
            nt(dgate[chunk, :], wzx_ref[:, :d_local]) + nt(dstack[chunk, :d_local], wzx_ref[:, d_local:])
            + nt(dstack[chunk, d_local:], wbc_ref[...]) + nt(draw_s[chunk, :], wdt_ref[...])
            + nt(dq[chunk, :], wq_ref[...]) + nt(dkv[chunk, :], wkv_ref[...])
        ).astype(bf16)
        copy = remote(two_out.at[chunk], two_in.at[chunk], two_send.at[i], two_recv.at[i], "head", partner)
        copy.start()
        two_copies.append(copy)

    def mix_weights(block, slot):
        left = normed_ref[:, block]
        at = 0
        for right in (dgate[...], dstack[:, :d_local], dq[...], dkv[...], draw_s[...]):
            gblk[slot, :, at:at + right.shape[1]] = tn(left, right).astype(bf16)
            at += right.shape[1]
        left = branch[:, block]
        for right in (gated_ref[...], att_ref[...]):
            gblk[slot, :, at:at + right.shape[1]] = tn(left, right).astype(bf16)
            at += right.shape[1]
        gbc_out[:, block] = tn(dstack[:, d_local:], normed_ref[:, block]).astype(bf16)
    store_blocks(mix_weights, gblk, gmix_out, grad_sem)

    for i, chunk in enumerate(chunks):
        two_copies[i].wait_recv()
        grad = two_out[chunk, :].astype(f32) + two_in[chunk, :].astype(f32)
        moved, gain = norm_back(h_ref[chunk, :].astype(f32), gain_mix_ref[...], grad)
        gains_ref[0:1, :] += gain
        g_out[chunk, :] = gmid[chunk, :] + moved
    for i in range(len(chunks)):
        one_copies[i].wait_send()
        two_copies[i].wait_send()

    @pl.when(place > 0)
    def _():
        rim_copy.wait_send()
        for copy in chain_copies:
            copy.wait_send()
    for j in range(1, count):
        @pl.when(place >= j)
        def _():
            kv_copies[j - 1].wait_send()


def layer_backward(layer, grad, w, saved, context):
    dcol, dloc, drow = context
    rows, model_width = grad.shape
    heads = w["heads"]
    d_local = w["out"].shape[1]
    ff_local = w["down"].shape[1]
    q_width = w["q"].shape[2]
    width = d_local + 2 * NS
    count = lax.axis_size("seq")
    length = count * rows
    parts = rows // CHUNK
    mix_width = 3 * d_local + 2 * q_width + 256
    outs = [
        ((rows, model_width), f32), ((model_width, 3 * ff_local), bf16), ((model_width, mix_width), bf16),
        ((2 * NS, model_width), bf16), ((8, width), f32), ((8, 128), f32), ((8, model_width), f32),
    ]
    full = (rows, model_width)
    state = (d_local, NS)
    names = ("hidden", "normed", "gate", "stack", "rim", "pre", "dt", "q", "kv", "att", "lse", "memory",
             "gated", "middle", "nff", "gu", "inner")

    def vm(shape, kind):
        return pltpu.VMEM(shape, kind)
    return pl.pallas_call(
        functools.partial(layer_backward_kernel, heads, layer),
        out_shape=[jax.ShapeDtypeStruct(shape, kind) for shape, kind in outs],
        in_specs=[VM] * 26 + [ANY] * 10,
        out_specs=[VM, ANY, ANY] + [VM] * 4,
        scratch_shapes=[
            vm((ff_local, model_width), bf16), vm((model_width, 2 * max(d_local, ff_local)), bf16),
            vm((d_local, model_width), bf16), vm((q_width, model_width), bf16), vm((model_width, 2 * NS), bf16),
            vm((model_width, q_width), bf16), vm((model_width, 2 * HD), bf16),
            vm(full, bf16), vm((rows, 2 * ff_local), bf16), vm(full, bf16), vm(full, bf16), vm(full, bf16),
            vm(full, bf16), vm(full, f32), vm(full, bf16), vm((rows, d_local), f32), vm((rows, q_width), bf16),
            vm((rows, d_local), bf16), vm((rows, d_local), f32), vm((rows, d_local), f32),
            vm((rows, heads * rows), bf16),
            vm((rows, q_width // HD * length), bf16), vm((length, 2 * HD), f32), vm((length, 2 * HD), bf16),
            vm(((count - 1) * rows, 2 * HD), bf16), vm(state, bf16), vm(state, bf16), vm((8, width), f32),
            vm((rows + RIM, width), f32), vm((rows + 16, width), f32), vm((rows + 8, width), f32),
            vm((rows, d_local), bf16), vm((rows, width), bf16), vm((rows, q_width), bf16),
            vm((rows, 2 * HD), bf16), vm((rows, 128), bf16),
            DMA((10,)), DMA((parts,)), DMA((parts,)), DMA((parts,)), DMA((parts,)), DMA((heads // 2,)),
            DMA((heads // 2,)), DMA, DMA, DMA((count - 1,)), DMA((count - 1,)),
            vm((2, 256, max(3 * ff_local, mix_width)), bf16), DMA((2,)),
        ],
        compiler_params=pltpu.CompilerParams(
            vmem_limit_bytes=VMEM_LIMIT, collective_id=2 + layer, has_side_effects=True),
    )(grad, *[saved[name] for name in names], w["gain_mix"][layer], w["gain_ff"][layer], w["dt"][layer],
      w["taps"][layer], w["head_vals"][layer], dcol, dloc, drow, w["down"], w["g"], w["u"], w["out"], w["o"],
      w["z"], w["x"], w["bc"], w["q"], w["kv"])


def pack_small(dtaps, dheads, gains, heads, d_local):
    shards = lax.axis_size("dp") * lax.axis_size("seq")
    taps = dtaps[:4, :d_local].reshape(4, heads, shards, -1)
    return jnp.concatenate(
        [gains[0].reshape(shards, -1), gains[1].reshape(shards, -1),
         jnp.transpose(taps, (2, 0, 1, 3)).reshape(shards, -1),
         jnp.broadcast_to(dheads[:3, :heads].reshape(1, -1), (shards, 3 * heads))], axis=1
    )


UNITS = 4


def add_rows(out, terms):
    rows = out.shape[0]
    size = min(64, rows)

    def one(i, carry):
        part = pl.ds(pl.multiple_of(i * size, size), size)
        total = terms[0][part, :].astype(f32)
        for term in terms[1:]:
            total = total + term[part, :].astype(f32)
        out[part, :] = total.astype(out.dtype)
        return carry
    lax.fori_loop(0, rows // size, one, 0)


def reduce_kernel(arrays, *refs):
    grads = refs[:arrays]
    outs = refs[arrays:2 * arrays]
    (own, first, second, right_in, left_in, load_sem, first_send, first_recv, second_send, second_recv,
     line_send, right_recv, left_recv) = refs[2 * arrays:]
    others = grads[0].shape[0]
    span = grads[0].shape[2]
    count = lax.axis_size("seq")
    shard = span // count
    spot = lax.axis_index("dp")
    place = lax.axis_index("seq")
    core = lax.rem(spot, 2)
    group = spot // 2
    barrier = pltpu.get_barrier_semaphore()
    sibling = spot + 1 - 2 * core
    pl.semaphore_signal(barrier, inc=1, device_id={"dp": sibling}, device_id_type=MESH_ID)
    peers = [lax.rem(group + k, others) * 2 + core for k in range(1, others)]
    for peer in peers:
        pl.semaphore_signal(barrier, inc=1, device_id={"dp": peer}, device_id_type=MESH_ID)

    @pl.when(place > 0)
    def _():
        pl.semaphore_signal(barrier, inc=1, device_id={"seq": place - 1}, device_id_type=MESH_ID)

    @pl.when(place < count - 1)
    def _():
        pl.semaphore_signal(barrier, inc=1, device_id={"seq": place + 1}, device_id_type=MESH_ID)
    waits = others + 2 - (place == 0).astype(jnp.int32) - (place == count - 1).astype(jnp.int32)
    pl.semaphore_wait(barrier, waits)

    units = []
    for a in range(arrays):
        columns = grads[a].shape[3] // UNITS
        for u in range(UNITS):
            units.append((a, pl.ds(u * columns, columns)))
    loads, firsts, seconds = [], [], []
    for n, (a, columns) in enumerate(units):
        loads.append(pltpu.make_async_copy(grads[a].at[:, core, :, columns], own.at[n], load_sem.at[n]))
        firsts.append(remote(grads[a].at[:, 1 - core, :, columns], first.at[n], first_send.at[n],
                             first_recv.at[n], "dp", sibling))
        loads[n].start()
        firsts[n].start()
    for n in range(len(units)):
        loads[n].wait()
        firsts[n].wait_recv()
        copies = []
        for k, peer in enumerate(peers):
            theirs = lax.rem(group + k + 1, others)
            add_rows(own.at[n, theirs], [own.at[n, theirs], first.at[n, theirs]])
            copy = remote(own.at[n, theirs], second.at[n, k], second_send.at[n, k], second_recv.at[n, k], "dp", peer)
            copy.start()
            copies.append(copy)
        seconds.append(copies)
    lines = []
    for n, (a, columns) in enumerate(units):
        for copy in seconds[n]:
            copy.wait_recv()
        total = own.at[n, group]
        add_rows(total, [total, first.at[n, group]] + [second.at[n, k] for k in range(others - 1)])
        copies = []
        for j in range(count):
            rows = pl.ds(j * shard, shard)
            right = remote(total.at[rows], right_in.at[n, rows], line_send.at[n, j], right_recv.at[n, j],
                           "seq", place + 1)
            left = remote(total.at[rows], left_in.at[n, rows], line_send.at[n, j], left_recv.at[n, j],
                          "seq", place - 1)

            @pl.when(place < j)
            def _():
                @pl.when(place > 0)
                def _():
                    right.wait_recv()
                    add_rows(total.at[rows], [total.at[rows], right_in.at[n, rows]])
                right.start()

            @pl.when(place > j)
            def _():
                @pl.when(place < count - 1)
                def _():
                    left.wait_recv()
                    add_rows(total.at[rows], [total.at[rows], left_in.at[n, rows]])
                left.start()
            copies.append((right, left))
        lines.append(copies)
    for n, (a, columns) in enumerate(units):
        total = own.at[n, group]
        for j in range(count):
            right, left = lines[n][j]
            rows = pl.ds(j * shard, shard)

            @pl.when(place == j)
            def _():
                terms = [total.at[rows]]
                if j > 0:
                    right.wait_recv()
                    terms.append(right_in.at[n, rows])
                if j < count - 1:
                    left.wait_recv()
                    terms.append(left_in.at[n, rows])
                add_rows(outs[a].at[:, columns], terms)
    for n in range(len(units)):
        firsts[n].wait_send()
        for copy in seconds[n]:
            copy.wait_send()
        for j in range(count):
            right, left = lines[n][j]

            @pl.when(place < j)
            def _():
                right.wait_send()

            @pl.when(place > j)
            def _():
                left.wait_send()


def reduce_grads(arrays):
    count = lax.axis_size("seq")
    others = lax.axis_size("dp") // 2
    rows = arrays[0].shape[0]
    span = rows // (2 * others)
    shard = span // count
    columns = arrays[0].shape[1] // UNITS
    total = len(arrays) * UNITS
    views = [a.reshape(others, 2, span, a.shape[1]) for a in arrays]
    return pl.pallas_call(
        functools.partial(reduce_kernel, len(arrays)),
        out_shape=[jax.ShapeDtypeStruct((shard, a.shape[1]), f32) for a in arrays],
        in_specs=[ANY] * len(arrays),
        out_specs=[VM] * len(arrays),
        scratch_shapes=[
            pltpu.VMEM((total, others, span, columns), bf16), pltpu.VMEM((total, others, span, columns), bf16),
            pltpu.VMEM((total, others - 1, span, columns), bf16),
            pltpu.VMEM((total, span, columns), bf16), pltpu.VMEM((total, span, columns), bf16),
            DMA((total,)), DMA((total,)), DMA((total,)), DMA((total, others - 1)), DMA((total, others - 1)),
            DMA((total, count)), DMA((total, count)), DMA((total, count)),
        ],
        compiler_params=pltpu.CompilerParams(
            vmem_limit_bytes=VMEM_LIMIT, collective_id=9, has_side_effects=True),
        cost_estimate=pl.CostEstimate(flops=0, bytes_accessed=400 * 1024 * 1024, transcendentals=0),
    )(*views)


def on_device(hidden_in, segment_ids, gain_mix, w_zx, w_bc, w_dt, conv_x, conv_bc, ssm_head, w_q, w_kv,
              w_o, w_out, gain_ff, w_gu, w_down, cotangent):
    rows, model_width = hidden_in.shape
    taps_count = conv_x.shape[1]
    place = lax.axis_index("seq")
    offset = place * rows
    doc_all = segment_ids[0]
    padded = jnp.concatenate([jnp.full((taps_count - 1,), -1, jnp.int32), doc_all])
    doc_ext = lax.dynamic_slice_in_dim(padded, offset, rows + taps_count - 1)
    docs = doc_ext[taps_count - 1:]
    columns = [docs.astype(f32)]
    for k in range(1, taps_count):
        columns.append((doc_ext[taps_count - 1 - k:taps_count - 1 - k + rows] == docs).astype(f32))
    columns.append((docs == doc_ext[taps_count - 2]).astype(f32))
    columns.append((docs == docs[-1]).astype(f32))
    dcol = jnp.pad(jnp.stack(columns, axis=1), ((0, 0), (0, 128 - len(columns))))
    dloc = jnp.broadcast_to(docs.astype(f32)[None], (8, rows))
    drow = jnp.broadcast_to(doc_all.astype(f32)[None], (8, doc_all.shape[0]))
    context = (dcol, dloc, drow)
    layers = gain_mix.shape[0]
    heads = ssm_head.shape[2]
    d_local = w_zx.shape[3]
    w = dict(
        heads=heads,
        gain_mix=gain_mix[:, None].astype(f32),
        gain_ff=gain_ff[:, None].astype(f32),
        z=w_zx[:, :, 0, :],
        x=w_zx[:, :, 1, :],
        bc=w_bc,
        dt=jnp.pad(w_dt, ((0, 0), (0, 0), (0, 128 - heads))),
        q=w_q,
        kv=w_kv.reshape(layers, model_width, -1),
        o=w_o,
        out=w_out,
        g=w_gu[:, :, 0, :],
        u=w_gu[:, :, 1, :],
        down=w_down,
        taps=jnp.pad(jnp.concatenate([conv_x.reshape(layers, taps_count, -1), conv_bc], axis=2).astype(f32),
                     ((0, 0), (0, 8 - taps_count), (0, 0))),
        head_vals=jnp.pad(ssm_head, ((0, 0), (0, 5), (0, 128 - heads))),
    )
    hidden = hidden_in
    saved = []
    for l in range(layers):
        hidden, kept = layer_forward(l, hidden, w, context)
        saved.append(kept)
    block_out = hidden
    gradient = cotangent.astype(f32)
    wide, narrow, small = [], [None] * layers, [None] * layers
    for l in reversed(range(layers)):
        gradient, ff_grads, mix_grads, g_bc, dtaps, dheads, gains = layer_backward(
            l, gradient, w, saved[l], context)
        wide = [ff_grads, mix_grads] + wide
        narrow[l] = jnp.concatenate(
            [g_bc, jnp.pad(jnp.transpose(dtaps[:4, d_local:]), ((0, 0), (0, 124))).astype(bf16)], axis=1)
        small[l] = pack_small(dtaps, dheads, gains, heads, d_local)
    g_bc = lax.psum_scatter(jnp.concatenate(narrow, axis=1), ("dp", "seq", "head"),
                            scatter_dimension=0, tiled=True)
    small = jnp.concatenate(small, axis=1)
    shards, used = small.shape
    room = -(-used // 1024) * 1024
    small = jnp.pad(small, ((0, 0), (0, room - used))).reshape(shards * (room // 128), 128)
    small = lax.psum_scatter(small, ("dp", "seq"), scatter_dimension=0, tiled=True)
    small = small.reshape(-1)[:used]
    summed = reduce_grads(wide)
    parts = [(summed[2 * l], summed[2 * l + 1]) for l in range(layers)]
    ff_local = w_down.shape[1]
    q_width = w_q.shape[2]
    part = model_width // (lax.axis_size("dp") * lax.axis_size("seq"))

    def both(pieces):
        return jnp.stack(pieces, axis=0).astype(f32)

    def cut(index, begin, size):
        return [p[index][:, begin:begin + size] for p in parts]

    down = both([jnp.transpose(a) for a in cut(0, 0, ff_local)])
    gu = both(cut(0, ff_local, 2 * ff_local)).reshape(layers, part, 2, ff_local)
    at = 2 * d_local
    zx = both(cut(1, 0, at)).reshape(layers, part, 2, d_local)
    q = both(cut(1, at, q_width))
    at += q_width
    kv = both(cut(1, at, 128)).reshape(layers, part, 1, 128)
    at += 128
    dt = both(cut(1, at, heads))
    at += 128
    out = both([jnp.transpose(a) for a in cut(1, at, d_local)])
    at += d_local
    o = both([jnp.transpose(a) for a in cut(1, at, q_width)])
    g_bc = g_bc.astype(f32).reshape(g_bc.shape[0], layers, -1)
    w_bc_grad = jnp.transpose(g_bc[:, :, :model_width], (1, 2, 0))
    conv_bc_grad = jnp.transpose(g_bc[:, :, model_width:model_width + taps_count], (1, 2, 0))
    small = small.reshape(layers, -1)
    gain_a = small[:, :part]
    gain_b = small[:, part:2 * part]
    taps_end = 2 * part + taps_count * d_local // (model_width // part)
    conv_x_grad = small[:, 2 * part:taps_end].reshape(layers, taps_count, heads, -1)
    head_grad = small[:, taps_end:].reshape(layers, 3, heads)
    return (block_out, gradient, gain_a, zx, w_bc_grad, dt, conv_x_grad, conv_bc_grad, head_grad, q, kv,
            o, out, gain_b, gu, down)


def solution(mesh):
    in_specs = (
        P(("dp", "seq"), None),
        P("dp", None),
        P(),
        P(None, None, None, "head"),
        P(),
        P(None, None, "head"),
        P(None, None, "head", None),
        P(),
        P(None, None, "head"),
        P(None, None, "head"),
        P(None, None, "head", None),
        P(None, "head", None),
        P(None, "head", None),
        P(),
        P(None, None, None, "head"),
        P(None, "head", None),
        P(("dp", "seq"), None),
    )
    out_specs = (
        P(("dp", "seq"), None),
        P(("dp", "seq"), None),
        P(None, ("dp", "seq")),
        P(None, ("dp", "seq"), None, "head"),
        P(None, None, ("dp", "seq", "head")),
        P(None, ("dp", "seq"), "head"),
        P(None, None, "head", ("dp", "seq")),
        P(None, None, ("dp", "seq", "head")),
        P(None, None, "head"),
        P(None, ("dp", "seq"), "head"),
        P(None, ("dp", "seq"), "head", None),
        P(None, "head", ("dp", "seq")),
        P(None, "head", ("dp", "seq")),
        P(None, ("dp", "seq")),
        P(None, ("dp", "seq"), None, "head"),
        P(None, "head", ("dp", "seq")),
    )
    return jax.shard_map(
        on_device, mesh=mesh, in_specs=in_specs, out_specs=out_specs, check_vma=False
    )
```

time: 927 us -> 515 us (0.56)
  waiting for transfers between devices: 423 us -> 0.04 us
  Pallas kernels: 170 us -> 393 us
  blocking collectives: 133 us -> 0 us
  matrix products: 39.2 us -> 0 us
  other arithmetic: 46.5 us -> 12.8 us
    reduce_scatter x7 -> x1, waiting for transfers between devices: 373 us -> 0.01 us  [on_device(): lax.psum_scatter(jnp.concatenate(narrow, axis=1), ('dp', 'seq', 'head'),...]
    pallas_call x10 -> x5, Pallas kernels: 170 us -> 393 us  [the longest x1 180 us: reduce_grads(): pl.pallas_call(functools.partial(reduce_kernel, len(arrays)), out_shape=[...]
    all_gather x4 -> x0, blocking collectives: 66.7 us -> none  [the longest x2 39.8 us: pass_states(): states = lax.all_gather(state.astype(bf16), 'seq')]
    unnamed x1 -> x0, blocking collectives: 66 us -> none
    psum x4 -> x0, waiting for transfers between devices: 48.6 us -> none  [the longest x2 31.4 us: layer_backward(): lax.psum(nt(grad_gu, weights['gu']).astype(bf16), 'head').astype(f32)]
    dot_general x18 -> x0, matrix products: 39.2 us -> none  [the longest x16 35.3 us: nt(): lax.dot_general(left, right, (((1,), (1,)), ((), ())), preferred_element_...]
    convert_element_type x18 -> x1, other arithmetic: 22.1 us -> 1.08 us  [on_device(): gradient = cotangent.astype(f32)]
    unnamed x155 -> x32, local copies, waits for them, and re-layouts: 26.8 us -> 7.06 us
  transfers between devices with their start and end apart: 13 -> 2, of which waited for: 11 -> 0; matrix products, arithmetic and copies ran while one was open for 7% -> 5% of each run, Pallas kernels for 4% -> 36%
where the time goes in v3:
time: 515 us; the launch traced here: 506 us
  Pallas kernels  393 us (76%)
  local copies, waits for them, and re-layouts  83.4 us (16%)
  between operations  16.9 us (3%)
  other arithmetic  12.8 us (2%)
    pallas_call x1, Pallas kernels, reduce_grads(): pl.pallas_call(functools.partial(reduce_kernel, len(arrays)), out_shape=[...  180 us
    pallas_call x2, Pallas kernels, layer_backward(): pl.pallas_call(functools.partial(layer_backward_kernel, heads, layer), ou...  116 us
    pallas_call x2, Pallas kernels, layer_forward(): pl.pallas_call(functools.partial(layer_forward_kernel, heads, layer), out...  95.8 us
    slice x1, local copies, waits for them, and re-layouts, on_device(): w_gu[:, :, 1, :]  17.4 us
    slice x1, local copies, waits for them, and re-layouts, on_device(): w_zx[:, :, 0, :]  13.7 us
  transfers between devices with their start and end apart: 2, of which 0 were waited for; matrix products, arithmetic and copies ran while one was open for 5% of the time, Pallas kernels for 36%

profile of v3, /device:TPU:0, one launch (start us, length us, event | category | flops | bytes accessed | tf_op | source)
XLA Modules:
  0.0 505.9 jit_solution(4124255710922740952)
XLA Ops:
  8.1 0.8 pad_dynamic-slice_fusion
  10.2 1.1 copy.99
  11.3 0.9 fusion.7
  15.6 1.4 compare_convert_fusion
  17.2 13.7 %fusion.16 = (bf16[2,1024,1,768]{3,2,1,0:T(2,128)(2,1)}, bf16[2,1024,1,768]{3,2,1,0:T(2,128)(2,1)}) fusion(bf16[2,1024,2,768]{3,2,1,0:T(2,128)(2,1)} %param.20), kind=kLoop, calls=%fused_computation.65 | loop fusion | bytes 12582912 | tf_op jit(solution)/shard_map/slice | solution.py:927
  30.9 17.4 %fusion.15 = (bf16[2,1024,1,1024]{3,2,1,0:T(2,128)(2,1)S(1)}, bf16[2,1024,1,1024]{3,2,1,0:T(2,128)(2,1)}) fusion(bf16[2,1024,2,1024]{3,2,1,0:T(2,128)(2,1)} %param.31), kind=kLoop, calls=%fused_computation.64 | loop fusion | bytes 16777216 | tf_op jit(solution)/shard_map/slice | solution.py:936
  48.3 1.1 convert_element_type.45.grad_ref
  50.7 8.4 %copy_bitcast_fusion.2 = (bf16[2,1024,768]{2,1,0:T(8,128)(2,1)}, bf16[2,1024,768]{2,1,0:T(8,128)(2,1)}) fusion(bf16[2,1024,1,768]{3,2,1,0:T(2,128)(2,1)} %get-tuple-element.190, bf16[2,1024,1,768]{3,2,1,0:T(2,128)(2,1)} %get-tuple-element.191), kind=kLoop, calls=%fused_computation.4 | loop fusion | bytes 12582912 | tf_op jit(solution)/shard_map/squeeze | solution.py:927
  59.0 7.9 %copy_bitcast_fusion = (bf16[2,1024,1024]{2,1,0:T(8,128)(2,1)}, bf16[2,1024,1024]{2,1,0:T(8,128)(2,1)}) fusion(bf16[2,1024,1,1024]{3,2,1,0:T(2,128)(2,1)S(1)} %get-tuple-element.188, bf16[2,1024,1,1024]{3,2,1,0:T(2,128)(2,1)} %get-tuple-element.189), kind=kLoop, calls=%fused_computation | loop fusion | bytes 16777216 | tf_op jit(solution)/shard_map/squeeze | solution.py:936
  68.1 47.1 %shard_map.288 = (bf16[256,1024]{1,0:T(8,128)(2,1)}, bf16[256,1024]{1,0:T(8,128)(2,1)}, bf16[256,768]{1,0:T(8,128)(2,1)}, bf16[256,1024]{1,0:T(8,128)(2,1)}, bf1...) custom-call(bf16[256,1024]{1,0:T(8,128)(2,1)} %h_ref.3, ...), custom_call_target="tpu_custom_call" | custom-call | tf_op jit(solution)/shard_map/pallas_call | solution.py:322
  115.2 48.7 %shard_map.289 = (bf16[256,1024]{1,0:T(8,128)(2,1)}, bf16[256,1024]{1,0:T(8,128)(2,1)}, bf16[256,768]{1,0:T(8,128)(2,1)}, bf16[256,1024]{1,0:T(8,128)(2,1)}, bf1...) custom-call(bf16[256,1024]{1,0:T(8,128)(2,1)} %get-tuple-element.68., ...), custom_call_target="tpu_custom_call" | custom-call | tf_op jit(solution)/shard_map/pallas_call | solution.py:322
  163.9 62.8 %shard_map.290 = (f32[256,1024]{1,0:T(8,128)}, bf16[1024,3072]{1,0:T(8,128)(2,1)}, bf16[1024,3072]{1,0:T(8,128)(2,1)}, bf16[256,1024]{1,0:T(8,128)(2,1)}, f32[8,...) custom-call(f32[256,1024]{1,0:T(8,128)} %convert_element_type.45.grad_ref, ...), custom_call_target="tpu_custom_call" | custom-call | tf_op jit(solution)/shard_map/pallas_call | solution.py:702
  226.8 53.6 %shard_map.291 = (f32[256,1024]{1,0:T(8,128)}, bf16[1024,3072]{1,0:T(8,128)(2,1)}, bf16[1024,3072]{1,0:T(8,128)(2,1)}, bf16[256,1024]{1,0:T(8,128)(2,1)}, f32[8,...) custom-call(f32[256,1024]{1,0:T(8,128)} %get-tuple-element.86.grad_ref, bf16[256,1024]{1,0:T(8,128)(2,1)} %h_ref.3, ...), custom_call_target="tpu_custom_call" | custom-call | tf_op jit(solution)/shard_map/pallas_call | solution.py:702
  280.4 0.9 slice_reduce_fusion.2
  283.7 0.9 slice_reduce_fusion
  289.0 1.2 fusion.5
  290.2 180.4 %shard_map.292 = (f32[64,3072]{1,0:T(8,128)}, f32[64,3072]{1,0:T(8,128)}, f32[64,3072]{1,0:T(8,128)}, f32[64,3072]{1,0:T(8,128)}) custom-call(bf16[2,2,256,3072]{3,2,1,0:T(8,128)(2,1)} %bitcast.96, bf16[2,2,256,3072]{3,2,1,0:T(8,128)(2,1)} %bitcast.97, bf16[2,2,256,3072]{3,2,1,0:T(8,128)(2,1)} %bitcast.94, bf16[2,2,256,3072]{3,2,1,0:T(8,128)(2,1)} %bitcast.95), custom_call_target="tpu_custom_call" | custom-call | bytes 419430400 | tf_op jit(solution)/shard_map/pallas_call | solution.py:883
  470.6 0.8 slice_bitcast_fusion.13
  471.4 0.9 slice_bitcast_fusion.5
  473.1 0.9 slice_bitcast_fusion.6
  475.5 1.0 slice_bitcast_fusion.2
  479.3 1.0 slice.207
  480.3 1.0 slice.206
  484.1 0.9 slice_bitcast_fusion.3
  485.1 0.8 pad_maximum_fusion.3
  485.8 1.0 slice_bitcast_fusion
  486.9 0.8 pad_maximum_fusion.2
  487.7 1.2 pad_maximum_fusion.1
  489.0 1.5 pad_maximum_fusion
  493.5 0.8 convert.22
  496.2 0.8 copy.132
  497.0 1.0 copy.133
  (97 shorter events, 26.4 us)
Async XLA Ops:
  8.0 482.5 %all-reduce.11.cloned.1.call-start = ((), (), s32[]{:S(2)}) async-start(), calls=%async_computation.2 | async-start | bytes 131072
  30.9 17.4 %copy-start.3 = (bf16[256,1024]{1,0:T(8,128)(2,1)S(1)}, bf16[256,1024]{1,0:T(8,128)(2,1)}, u32[]{:S(2)}) copy-start(bf16[256,1024]{1,0:T(8,128)(2,1)} %param.33) | copy-start | bytes 1572868
  30.9 18.5 %copy-start.7 = (bf16[2,1024]{1,0:T(2,128)(2,1)S(1)}, bf16[2,1024]{1,0:T(2,128)(2,1)}, u32[]{:S(2)}) copy-start(bf16[2,1024]{1,0:T(2,128)(2,1)} %param.30) | copy-start | bytes 12292
  30.9 18.5 %copy-start.8 = (bf16[2,1024]{1,0:T(2,128)(2,1)S(1)}, bf16[2,1024]{1,0:T(2,128)(2,1)}, u32[]{:S(2)}) copy-start(bf16[2,1024]{1,0:T(2,128)(2,1)} %param.19) | copy-start | bytes 12292
  226.7 59.6 %copy-start.9 = (f32[8,128]{1,0:T(8,128)S(1)}, f32[8,128]{1,0:T(8,128)}, u32[]{:S(2)}) copy-start(f32[8,128]{1,0:T(8,128)} %get-tuple-element.109) | copy-start | bytes 12292
  280.3 8.6 %copy-start.5 = (bf16[256,1024]{1,0:T(8,128)(2,1)S(1)}, bf16[256,1024]{1,0:T(8,128)(2,1)}, u32[]{:S(2)}) copy-start(bf16[256,1024]{1,0:T(8,128)(2,1)} %get-tuple-element.117) | copy-start | bytes 1572868
  280.4 8.6 %copy-start.6 = (bf16[256,1024]{1,0:T(8,128)(2,1)S(1)}, bf16[256,1024]{1,0:T(8,128)(2,1)}, u32[]{:S(2)}) copy-start(bf16[256,1024]{1,0:T(8,128)(2,1)} %get-tuple-element.116) | copy-start | bytes 1572868
  287.2 206.3 %reduce-scatter.2.cloned.1.call-start = ((), (), s32[]{:S(2)}) async-start(), calls=%async_computation.1 | async-start | bytes 1216512 | tf_op jit(solution)/shard_map/reduce_scatter | solution.py:957
  470.6 11.3 %copy-start.2 = (f32[64,3072]{1,0:T(8,128)S(1)}, f32[64,3072]{1,0:T(8,128)}, u32[]{:S(2)}) copy-start(f32[64,3072]{1,0:T(8,128)} %get-tuple-element.119) | copy-start | bytes 2359300
  475.5 6.9 %copy-start.1 = (f32[64,3072]{1,0:T(8,128)S(1)}, f32[64,3072]{1,0:T(8,128)}, u32[]{:S(2)}) copy-start(f32[64,3072]{1,0:T(8,128)} %get-tuple-element.118) | copy-start | bytes 2359300
  480.3 2.6 copy-start.10
  485.8 10.4 %copy-start.4 = (bf16[256,1024]{1,0:T(8,128)(2,1)S(1)}, bf16[256,1024]{1,0:T(8,128)(2,1)}, u32[]{:S(2)}) copy-start(bf16[256,1024]{1,0:T(8,128)(2,1)} %get-tuple-element.237) | copy-start | bytes 1572868
  486.9 10.1 %copy-start = (f32[256,1024]{1,0:T(8,128)S(1)}, f32[256,1024]{1,0:T(8,128)}, u32[]{:S(2)}) copy-start(f32[256,1024]{1,0:T(8,128)} %get-tuple-element.238) | copy-start | bytes 3145732
Sparse Core Ops, SparseCore 0:
  287.3 84.4 all-reduce.10
Sparse Core Ops, SparseCore 1:
  293.6 97.2 reduce-scatter.1

commit v4 on v3

--- a/solution.py
+++ b/solution.py
@@ -16,7 +16,7 @@
 masked_score = -1e30
 bf16 = jnp.bfloat16
 f32 = jnp.float32
-VMEM_LIMIT = 61 * 1024 * 1024
+VMEM_LIMIT = 63 * 1024 * 1024
 
 
 def nn(left, right):
@@ -94,10 +94,10 @@
     )
 
 
-def meet(count, later_sends):
+def meet(count, later_sends, extra=None):
     place = lax.axis_index("seq")
     barrier = pltpu.get_barrier_semaphore()
-    for j in range(1, count):
+    for j in range(1, count if extra is None else 1):
         here = place - j if not later_sends else place + j
 
         @pl.when((here >= 0) & (here < count))
@@ -107,34 +107,311 @@
     partner = lax.rem(lax.axis_index("head") + 1, heads_axis)
     pl.semaphore_signal(barrier, inc=1, device_id={"head": partner}, device_id_type=MESH_ID)
     waits = (place if later_sends else count - 1 - place) + 1
+    if extra is not None:
+        waits = extra() + 1
     pl.semaphore_wait(barrier, waits)
     return partner
 
 
-def layer_forward_kernel(heads, layer, h_ref, gain_mix_ref, gain_ff_ref, wdt_ref,
+VM = pl.BlockSpec(memory_space=pltpu.VMEM)
+ANY = pl.BlockSpec(memory_space=pl.ANY)
+DMA = pltpu.SemaphoreType.DMA
+UNITS = 4
+
+
+def add_rows(out, terms):
+    rows = out.shape[0]
+    size = min(64, rows)
+
+    def one(i, carry):
+        part = pl.ds(pl.multiple_of(i * size, size), size)
+        total = terms[0][part, :].astype(f32)
+        for term in terms[1:]:
+            total = total + term[part, :].astype(f32)
+        out[part, :] = total.astype(out.dtype)
+        return carry
+    lax.fori_loop(0, rows // size, one, 0)
+
+
+def dp_spot():
+    spot = lax.axis_index("dp")
+    return lax.rem(spot, 2), spot // 2, lax.axis_size("dp") // 2
+
+
+def greet_sums():
+    barrier = pltpu.get_barrier_semaphore()
+    core, group, others = dp_spot()
+    count = lax.axis_size("seq")
+    place = lax.axis_index("seq")
+    targets = [{"dp": group * 2 + 1 - core}]
+    targets += [{"dp": lax.rem(group + k, others) * 2 + core} for k in range(1, others)]
+    targets += [{"seq": lax.rem(place + k, count)} for k in range(1, count)]
+    for target in targets:
+        pl.semaphore_signal(barrier, inc=1, device_id=target, device_id_type=MESH_ID)
+    return len(targets)
+
+
+class CrossSum:
+    def __init__(self, ranges, buffers, sems):
+        self.ranges = ranges
+        self.own, self.first, self.second = buffers
+        self.load_sem, self.first_send, self.first_recv, self.second_send, self.second_recv = sems
+        self.core, self.group, self.others = dp_spot()
+        self.loads, self.firsts, self.seconds = [], [], []
+
+    def start(self):
+        span = self.own.shape[2]
+        for n, (grad, columns) in enumerate(self.ranges):
+            self.firsts.append([])
+            self.loads.append([])
+            for g in range(self.others):
+                theirs = pl.ds(pl.multiple_of((2 * g + 1 - self.core) * span, span), span)
+                mine = pl.ds(pl.multiple_of((2 * g + self.core) * span, span), span)
+                self.firsts[n].append(remote(
+                    grad.at[theirs, columns], self.first.at[n, g], self.first_send.at[n, g],
+                    self.first_recv.at[n, g], "dp", self.group * 2 + 1 - self.core))
+                self.loads[n].append(pltpu.make_async_copy(
+                    grad.at[mine, columns], self.own.at[n, g], self.load_sem.at[n, g]))
+                self.firsts[n][g].start()
+                self.loads[n][g].start()
+
+    def step_a(self, n):
+        for g in range(self.others):
+            self.loads[n][g].wait()
+            self.firsts[n][g].wait_recv()
+        copies = []
+        for k in range(1, self.others):
+            peer = lax.rem(self.group + k, self.others)
+            theirs = self.own.at[n, peer]
+            add_rows(theirs, [theirs, self.first.at[n, peer]])
+            copies.append(remote(
+                theirs, self.second.at[n, k - 1], self.second_send.at[n, k - 1], self.second_recv.at[n, k - 1],
+                "dp", peer * 2 + self.core))
+            copies[-1].start()
+        self.seconds.append(copies)
+
+    def step_b(self, n, out):
+        for copy in self.seconds[n]:
+            copy.wait_recv()
+        add_rows(out, [self.own.at[n, self.group], self.first.at[n, self.group]]
+                 + [self.second.at[n, k] for k in range(self.others - 1)])
+
+    def finish(self):
+        for n in range(len(self.ranges)):
+            for copy in self.firsts[n] + self.seconds[n]:
+                copy.wait_send()
+
+
+class LineSum:
+    def __init__(self, pieces, received, send_sem, recv_sem):
+        self.pieces = pieces
+        self.received, self.send_sem, self.recv_sem = received, send_sem, recv_sem
+        self.count = lax.axis_size("seq")
+        self.place = lax.axis_index("seq")
+        self.shard = received.shape[2]
+        self.copies = [[] for _ in pieces]
+
+    def rows(self, shard):
+        return pl.ds(pl.multiple_of(shard * self.shard, self.shard), self.shard)
+
+    def pass_on(self, n, bit):
+        step = 2 ** bit
+        side = lax.rem(lax.div(self.place, step), 2)
+        target = self.place + step - 2 * step * side
+        low = lax.rem(target, 2 * step)
+        copies = []
+        slot = self.count - self.count // step
+        for m in range(self.count // (2 * step)):
+            copies.append(remote(
+                self.pieces[n].at[self.rows(low + 2 * step * m)], self.received.at[n, slot + m],
+                self.send_sem.at[n, slot + m], self.recv_sem.at[n, slot + m], "seq", target))
+            copies[-1].start()
+        self.copies[n].append(copies)
+
+    def take_in(self, n, bit):
+        step = 2 ** bit
+        low = lax.rem(self.place, 2 * step)
+        slot = self.count - self.count // step
+        for m, copy in enumerate(self.copies[n][bit]):
+            copy.wait_recv()
+            rows = self.pieces[n].at[self.rows(low + 2 * step * m)]
+            if 2 * step == self.count:
+                return [rows, self.received.at[n, slot + m]]
+            add_rows(rows, [rows, self.received.at[n, slot + m]])
+
+    def step_c(self, n):
+        self.pass_on(n, 0)
+
+    def step_d(self, n):
+        bit = 1
+        while 2 ** bit < self.count:
+            self.take_in(n, bit - 1)
+            self.pass_on(n, bit)
+            bit += 1
+
+    def step_e(self, n, write):
+        write(n, self.take_in(n, len(self.copies[n]) - 1))
+
+    def finish(self):
+        for steps in self.copies:
+            for copies in steps:
+                for copy in copies:
+                    copy.wait_send()
+
+
+def cut_columns(refs):
+    ranges = []
+    for ref in refs:
+        size = ref.shape[1] // UNITS
+        ranges += [(ref, pl.ds(u * size, size)) for u in range(UNITS)]
+    return ranges
+
+
+def cross_scratch(ranges, span, columns):
+    others = lax.axis_size("dp") // 2
+    size = columns // UNITS
+    peers = max(others - 1, 1)
+    return [
+        pltpu.VMEM((ranges, others, span, size), bf16), pltpu.VMEM((ranges, others, span, size), bf16),
+        pltpu.VMEM((ranges, peers, span, size), bf16), DMA((ranges, others)), DMA((ranges, others)),
+        DMA((ranges, others)), DMA((ranges, peers)), DMA((ranges, peers)),
+    ]
+
+
+def line_scratch(ranges, span, columns):
+    count = lax.axis_size("seq")
+    return [pltpu.VMEM((ranges, count - 1, span // count, columns // UNITS), bf16),
+            DMA((ranges, count - 1)), DMA((ranges, count - 1))]
+
+
+CROSS_REFS = 8
+LINE_REFS = 3
+
+
+def last_sum_kernel(widths, *refs):
+    grads, half, done = refs[:2], refs[2], refs[3]
+    kinds = len(widths[0]) + len(widths[1])
+    outs = refs[4:4 + kinds]
+    scratch = refs[4 + kinds:]
+    partners = greet_sums()
+    pl.semaphore_wait(pltpu.get_barrier_semaphore(), partners)
+    halves, early_half = scratch[:2]
+    for n, (_, columns) in enumerate(cut_columns([half])):
+        early_half[n] = half[:, columns]
+    early = LineSum([early_half.at[n] for n in range(UNITS)], *scratch[2:5])
+    cross = CrossSum(cut_columns(grads), scratch[5:8], scratch[8:13])
+    total = len(cross.ranges)
+    line = LineSum([halves.at[n] for n in range(total)], *scratch[13:])
+    cross.start()
+    for n in range(UNITS):
+        early.step_c(n)
+    pieces = []
+    which = 0
+    for a in range(2):
+        at = 0
+        for width in widths[a]:
+            pieces.append((a, at, width, outs[which]))
+            at += width
+            which += 1
+
+    def write(layer, array, n, terms):
+        size = terms[0].shape[1]
+        begin = n % UNITS * size
+        for a, at, width, out in pieces:
+            low, high = max(at, begin), min(at + width, begin + size)
+            if a == array and low < high:
+                add_rows(out.at[layer, :, pl.ds(low - at, high - low)],
+                         [term.at[:, pl.ds(low - begin, high - low)] for term in terms])
+
+    def write_early(n, terms):
+        write(1, 1, n, terms)
+
+    def write_line(n, terms):
+        write(0, n // UNITS, n, terms)
+    for n in range(total):
+        cross.step_a(n)
+        if n < UNITS:
+            early.step_d(n)
+    for a, at, width, out in pieces:
+        if a == 0:
+            out[1] = done[:, at:at + width]
+    for n in range(total + 2):
+        if n < total:
+            cross.step_b(n, halves.at[n])
+            line.step_c(n)
+        if 1 <= n <= total:
+            line.step_d(n - 1)
+        if n < UNITS:
+            early.step_e(n, write_early)
+        if n >= 2:
+            line.step_e(n - 2, write_line)
+    early.finish()
+    cross.finish()
+    line.finish()
+
+
+def last_sum(grads, half, done, widths):
+    columns = grads[0].shape[1]
+    span = half.shape[0]
+    shard = span // lax.axis_size("seq")
+    total = 2 * UNITS
+    return pl.pallas_call(
+        functools.partial(last_sum_kernel, widths),
+        out_shape=[jax.ShapeDtypeStruct((2, shard, width), f32) for width in widths[0] + widths[1]],
+        in_specs=[ANY] * 2 + [VM] * 2,
+        out_specs=[VM] * (len(widths[0]) + len(widths[1])),
+        scratch_shapes=[pltpu.VMEM((total, span, columns // UNITS), bf16),
+                        pltpu.VMEM((UNITS, span, columns // UNITS), bf16), *line_scratch(UNITS, span, columns),
+                        *cross_scratch(total, span, columns), *line_scratch(total, span, columns)],
+        compiler_params=pltpu.CompilerParams(
+            vmem_limit_bytes=VMEM_LIMIT, collective_id=9, has_side_effects=True),
+        cost_estimate=pl.CostEstimate(flops=0, bytes_accessed=400 * 1024 * 1024, transcendentals=0),
+    )(*grads, half, done)
+
+
+def unpack(pairs, out):
+    def one(i, carry):
+        rows = pl.ds(pl.multiple_of(i * 128, 128), 128)
+        out[rows, :] = pairs[rows].reshape(128, out.shape[1])
+        return carry
+    lax.fori_loop(0, out.shape[0] // 128, one, 0)
+
+
+def layer_forward_kernel(heads, layer, layers, h_ref, gain_mix_ref, gain_ff_ref, wdt_ref,
                          taps_ref, heads_ref, dcol_ref, dloc_ref, drow_ref,
-                         wkv_hbm, wbc_hbm, wx_hbm, wz_hbm, wq_hbm, wout_hbm, wo_hbm, wg_hbm, wu_hbm, wdown_hbm,
-                         h_out, normed_ref, gate_ref, stack_ref, rim_ref, pre_ref, dt_ref, q_ref, kvall_ref,
-                         att_ref, lse_ref, mem_ref, gated_ref, middle_ref, nff_ref, gu_ref, inner_ref,
-                         ext, y, wkv_ref, wbc_ref, wzx_ref, wq_ref, wo_ref, wout_ref, wgu_ref, wdown_ref, rim_in, kv_in, chain_in, chain_out,
-                         part_out, part_in, down_out, down_in,
-                         load_sem, kv_send, kv_recv, rim_send, rim_recv, chain_send, chain_recv,
-                         part_send, part_recv, down_send, down_recv):
+                         wkv_hbm, wbc_hbm, zx_hbm, wq_hbm, wout_hbm, wo_hbm, gu_hbm, wdown_hbm, *refs):
+    ready = layer > 0
+    follows = layer + 1 < layers
+    refs = list(refs)
+    zx_ready = refs.pop(0) if ready else None
+    (h_out, normed_ref, gate_ref, stack_ref, rim_ref, pre_ref, dt_ref, q_ref, kvall_ref,
+     att_ref, lse_ref, mem_ref, gated_ref, middle_ref, nff_ref, gu_ref, inner_ref, gu_out) = refs[:18]
+    refs = refs[18:]
+    zx_out = None if ready else refs.pop(0)
+    zx_next = refs.pop(0) if follows else None
+    (ext, y, wkv_ref, wbc_ref, wzx_ref, wq_ref, wo_ref, wout_ref, wgu_ref, wdown_ref, raw_zx, raw_gu,
+     rim_in, kv_in, chain_in, chain_out, part_out, part_in, down_out, down_in,
+     load_sem, kv_send, kv_recv, rim_send, rim_recv, chain_send, chain_recv,
+     part_send, part_recv, down_send, down_recv) = refs
     rows = dt_ref.shape[0]
     d_local = gate_ref.shape[1]
     ff_local = inner_ref.shape[1]
     count = lax.axis_size("seq")
     place = lax.axis_index("seq")
     loads = {}
-    for name, src, dst in (
-        ("kv", wkv_hbm, wkv_ref), ("bc", wbc_hbm, wbc_ref), ("x", wx_hbm, wzx_ref.at[:, pl.ds(d_local, d_local)]),
-        ("z", wz_hbm, wzx_ref.at[:, pl.ds(0, d_local)]), ("q", wq_hbm, wq_ref), ("out", wout_hbm, wout_ref),
-        ("o", wo_hbm, wo_ref), ("g", wg_hbm, wgu_ref.at[:, pl.ds(0, ff_local)]),
-        ("u", wu_hbm, wgu_ref.at[:, pl.ds(ff_local, ff_local)]), ("down", wdown_hbm, wdown_ref),
-    ):
-        loads[name] = pltpu.make_async_copy(src.at[layer], dst, load_sem.at[len(loads)])
-    for load in loads.values():
-        load.start()
+    plan = [("kv", wkv_hbm.at[layer], wkv_ref), ("bc", wbc_hbm.at[layer], wbc_ref)]
+    plan.append(("zx", zx_ready, wzx_ref) if ready else ("zx", zx_hbm.at[layer], raw_zx))
+    plan += [("q", wq_hbm.at[layer], wq_ref), ("out", wout_hbm.at[layer], wout_ref), ("o", wo_hbm.at[layer], wo_ref),
+             ("gu", gu_hbm.at[layer], raw_gu), ("down", wdown_hbm.at[layer], wdown_ref)]
+    later = [("gu_store", wgu_ref, gu_out)]
+    if not ready:
+        later.append(("zx_store", wzx_ref, zx_out))
+    if follows:
+        later += [("next", zx_hbm.at[layer + 1], raw_zx), ("next_store", wzx_ref, zx_next)]
+    for name, src, dst in plan + later:
+        loads[name] = pltpu.make_async_copy(src, dst, load_sem.at[len(loads)])
+    for name, src, dst in plan:
+        loads[name].start()
     partner = meet(count, False)
 
     normed_ref[...] = rms_scaled(h_ref[...].astype(f32), gain_mix_ref[...]).astype(bf16)
@@ -156,7 +433,12 @@
             kv_copies[j - 1].start()
     loads["bc"].wait()
     stack_ref[:, d_local:] = nn(normed, wbc_ref[...]).astype(bf16)
-    loads["x"].wait()
+    loads["zx"].wait()
+    if not ready:
+        unpack(raw_zx, wzx_ref)
+        loads["zx_store"].start()
+    if follows:
+        loads["next"].start()
     stack_ref[:, :d_local] = nn(normed, wzx_ref[:, d_local:]).astype(bf16)
     rim_copy = remote(stack_ref.at[pl.ds(rows - RIM, RIM)], rim_in, rim_send, rim_recv, "seq", place + 1)
 
@@ -169,7 +451,6 @@
         rim_in[...] = jnp.zeros(rim_in.shape, bf16)
         chain_in[...] = jnp.zeros(chain_in.shape, bf16)
     dt_ref[...] = nn(normed, wdt_ref[...]).astype(bf16).astype(f32)
-    loads["z"].wait()
     gate_ref[...] = nn(normed, wzx_ref[:, :d_local]).astype(bf16)
     loads["q"].wait()
     q_ref[...] = nn(normed, wq_ref[...]).astype(bf16)
@@ -261,8 +542,9 @@
         copy = remote(part_out.at[chunk], part_in.at[chunk], part_send.at[i], part_recv.at[i], "head", partner)
         copy.start()
         part_copies.append(copy)
-    loads["g"].wait()
-    loads["u"].wait()
+    loads["gu"].wait()
+    unpack(raw_gu, wgu_ref)
+    loads["gu_store"].start()
     loads["down"].wait()
     for i, chunk in enumerate(chunks):
         part_copies[i].wait_recv()
@@ -276,10 +558,19 @@
         copy = remote(down_out.at[chunk], down_in.at[chunk], down_send.at[i], down_recv.at[i], "head", partner)
         copy.start()
         down_copies.append(copy)
+    if not ready:
+        loads["zx_store"].wait()
+    if follows:
+        loads["next"].wait()
+        unpack(raw_zx, wzx_ref)
+        loads["next_store"].start()
     for i, chunk in enumerate(chunks):
         down_copies[i].wait_recv()
         h_out[chunk, :] = (middle_ref[chunk, :] + (
             down_out[chunk, :].astype(f32) + down_in[chunk, :].astype(f32))).astype(bf16)
+    loads["gu_store"].wait()
+    if follows:
+        loads["next_store"].wait()
     for i in range(len(chunks)):
         part_copies[i].wait_send()
         down_copies[i].wait_send()
@@ -295,15 +586,11 @@
             kv_copies[j - 1].wait_send()
 
 
-VM = pl.BlockSpec(memory_space=pltpu.VMEM)
-ANY = pl.BlockSpec(memory_space=pl.ANY)
-DMA = pltpu.SemaphoreType.DMA
-
-
-def layer_forward(layer, hidden, w, context):
+def layer_forward(layer, hidden, zx, w, context):
     dcol, dloc, drow = context
     rows, model_width = hidden.shape
     heads = w["heads"]
+    layers = w["out"].shape[0]
     d_local = w["out"].shape[1]
     ff_local = w["down"].shape[1]
     q_width = w["q"].shape[2]
@@ -311,40 +598,47 @@
     count = lax.axis_size("seq")
     length = count * rows
     parts = rows // CHUNK
+    wide = ((model_width, 2 * d_local), bf16)
     outs = [
         ((rows, model_width), bf16), ((rows, model_width), bf16), ((rows, d_local), bf16), ((rows, width), bf16),
         ((RIM, width), bf16), ((rows, width), f32), ((rows, 128), f32), ((rows, q_width), bf16),
         ((length, 2 * HD), bf16), ((rows, q_width), bf16), ((rows, 128), f32), ((d_local, NS), bf16),
         ((rows, d_local), bf16), ((rows, model_width), f32), ((rows, model_width), bf16),
-        ((rows, 2 * ff_local), bf16), ((rows, ff_local), bf16),
+        ((rows, 2 * ff_local), bf16), ((rows, ff_local), bf16), ((model_width, 2 * ff_local), bf16),
     ]
+    kept = len(outs) - 1
+    outs += [wide] * ((layer == 0) + (layer + 1 < layers))
     full = (rows, model_width)
+    given = [] if layer == 0 else [zx]
     result = pl.pallas_call(
-        functools.partial(layer_forward_kernel, heads, layer),
+        functools.partial(layer_forward_kernel, heads, layer, layers),
         out_shape=[jax.ShapeDtypeStruct(shape, kind) for shape, kind in outs],
-        in_specs=[VM] * 9 + [ANY] * 10,
-        out_specs=[VM] * len(outs),
+        in_specs=[VM] * 9 + [ANY] * (8 + len(given)),
+        out_specs=[VM] * kept + [ANY] * (len(outs) - kept),
         scratch_shapes=[
             pltpu.VMEM((rows + RIM, width), f32), pltpu.VMEM((rows, d_local), f32),
             pltpu.VMEM((model_width, 2 * HD), bf16), pltpu.VMEM((model_width, 2 * NS), bf16),
             pltpu.VMEM((model_width, 2 * d_local), bf16), pltpu.VMEM((model_width, q_width), bf16),
             pltpu.VMEM((q_width, model_width), bf16), pltpu.VMEM((d_local, model_width), bf16),
             pltpu.VMEM((model_width, 2 * ff_local), bf16), pltpu.VMEM((ff_local, model_width), bf16),
+            pltpu.VMEM((model_width, 2, d_local), bf16), pltpu.VMEM((model_width, 2, ff_local), bf16),
             pltpu.VMEM((RIM, width), bf16), pltpu.VMEM((length, 2 * HD), bf16),
             pltpu.VMEM((d_local, NS), bf16), pltpu.VMEM((d_local, NS), bf16),
             pltpu.VMEM(full, bf16), pltpu.VMEM(full, bf16), pltpu.VMEM(full, bf16), pltpu.VMEM(full, bf16),
-            DMA((10,)), DMA((count - 1,)), DMA((count - 1,)), DMA, DMA, DMA((heads // 2,)), DMA((heads // 2,)),
+            DMA((12,)), DMA((count - 1,)), DMA((count - 1,)), DMA, DMA, DMA((heads // 2,)), DMA((heads // 2,)),
             DMA((parts,)), DMA((parts,)), DMA((parts,)), DMA((parts,)),
         ],
         compiler_params=pltpu.CompilerParams(
             vmem_limit_bytes=VMEM_LIMIT, collective_id=layer, has_side_effects=True),
     )(hidden, w["gain_mix"][layer], w["gain_ff"][layer], w["dt"][layer], w["taps"][layer], w["head_vals"][layer],
-      dcol, dloc, drow, w["kv"], w["bc"], w["x"], w["z"], w["q"], w["out"], w["o"], w["g"], w["u"], w["down"])
+      dcol, dloc, drow, w["kv"], w["bc"], w["zx"], w["q"], w["out"], w["o"], w["gu"], w["down"], *given)
     names = ("out", "normed", "gate", "stack", "rim", "pre", "dt", "q", "kv", "att", "lse", "memory",
-             "gated", "middle", "nff", "gu", "inner")
+             "gated", "middle", "nff", "gu", "inner", "w_gu")
     saved = dict(zip(names, result))
     saved["hidden"] = hidden
-    return saved.pop("out"), saved
+    extra = list(result[len(names):])
+    saved["w_zx"] = extra.pop(0) if layer == 0 else zx
+    return saved.pop("out"), (extra.pop(0) if extra else None), saved
 
 
 def norm_back(hidden, gain, grad):
@@ -356,12 +650,15 @@
 
 
 def store_blocks(compute, slots, out, sems):
+    size = slots.shape[1]
     columns = out.shape[1]
+    blocks = out.shape[0] // size
+
+    def rows(i):
+        return pl.ds(pl.multiple_of(i * size, size), size)
 
     def copy(i, slot):
-        rows = pl.ds(pl.multiple_of(i * 256, 256), 256)
-        return pltpu.make_async_copy(slots.at[slot, :, pl.ds(0, columns)], out.at[rows], sems.at[slot])
-    blocks = out.shape[0] // 256
+        return pltpu.make_async_copy(slots.at[slot, :, pl.ds(0, columns)], out.at[rows(i)], sems.at[slot])
 
     def one(i, carry):
         slot = lax.rem(i, 2)
@@ -369,7 +666,7 @@
         @pl.when(i >= 2)
         def _():
             copy(i - 2, slot).wait()
-        compute(pl.ds(pl.multiple_of(i * 256, 256), 256), slot)
+        compute(rows(i), slot)
         copy(i, slot).start()
         return carry
     lax.fori_loop(0, blocks, one, 0)
@@ -377,18 +674,26 @@
         copy(i, i % 2).wait()
 
 
-def layer_backward_kernel(heads, layer, grad_ref, h_ref, normed_ref, gate_ref, stack_ref, rim_ref, pre_ref, dt_ref,
+def layer_backward_kernel(heads, layer, schedule, grad_ref, h_ref, normed_ref, gate_ref, stack_ref, rim_ref, pre_ref, dt_ref,
                           q_ref, kv_ref, att_ref, lse_ref, mem_ref, gated_ref, middle_ref, nff_ref, gu_ref,
                           inner_ref, gain_mix_ref, gain_ff_ref, wdt_ref,
                           taps_ref, heads_ref, dcol_ref, dloc_ref, drow_ref,
-                          wdown_hbm, wg_hbm, wu_hbm, wout_hbm, wo_hbm, wz_hbm, wx_hbm, wbc_hbm, wq_hbm, wkv_hbm,
-                          g_out, gff_out, gmix_out, gbc_out, dtaps_ref, dheads_ref, gains_ref,
-                          wdown_ref, wide_ref, wout_ref, wo_ref, wbc_ref, wq_ref, wkv_ref,
-                          gff, dgu, one_out, one_in, two_out, two_in, gmid, branch, gg, datt, dy_s, dxs_s, u_s,
-                          decay_s, probs_s, acc, dkv_out, dkv_in, chain_in, chain_out, rim_in,
-                          ext, pad, dext, dgate, dstack, dq, dkv, draw_s,
-                          load_sem, one_send, one_recv, two_send, two_recv, chain_send, chain_recv,
-                          rim_send, rim_recv, kv_send, kv_recv, gblk, grad_sem):
+                          wdown_hbm, wgu_hbm, wout_hbm, wo_hbm, wzx_hbm, wbc_hbm, wq_hbm, wkv_hbm, *refs):
+    refs = list(refs)
+    own_sum = schedule["own"]
+    source = None if own_sum else refs.pop(0)
+    half_in = None if own_sum else refs.pop(0)
+    if not own_sum:
+        line_refs, refs = refs[-LINE_REFS - 1:], refs[:-LINE_REFS - 1]
+    cross_refs, refs = refs[-CROSS_REFS:], refs[:-CROSS_REFS]
+    summed_ref = None if own_sum else refs.pop(0)
+    (g_out, gff_out, gmix_out, gbc_out, small_ref, half_ref,
+     wdown_ref, wide_ref, wout_ref, wo_ref, wbc_ref, wq_ref, wkv_ref,
+     gff, dgu, one_out, one_in, two_out, two_in, gmid, branch, gg, datt, dy_s, dxs_s, u_s,
+     decay_s, probs_s, acc, dkv_out, dkv_in, chain_in, chain_out, rim_in,
+     ext, pad, dext, dgate, dstack, dq, dkv, draw_s,
+     load_sem, one_send, one_recv, two_send, two_recv, chain_send, chain_recv,
+     rim_send, rim_recv, kv_send, kv_recv, gblk, grad_sem) = refs
     rows = dt_ref.shape[0]
     d_local = gate_ref.shape[1]
     ff_local = inner_ref.shape[1]
@@ -402,21 +707,47 @@
     wzx_ref = wide_ref.at[:, pl.ds(0, 2 * d_local)]
     loads = {}
     for name, src, dst in (
-        ("down", wdown_hbm, wdown_ref), ("g", wg_hbm, wide_ref.at[:, pl.ds(0, ff_local)]),
-        ("u", wu_hbm, wide_ref.at[:, pl.ds(ff_local, ff_local)]), ("out", wout_hbm, wout_ref),
-        ("o", wo_hbm, wo_ref), ("bc", wbc_hbm, wbc_ref), ("q", wq_hbm, wq_ref), ("kv", wkv_hbm, wkv_ref),
-        ("z", wz_hbm, wide_ref.at[:, pl.ds(0, d_local)]), ("x", wx_hbm, wide_ref.at[:, pl.ds(d_local, d_local)]),
+        ("down", wdown_hbm.at[layer], wdown_ref), ("gu", wgu_hbm, wgu_ref), ("out", wout_hbm.at[layer], wout_ref),
+        ("o", wo_hbm.at[layer], wo_ref), ("bc", wbc_hbm.at[layer], wbc_ref), ("q", wq_hbm.at[layer], wq_ref),
+        ("kv", wkv_hbm.at[layer], wkv_ref), ("zx", wzx_hbm, wzx_ref),
     ):
-        loads[name] = pltpu.make_async_copy(src.at[layer], dst, load_sem.at[len(loads)])
-    for name in ("down", "g", "u", "out", "o", "bc", "q", "kv"):
+        loads[name] = pltpu.make_async_copy(src, dst, load_sem.at[len(loads)])
+    for name in ("down", "gu", "out", "o", "bc", "q", "kv"):
         loads[name].start()
-    partner = meet(count, True)
+    partner = meet(count, True, greet_sums)
+    cross = CrossSum(cut_columns([gff_out if own_sum else source]), cross_refs[:3], cross_refs[3:])
+    ranges = [columns for _, columns in cut_columns([half_ref])]
+    steps_of = {"a": cross.step_a, "b": lambda n: cross.step_b(n, half_ref.at[:, ranges[n]])}
+    if not own_sum:
+        fetches = [pltpu.make_async_copy(half_in.at[:, columns], line_refs[0].at[n], load_sem.at[len(loads) + n])
+                   for n, (_, columns) in enumerate(cut_columns([half_in]))]
+        for fetch in fetches:
+            fetch.start()
+        for fetch in fetches:
+            fetch.wait()
+        line = LineSum([line_refs[0].at[n] for n in range(UNITS)], *line_refs[1:])
+
+        def write(n, terms):
+            size = terms[0].shape[1]
+            add_rows(summed_ref.at[:, pl.ds(n * size, size)], terms)
+        steps_of.update({"c": line.step_c, "d": line.step_d, "e": lambda n: line.step_e(n, write)})
+
+    def pump(spot):
+        for step in schedule.get(spot, ()):
+            if step == "start":
+                cross.start()
+            elif step == "finish":
+                cross.finish()
+                if not own_sum:
+                    line.finish()
+            else:
+                steps_of[step[0]](int(step[1]))
+    pump("begin")
     chunks = [pl.ds(begin, CHUNK) for begin in range(0, rows, CHUNK)]
 
     gff[...] = grad_ref[...].astype(bf16)
     loads["down"].wait()
-    loads["g"].wait()
-    loads["u"].wait()
+    loads["gu"].wait()
     one_copies, two_copies = [], []
     for i, chunk in enumerate(chunks):
         grad_inner = nt(gff[chunk, :], wdown_ref[...])
@@ -429,8 +760,7 @@
         copy = remote(one_out.at[chunk], one_in.at[chunk], one_send.at[i], one_recv.at[i], "head", partner)
         copy.start()
         one_copies.append(copy)
-    loads["z"].start()
-    loads["x"].start()
+    loads["zx"].start()
 
     @pl.when(place == count - 1)
     def _():
@@ -441,10 +771,13 @@
         def _():
             dkv_in[(j - 1) * rows:j * rows, :] = jnp.zeros((rows, 2 * HD), bf16)
 
+    pump("ff0")
+
     def ff_weights(block, slot):
         gblk[slot, :, :ff_local] = tn(gff[:, block], inner_ref[...]).astype(bf16)
         gblk[slot, :, ff_local:3 * ff_local] = tn(nff_ref[:, block], dgu[...]).astype(bf16)
     store_blocks(ff_weights, gblk, gff_out, grad_sem)
+    pump("ff")
 
     raw, step, log_decay, running, running_t, ordered = ssm_scalars(dt_ref, heads_ref)
     mapping = head_map(heads, d_local // heads)
@@ -493,8 +826,12 @@
     gate_act = gate * gate_sig
     loads["out"].wait()
     loads["o"].wait()
+    dtaps_ref = small_ref.at[pl.ds(0, 8)]
+    gains_ref = small_ref.at[pl.ds(8, 8)]
+    dheads_ref = small_ref.at[pl.ds(16, 8)]
     gains_ref[...] = jnp.zeros(gains_ref.shape, f32)
     for i, chunk in enumerate(chunks):
+        pump("one%d" % i)
         one_copies[i].wait_recv()
         grad = one_out[chunk, :].astype(f32) + one_in[chunk, :].astype(f32)
         moved, gain = norm_back(middle_ref[chunk, :], gain_ff_ref[...], grad)
@@ -509,6 +846,7 @@
     dcb = jnp.zeros((rows, rows), f32)
     chain_copies = []
     for pair in range(pairs):
+        pump("pair%d" % pair)
         span = slice(pair * 128, pair * 128 + 128)
         copy = remote(chain_out.at[pl.ds(pair * 128, 128)], chain_in.at[pl.ds(pair * 128, 128)],
                       chain_send.at[pair], chain_recv.at[pair], "seq", place - 1)
@@ -560,6 +898,7 @@
         @pl.when(place >= j)
         def _():
             copy.start()
+    pump("post")
     memory = mem_ref[...]
     gmem = chain_in[...]
     carried = decs * nt(c_rows, memory)
@@ -609,17 +948,18 @@
     draw = (gstep - jnp.exp(heads_ref[1:2, :]) * dlog) * sigmoid(raw)
     draw_s[...] = draw.astype(bf16)
     dskip = exact(jnp.sum(grad_ssm * values, axis=0, keepdims=True) + jnp.zeros((8, 1), f32), mapping, (1, 1))
-    dheads_ref[...] = jnp.zeros((8, 128), f32)
-    dheads_ref[0:1, :] = jnp.sum(draw, axis=0, keepdims=True)
-    dheads_ref[1:2, :] = jnp.sum(dlog * log_decay, axis=0, keepdims=True)
-    dheads_ref[2:3, :] = dskip[0:1, :]
-    for name in ("z", "x", "bc", "q", "kv"):
+    dheads_ref[...] = jnp.zeros(dheads_ref.shape, f32)
+    dheads_ref[0:1, :128] = jnp.sum(draw, axis=0, keepdims=True)
+    dheads_ref[1:2, :128] = jnp.sum(dlog * log_decay, axis=0, keepdims=True)
+    dheads_ref[2:3, :128] = dskip[0:1, :]
+    for name in ("zx", "bc", "q", "kv"):
         loads[name].wait()
 
     for j in range(1, count):
         @pl.when(place + j < count)
         def _():
             kv_copies[j - 1].wait_recv()
+    pump("two")
     own = pl.ds(pl.multiple_of(place * rows, rows), rows)
     total = acc[own, :]
     for j in range(1, count):
@@ -642,6 +982,10 @@
         copy.start()
         two_copies.append(copy)
 
+    gbc_out[:, model_width:] = jnp.transpose(jnp.concatenate(
+        [dtaps_ref[:, d_local:], jnp.zeros((120, 2 * NS), f32)], axis=0)).astype(bf16)
+    pump("mix")
+
     def mix_weights(block, slot):
         left = normed_ref[:, block]
         at = 0
@@ -656,11 +1000,13 @@
     store_blocks(mix_weights, gblk, gmix_out, grad_sem)
 
     for i, chunk in enumerate(chunks):
+        pump("last%d" % i)
         two_copies[i].wait_recv()
         grad = two_out[chunk, :].astype(f32) + two_in[chunk, :].astype(f32)
         moved, gain = norm_back(h_ref[chunk, :].astype(f32), gain_mix_ref[...], grad)
         gains_ref[0:1, :] += gain
         g_out[chunk, :] = gmid[chunk, :] + moved
+    pump("end")
     for i in range(len(chunks)):
         one_copies[i].wait_send()
         two_copies[i].wait_send()
@@ -676,7 +1022,16 @@
             kv_copies[j - 1].wait_send()
 
 
-def layer_backward(layer, grad, w, saved, context):
+SCHEDULES = (
+    {"own": False, "begin": ("start", "c0", "c1", "c2", "c3"), "ff0": ("a0", "a1", "a2", "a3"), "ff": ("d0", "d1"),
+     "one0": ("d2",), "one1": ("d3",), "mix": ("b0", "b1"), "last0": ("e0", "e1", "e2", "e3", "b2"),
+     "end": ("b3", "finish")},
+    {"own": True, "ff": ("start",), "one0": ("a0", "a1"), "one1": ("a2", "a3"), "mix": ("b0",), "last0": ("b1", "b2"),
+     "end": ("b3", "finish")},
+)
+
+
+def layer_backward(layer, grad, waiting, w, saved, context):
     dcol, dloc, drow = context
     rows, model_width = grad.shape
     heads = w["heads"]
@@ -688,10 +1043,16 @@
     length = count * rows
     parts = rows // CHUNK
     mix_width = 3 * d_local + 2 * q_width + 256
+    schedule = SCHEDULES[1 if waiting is None else 0]
+    given = [] if waiting is None else list(waiting)
     outs = [
         ((rows, model_width), f32), ((model_width, 3 * ff_local), bf16), ((model_width, mix_width), bf16),
-        ((2 * NS, model_width), bf16), ((8, width), f32), ((8, 128), f32), ((8, model_width), f32),
+        ((2 * NS, model_width + 128), bf16), ((24, max(width, model_width)), f32),
     ]
+    span = model_width // lax.axis_size("dp")
+    if waiting is not None:
+        outs.insert(0, ((span // count, 3 * ff_local), f32))
+    outs.append(((span, 3 * ff_local if waiting is None else mix_width), bf16))
     full = (rows, model_width)
     state = (d_local, NS)
     names = ("hidden", "normed", "gate", "stack", "rim", "pre", "dt", "q", "kv", "att", "lse", "memory",
@@ -700,10 +1061,10 @@
     def vm(shape, kind):
         return pltpu.VMEM(shape, kind)
     return pl.pallas_call(
-        functools.partial(layer_backward_kernel, heads, layer),
+        functools.partial(layer_backward_kernel, heads, layer, schedule),
         out_shape=[jax.ShapeDtypeStruct(shape, kind) for shape, kind in outs],
-        in_specs=[VM] * 26 + [ANY] * 10,
-        out_specs=[VM, ANY, ANY] + [VM] * 4,
+        in_specs=[VM] * 26 + [ANY] * (8 + len(given)),
+        out_specs=[VM] * (len(outs) - 5) + [ANY, ANY] + [VM] * 3,
         scratch_shapes=[
             vm((ff_local, model_width), bf16), vm((model_width, 2 * max(d_local, ff_local)), bf16),
             vm((d_local, model_width), bf16), vm((q_width, model_width), bf16), vm((model_width, 2 * NS), bf16),
@@ -717,185 +1078,18 @@
             vm((rows + RIM, width), f32), vm((rows + 16, width), f32), vm((rows + 8, width), f32),
             vm((rows, d_local), bf16), vm((rows, width), bf16), vm((rows, q_width), bf16),
             vm((rows, 2 * HD), bf16), vm((rows, 128), bf16),
-            DMA((10,)), DMA((parts,)), DMA((parts,)), DMA((parts,)), DMA((parts,)), DMA((heads // 2,)),
+            DMA((8 + UNITS,)), DMA((parts,)), DMA((parts,)), DMA((parts,)), DMA((parts,)), DMA((heads // 2,)),
             DMA((heads // 2,)), DMA, DMA, DMA((count - 1,)), DMA((count - 1,)),
-            vm((2, 256, max(3 * ff_local, mix_width)), bf16), DMA((2,)),
+            vm((2, 128, max(3 * ff_local, mix_width)), bf16), DMA((2,)),
+            *cross_scratch(UNITS, span, outs[-1][0][1]),
+            *([] if waiting is None else
+              [vm((UNITS, span, 3 * ff_local // UNITS), bf16), *line_scratch(UNITS, span, 3 * ff_local)]),
         ],
         compiler_params=pltpu.CompilerParams(
             vmem_limit_bytes=VMEM_LIMIT, collective_id=2 + layer, has_side_effects=True),
     )(grad, *[saved[name] for name in names], w["gain_mix"][layer], w["gain_ff"][layer], w["dt"][layer],
-      w["taps"][layer], w["head_vals"][layer], dcol, dloc, drow, w["down"], w["g"], w["u"], w["out"], w["o"],
-      w["z"], w["x"], w["bc"], w["q"], w["kv"])
-
-
-def pack_small(dtaps, dheads, gains, heads, d_local):
-    shards = lax.axis_size("dp") * lax.axis_size("seq")
-    taps = dtaps[:4, :d_local].reshape(4, heads, shards, -1)
-    return jnp.concatenate(
-        [gains[0].reshape(shards, -1), gains[1].reshape(shards, -1),
-         jnp.transpose(taps, (2, 0, 1, 3)).reshape(shards, -1),
-         jnp.broadcast_to(dheads[:3, :heads].reshape(1, -1), (shards, 3 * heads))], axis=1
-    )
-
-
-UNITS = 4
-
-
-def add_rows(out, terms):
-    rows = out.shape[0]
-    size = min(64, rows)
-
-    def one(i, carry):
-        part = pl.ds(pl.multiple_of(i * size, size), size)
-        total = terms[0][part, :].astype(f32)
-        for term in terms[1:]:
-            total = total + term[part, :].astype(f32)
-        out[part, :] = total.astype(out.dtype)
-        return carry
-    lax.fori_loop(0, rows // size, one, 0)
-
-
-def reduce_kernel(arrays, *refs):
-    grads = refs[:arrays]
-    outs = refs[arrays:2 * arrays]
-    (own, first, second, right_in, left_in, load_sem, first_send, first_recv, second_send, second_recv,
-     line_send, right_recv, left_recv) = refs[2 * arrays:]
-    others = grads[0].shape[0]
-    span = grads[0].shape[2]
-    count = lax.axis_size("seq")
-    shard = span // count
-    spot = lax.axis_index("dp")
-    place = lax.axis_index("seq")
-    core = lax.rem(spot, 2)
-    group = spot // 2
-    barrier = pltpu.get_barrier_semaphore()
-    sibling = spot + 1 - 2 * core
-    pl.semaphore_signal(barrier, inc=1, device_id={"dp": sibling}, device_id_type=MESH_ID)
-    peers = [lax.rem(group + k, others) * 2 + core for k in range(1, others)]
-    for peer in peers:
-        pl.semaphore_signal(barrier, inc=1, device_id={"dp": peer}, device_id_type=MESH_ID)
-
-    @pl.when(place > 0)
-    def _():
-        pl.semaphore_signal(barrier, inc=1, device_id={"seq": place - 1}, device_id_type=MESH_ID)
-
-    @pl.when(place < count - 1)
-    def _():
-        pl.semaphore_signal(barrier, inc=1, device_id={"seq": place + 1}, device_id_type=MESH_ID)
-    waits = others + 2 - (place == 0).astype(jnp.int32) - (place == count - 1).astype(jnp.int32)
-    pl.semaphore_wait(barrier, waits)
-
-    units = []
-    for a in range(arrays):
-        columns = grads[a].shape[3] // UNITS
-        for u in range(UNITS):
-            units.append((a, pl.ds(u * columns, columns)))
-    loads, firsts, seconds = [], [], []
-    for n, (a, columns) in enumerate(units):
-        loads.append(pltpu.make_async_copy(grads[a].at[:, core, :, columns], own.at[n], load_sem.at[n]))
-        firsts.append(remote(grads[a].at[:, 1 - core, :, columns], first.at[n], first_send.at[n],
-                             first_recv.at[n], "dp", sibling))
-        loads[n].start()
-        firsts[n].start()
-    for n in range(len(units)):
-        loads[n].wait()
-        firsts[n].wait_recv()
-        copies = []
-        for k, peer in enumerate(peers):
-            theirs = lax.rem(group + k + 1, others)
-            add_rows(own.at[n, theirs], [own.at[n, theirs], first.at[n, theirs]])
-            copy = remote(own.at[n, theirs], second.at[n, k], second_send.at[n, k], second_recv.at[n, k], "dp", peer)
-            copy.start()
-            copies.append(copy)
-        seconds.append(copies)
-    lines = []
-    for n, (a, columns) in enumerate(units):
-        for copy in seconds[n]:
-            copy.wait_recv()
-        total = own.at[n, group]
-        add_rows(total, [total, first.at[n, group]] + [second.at[n, k] for k in range(others - 1)])
-        copies = []
-        for j in range(count):
-            rows = pl.ds(j * shard, shard)
-            right = remote(total.at[rows], right_in.at[n, rows], line_send.at[n, j], right_recv.at[n, j],
-                           "seq", place + 1)
-            left = remote(total.at[rows], left_in.at[n, rows], line_send.at[n, j], left_recv.at[n, j],
-                          "seq", place - 1)
-
-            @pl.when(place < j)
-            def _():
-                @pl.when(place > 0)
-                def _():
-                    right.wait_recv()
-                    add_rows(total.at[rows], [total.at[rows], right_in.at[n, rows]])
-                right.start()
-
-            @pl.when(place > j)
-            def _():
-                @pl.when(place < count - 1)
-                def _():
-                    left.wait_recv()
-                    add_rows(total.at[rows], [total.at[rows], left_in.at[n, rows]])
-                left.start()
-            copies.append((right, left))
-        lines.append(copies)
-    for n, (a, columns) in enumerate(units):
-        total = own.at[n, group]
-        for j in range(count):
-            right, left = lines[n][j]
-            rows = pl.ds(j * shard, shard)
-
-            @pl.when(place == j)
-            def _():
-                terms = [total.at[rows]]
-                if j > 0:
-                    right.wait_recv()
-                    terms.append(right_in.at[n, rows])
-                if j < count - 1:
-                    left.wait_recv()
-                    terms.append(left_in.at[n, rows])
-                add_rows(outs[a].at[:, columns], terms)
-    for n in range(len(units)):
-        firsts[n].wait_send()
-        for copy in seconds[n]:
-            copy.wait_send()
-        for j in range(count):
-            right, left = lines[n][j]
-
-            @pl.when(place < j)
-            def _():
-                right.wait_send()
-
-            @pl.when(place > j)
-            def _():
-                left.wait_send()
-
-
-def reduce_grads(arrays):
-    count = lax.axis_size("seq")
-    others = lax.axis_size("dp") // 2
-    rows = arrays[0].shape[0]
-    span = rows // (2 * others)
-    shard = span // count
-    columns = arrays[0].shape[1] // UNITS
-    total = len(arrays) * UNITS
-    views = [a.reshape(others, 2, span, a.shape[1]) for a in arrays]
-    return pl.pallas_call(
-        functools.partial(reduce_kernel, len(arrays)),
-        out_shape=[jax.ShapeDtypeStruct((shard, a.shape[1]), f32) for a in arrays],
-        in_specs=[ANY] * len(arrays),
-        out_specs=[VM] * len(arrays),
-        scratch_shapes=[
-            pltpu.VMEM((total, others, span, columns), bf16), pltpu.VMEM((total, others, span, columns), bf16),
-            pltpu.VMEM((total, others - 1, span, columns), bf16),
-            pltpu.VMEM((total, span, columns), bf16), pltpu.VMEM((total, span, columns), bf16),
-            DMA((total,)), DMA((total,)), DMA((total,)), DMA((total, others - 1)), DMA((total, others - 1)),
-            DMA((total, count)), DMA((total, count)), DMA((total, count)),
-        ],
-        compiler_params=pltpu.CompilerParams(
-            vmem_limit_bytes=VMEM_LIMIT, collective_id=9, has_side_effects=True),
-        cost_estimate=pl.CostEstimate(flops=0, bytes_accessed=400 * 1024 * 1024, transcendentals=0),
-    )(*views)
+      w["taps"][layer], w["head_vals"][layer], dcol, dloc, drow, w["down"], saved["w_gu"], w["out"], w["o"],
+      saved["w_zx"], w["bc"], w["q"], w["kv"], *given)
 
 
 def on_device(hidden_in, segment_ids, gain_mix, w_zx, w_bc, w_dt, conv_x, conv_bc, ssm_head, w_q, w_kv,
@@ -924,16 +1118,14 @@
         heads=heads,
         gain_mix=gain_mix[:, None].astype(f32),
         gain_ff=gain_ff[:, None].astype(f32),
-        z=w_zx[:, :, 0, :],
-        x=w_zx[:, :, 1, :],
+        zx=w_zx,
         bc=w_bc,
         dt=jnp.pad(w_dt, ((0, 0), (0, 0), (0, 128 - heads))),
         q=w_q,
         kv=w_kv.reshape(layers, model_width, -1),
         o=w_o,
         out=w_out,
-        g=w_gu[:, :, 0, :],
-        u=w_gu[:, :, 1, :],
+        gu=w_gu,
         down=w_down,
         taps=jnp.pad(jnp.concatenate([conv_x.reshape(layers, taps_count, -1), conv_bc], axis=2).astype(f32),
                      ((0, 0), (0, 8 - taps_count), (0, 0))),
@@ -941,61 +1133,43 @@
     )
     hidden = hidden_in
     saved = []
+    zx = None
     for l in range(layers):
-        hidden, kept = layer_forward(l, hidden, w, context)
+        hidden, zx, kept = layer_forward(l, hidden, zx, w, context)
         saved.append(kept)
     block_out = hidden
     gradient = cotangent.astype(f32)
-    wide, narrow, small = [], [None] * layers, [None] * layers
+    narrow, small = [None] * layers, [None] * layers
+    waiting = None
     for l in reversed(range(layers)):
-        gradient, ff_grads, mix_grads, g_bc, dtaps, dheads, gains = layer_backward(
-            l, gradient, w, saved[l], context)
-        wide = [ff_grads, mix_grads] + wide
-        narrow[l] = jnp.concatenate(
-            [g_bc, jnp.pad(jnp.transpose(dtaps[:4, d_local:]), ((0, 0), (0, 124))).astype(bf16)], axis=1)
-        small[l] = pack_small(dtaps, dheads, gains, heads, d_local)
-    g_bc = lax.psum_scatter(jnp.concatenate(narrow, axis=1), ("dp", "seq", "head"),
-                            scatter_dimension=0, tiled=True)
-    small = jnp.concatenate(small, axis=1)
-    shards, used = small.shape
-    room = -(-used // 1024) * 1024
-    small = jnp.pad(small, ((0, 0), (0, room - used))).reshape(shards * (room // 128), 128)
-    small = lax.psum_scatter(small, ("dp", "seq"), scatter_dimension=0, tiled=True)
-    small = small.reshape(-1)[:used]
-    summed = reduce_grads(wide)
-    parts = [(summed[2 * l], summed[2 * l + 1]) for l in range(layers)]
+        *summed, gradient, ff_grads, mix_grads, narrow[l], small[l], half = layer_backward(
+            l, gradient, waiting, w, saved[l], context)
+        waiting = (mix_grads, half)
+    g_bc = lax.psum_scatter(jnp.concatenate(narrow, axis=1), ("dp", "seq", "head"), scatter_dimension=0, tiled=True)
+    small = [lax.psum(a, ("dp", "seq")) for a in small]
+    shards = lax.axis_size("dp") * lax.axis_size("seq")
+    shard = lax.axis_index("dp") * lax.axis_size("seq") + place
     ff_local = w_down.shape[1]
     q_width = w_q.shape[2]
-    part = model_width // (lax.axis_size("dp") * lax.axis_size("seq"))
-
-    def both(pieces):
-        return jnp.stack(pieces, axis=0).astype(f32)
-
-    def cut(index, begin, size):
-        return [p[index][:, begin:begin + size] for p in parts]
-
-    down = both([jnp.transpose(a) for a in cut(0, 0, ff_local)])
-    gu = both(cut(0, ff_local, 2 * ff_local)).reshape(layers, part, 2, ff_local)
-    at = 2 * d_local
-    zx = both(cut(1, 0, at)).reshape(layers, part, 2, d_local)
-    q = both(cut(1, at, q_width))
-    at += q_width
-    kv = both(cut(1, at, 128)).reshape(layers, part, 1, 128)
-    at += 128
-    dt = both(cut(1, at, heads))
-    at += 128
-    out = both([jnp.transpose(a) for a in cut(1, at, d_local)])
-    at += d_local
-    o = both([jnp.transpose(a) for a in cut(1, at, q_width)])
+    part = model_width // shards
+    down, gu, zx, q, kv, dt, out, o = last_sum(
+        (ff_grads, mix_grads), half, summed[0],
+        ((ff_local, 2 * ff_local), (2 * d_local, q_width, 128, 128, d_local, q_width)))
+    down, out, o = (jnp.transpose(a, (0, 2, 1)) for a in (down, out, o))
+    gu = gu.reshape(layers, part, 2, ff_local)
+    zx = zx.reshape(layers, part, 2, d_local)
+    kv = kv.reshape(layers, part, 1, 128)
+    dt = dt[:, :, :heads]
     g_bc = g_bc.astype(f32).reshape(g_bc.shape[0], layers, -1)
     w_bc_grad = jnp.transpose(g_bc[:, :, :model_width], (1, 2, 0))
     conv_bc_grad = jnp.transpose(g_bc[:, :, model_width:model_width + taps_count], (1, 2, 0))
-    small = small.reshape(layers, -1)
-    gain_a = small[:, :part]
-    gain_b = small[:, part:2 * part]
-    taps_end = 2 * part + taps_count * d_local // (model_width // part)
-    conv_x_grad = small[:, 2 * part:taps_end].reshape(layers, taps_count, heads, -1)
-    head_grad = small[:, taps_end:].reshape(layers, 3, heads)
+    small = jnp.stack(small, axis=0)
+    gain_a = lax.dynamic_slice_in_dim(small[:, 8, :model_width], shard * part, part, 1)
+    gain_b = lax.dynamic_slice_in_dim(small[:, 9, :model_width], shard * part, part, 1)
+    taps = small[:, :taps_count, :d_local].reshape(layers, taps_count, heads, -1)
+    taps_part = taps.shape[3] // shards
+    conv_x_grad = lax.dynamic_slice_in_dim(taps, shard * taps_part, taps_part, 3)
+    head_grad = small[:, 16:19, :heads]
     return (block_out, gradient, gain_a, zx, w_bc_grad, dt, conv_x_grad, conv_bc_grad, head_grad, q, kv,
             o, out, gain_b, gu, down)
 

time: 515 us -> 391 us (0.76); the launches traced: 506 us -> 388 us
  Pallas kernels: 393 us -> 336 us
  local copies, waits for them, and re-layouts: 83.4 us -> 28 us
    pallas_call x5, Pallas kernels: 393 us -> 336 us  [the longest x2 143 us: layer_backward(): pl.pallas_call(functools.partial(layer_backward_kernel, heads, layer, sch...]
    slice x17 -> x3, local copies, waits for them, and re-layouts: 38.7 us -> 0.02 us  [the longest x1 0.01 us: on_device(): small[:, 9, :model_width]]
    squeeze x2 -> x0, local copies, waits for them, and re-layouts: 16.2 us -> none  [the longest x1 8.36 us: on_device(): w_zx[:, :, 0, :]]
    another operation x20 -> x1, local copies, waits for them, and re-layouts: 9.7 us -> 0.9 us  [on_device(): small = jnp.stack(small, axis=0)]
    another operation x8 -> x0, other arithmetic: 6.95 us -> none  [both(): return jnp.stack(pieces, axis=0).astype(f32)]
    unnamed x32 -> x35, local copies, waits for them, and re-layouts: 7.06 us -> 12.3 us
  transfers between devices with their start and end apart: 2 -> 2, of which waited for: 0 -> 0; matrix products, arithmetic and copies ran while one was open for 5% -> 4% of each run, Pallas kernels for 36% -> 25%
where the time goes in v4:
time: 391 us; the launch traced here: 388 us
  Pallas kernels  336 us (86%)
  local copies, waits for them, and re-layouts  28 us (7%)
  between operations  15.8 us (4%)
  other arithmetic  7.89 us (2%)
    pallas_call x2, Pallas kernels, layer_backward(): pl.pallas_call(functools.partial(layer_backward_kernel, heads, layer, sch...  143 us
    pallas_call x2, Pallas kernels, layer_forward(): pl.pallas_call(functools.partial(layer_forward_kernel, heads, layer, laye...  96.8 us
    pallas_call x1, Pallas kernels, last_sum(): pl.pallas_call(functools.partial(last_sum_kernel, widths), out_shape=[jax...  96.5 us
    unnamed x35, local copies, waits for them, and re-layouts  12.3 us
  transfers between devices with their start and end apart: 2, of which 0 were waited for; matrix products, arithmetic and copies ran while one was open for 4% of the time, Pallas kernels for 25%

profile of v4, /device:TPU:0, one launch (start us, length us, event | category | flops | bytes accessed | tf_op | source)
XLA Modules:
  0.0 388.0 jit_solution(1764502974281350869)
XLA Ops:
  8.1 0.8 pad_dynamic-slice_fusion
  9.5 0.7 convert_element_type.37
  10.2 0.7 copy.57
  11.5 0.7 copy.56
  12.3 0.7 fusion.5
  13.7 1.4 compare_convert_fusion
  15.2 1.1 copy.55
  16.3 0.9 fusion.1
  17.2 2.1 convert_element_type.38.grad_ref
  20.0 0.7 pad.24.dcol_ref
  21.8 48.2 %shard_map.288 = (bf16[256,1024]{1,0:T(8,128)(2,1)}, bf16[256,1024]{1,0:T(8,128)(2,1)}, bf16[256,768]{1,0:T(8,128)(2,1)}, bf16[256,1024]{1,0:T(8,128)(2,1)}, bf1...) custom-call(bf16[256,1024]{1,0:T(8,128)(2,1)} %h_ref.3, ...), custom_call_target="tpu_custom_call" | custom-call | tf_op jit(solution)/shard_map/pallas_call | solution.py:613
  70.0 48.7 %shard_map.289 = (bf16[256,1024]{1,0:T(8,128)(2,1)}, bf16[256,1024]{1,0:T(8,128)(2,1)}, bf16[256,768]{1,0:T(8,128)(2,1)}, bf16[256,1024]{1,0:T(8,128)(2,1)}, bf1...) custom-call(bf16[256,1024]{1,0:T(8,128)(2,1)} %get-tuple-element.74., ...), custom_call_target="tpu_custom_call" | custom-call | tf_op jit(solution)/shard_map/pallas_call | solution.py:613
  118.7 69.5 %shard_map.290 = (f32[256,1024]{1,0:T(8,128)}, bf16[1024,3072]{1,0:T(8,128)(2,1)}, bf16[1024,3072]{1,0:T(8,128)(2,1)}, bf16[256,1152]{1,0:T(8,128)(2,1)}, f32[24,1024]{1,0:T(8,128)}, /*index=5*/bf16[256,3072]{1,0:T(8,128)(2,1)}) custom-call(f32[256,1024]{1,0:T(8,128)} %convert_element_type.38.grad_ref, bf16[256,1024]{1,0:T(8,128)(2,1)} %get-tuple-element.74.h_ref, ...), custom_call_target="tpu_custom_call" | custom-call | tf_op jit(solution)/shard_map/pallas_call | solution.py:1063
  188.2 73.3 %shard_map.291 = (f32[64,3072]{1,0:T(8,128)}, f32[256,1024]{1,0:T(8,128)}, bf16[1024,3072]{1,0:T(8,128)(2,1)}, bf16[1024,3072]{1,0:T(8,128)(2,1)}, bf16[256,1152...) custom-call(f32[256,1024]{1,0:T(8,128)} %get-tuple-element.94.grad_ref, bf16[256,1024]{1,0:T(8,128)(2,1)} %h_ref.3, ...), custom_call_target="tpu_custom_call" | custom-call | tf_op jit(solution)/shard_map/pallas_call | solution.py:1063
  261.6 2.2 pad_maximum_fusion
  263.8 96.5 %shard_map.292 = (f32[2,64,1024]{2,1,0:T(8,128)}, f32[2,64,2048]{2,1,0:T(8,128)}, f32[2,64,1536]{2,1,0:T(8,128)}, f32[2,64,256]{2,1,0:T(8,128)}, f32[2,64,128]{2...) custom-call(bf16[1024,3072]{1,0:T(8,128)(2,1)} %get-tuple-element.118.refs_0_, ...), custom_call_target="tpu_custom_call" | custom-call | bytes 419430400 | tf_op jit(solution)/shard_map/pallas_call | solution.py:358
  360.3 2.6 reshape.71
  363.0 1.5 copy.60
  364.5 3.2 reshape.76
  367.7 1.0 constant_dynamic-update-slice_fusion.1
  368.6 0.9 constant_dynamic-update-slice_fusion
  370.3 0.7 copy.61
  371.1 0.6 constant_dynamic-slice_fusion
  372.3 0.7 slice.116
  373.0 0.8 convert.8
  373.8 0.7 copy.64
  375.1 0.8 copy.75
  375.9 1.0 copy.76
  376.9 0.7 copy.77
  378.2 0.7 copy.79
  378.8 0.7 copy.80
  379.6 0.8 copy.81
  (45 shorter events, 6.8 us)
Async XLA Ops:
  8.0 11.3 %copy-start.8 = (bf16[2,1024]{1,0:T(2,128)(2,1)S(1)}, bf16[2,1024]{1,0:T(2,128)(2,1)}, u32[]{:S(2)}) copy-start(bf16[2,1024]{1,0:T(2,128)(2,1)} %param.30) | copy-start | bytes 12292
  8.0 11.3 %copy-start.9 = (bf16[2,1024]{1,0:T(2,128)(2,1)S(1)}, bf16[2,1024]{1,0:T(2,128)(2,1)}, u32[]{:S(2)}) copy-start(bf16[2,1024]{1,0:T(2,128)(2,1)} %param.19) | copy-start | bytes 12292
  8.0 359.6 %all-reduce.8.cloned.1.call-start = ((), (), s32[]{:S(2)}) async-start(), calls=%async_computation.2 | async-start | bytes 393216 | tf_op jit(solution)/shard_map/psum | solution.py:1149
  188.2 73.4 %copy-start.1 = (bf16[256,1152]{1,0:T(8,128)(2,1)S(1)}, bf16[256,1152]{1,0:T(8,128)(2,1)}, u32[]{:S(2)}) copy-start(bf16[256,1152]{1,0:T(8,128)(2,1)} %get-tuple-element.124) | copy-start | bytes 1769476
  261.5 110.8 %reduce-scatter.2.cloned.1.call-start = ((), (), s32[]{:S(2)}) async-start(), calls=%async_computation.1 | async-start | bytes 1216512 | tf_op jit(solution)/shard_map/reduce_scatter | solution.py:1148
  360.3 14.8 %copy-start.2 = (bf16[256,1024]{1,0:T(8,128)(2,1)S(1)}, bf16[256,1024]{1,0:T(8,128)(2,1)}, u32[]{:S(2)}) copy-start(bf16[256,1024]{1,0:T(8,128)(2,1)} %get-tuple-element.219) | copy-start | bytes 1572868
  360.3 15.6 %copy-start = (f32[256,1024]{1,0:T(8,128)S(1)}, f32[256,1024]{1,0:T(8,128)}, u32[]{:S(2)}) copy-start(f32[256,1024]{1,0:T(8,128)} %get-tuple-element.220) | copy-start | bytes 3145732
  364.5 12.4 %copy-start.6 = (f32[2,64,256]{2,1,0:T(8,128)S(1)}, f32[2,64,256]{2,1,0:T(8,128)}, u32[]{:S(2)}) copy-start(f32[2,64,256]{2,1,0:T(8,128)} %get-tuple-element.228) | copy-start | bytes 393220
  364.5 13.0 %copy-start.7 = (f32[2,64,128]{2,1,0:T(8,128)S(1)}, f32[2,64,128]{2,1,0:T(8,128)}, u32[]{:S(2)}) copy-start(f32[2,64,128]{2,1,0:T(8,128)} %get-tuple-element.127) | copy-start | bytes 196612
  364.5 13.6 %copy-start.5 = (f32[2,64,256]{2,1,0:T(8,128)S(1)}, f32[2,64,256]{2,1,0:T(8,128)}, u32[]{:S(2)}) copy-start(f32[2,64,256]{2,1,0:T(8,128)} %get-tuple-element.128) | copy-start | bytes 393220
  364.5 14.3 %copy-start.4 = (f32[2,64,768]{2,1,0:T(8,128)S(1)}, f32[2,64,768]{2,1,0:T(8,128)}, u32[]{:S(2)}) copy-start(f32[2,64,768]{2,1,0:T(8,128)} %get-tuple-element.129) | copy-start | bytes 1179652
  367.7 11.9 %copy-start.3 = (f32[2,64,1024]{2,1,0:T(8,128)S(1)}, f32[2,64,1024]{2,1,0:T(8,128)}, u32[]{:S(2)}) copy-start(f32[2,64,1024]{2,1,0:T(8,128)} %get-tuple-element.131) | copy-start | bytes 1572868
Sparse Core Ops, SparseCore 0:
  261.7 98.4 all-reduce.7
Sparse Core Ops, SparseCore 1:
  267.1 99.3 reduce-scatter.1
